TPU v7x, 32 devices: a whole 2x2x4 slice. The times are simulated.
32 devices in a mesh: dp: 8 (over z, y), ctx: 2 (over x), tp: 2 (over core).
Axes of the slice: x: 2, y: 2, z: 4, core: 2. Of those that a mesh axis runs over, the one named last changes fastest.
Arguments:
- tokens_in: bfloat16 [8, 1032, 1024], P('dp', 'ctx'), may hold values from -6 to 6
- cotangent: bfloat16 [8, 1032, 1024], P('dp', 'ctx'), may hold values from -6 to 6
- key_mask: int32 [8, 1032], P('dp', 'ctx'), may hold values from 0 to 1, as said below
- grid_pos: int32 [2, 8, 1032], P(None, 'dp', 'ctx'), may hold values from 0 to 31, as said below
- class_index: int32 [8], P('dp'), may hold values from 0 to 1031, as said below
- input_weight: bfloat16 [2, 1024, 3, 1024], P(None, ('dp', 'ctx'), None, 'tp'), may hold values from -0.1875 to 0.1875
- output_weight: bfloat16 [2, 1024, 1024], P(None, ('dp', 'ctx'), 'tp'), may hold values from -0.1875 to 0.1875
- gate_up_weight: bfloat16 [2, 1024, 2, 2730], P(None, ('dp', 'ctx'), None, 'tp'), may hold values from -0.1875 to 0.1875
- down_weight: bfloat16 [2, 1024, 2730], P(None, ('dp', 'ctx'), 'tp'), may hold values from -0.109375 to 0.109375
- norm_gains: bfloat16 [2, 2, 1024], replicated, may hold values from 0.099609375 to 1.8984375
- norm_biases: bfloat16 [2, 4, 1024], replicated, may hold values from -3 to 3
- head_gains: bfloat16 [2, 1024], P(None, 'tp'), may hold values from 0.099609375 to 1.8984375
- head_biases: bfloat16 [2, 3, 1024], P(None, None, 'tp'), may hold values from -3 to 3
- hidden_gains: bfloat16 [2, 2730], P(None, 'tp'), may hold values from 0.099609375 to 1.8984375
- hidden_biases: bfloat16 [2, 3, 2730], P(None, None, 'tp'), may hold values from -3 to 3
Outputs:
- activations: bfloat16 [8, 1032, 1024], P('dp', 'ctx')
- input_grad: float32 [8, 1032, 1024], P('dp', 'ctx')
- grad_input_weight: float32 [2, 1024, 3, 1024], P(None, ('dp', 'ctx'), None, 'tp')
- grad_output_weight: float32 [2, 1024, 1024], P(None, ('dp', 'ctx'), 'tp')
- grad_gate_up_weight: float32 [2, 1024, 2, 2730], P(None, ('dp', 'ctx'), None, 'tp')
- grad_down_weight: float32 [2, 1024, 2730], P(None, ('dp', 'ctx'), 'tp')
- grad_norm_gains: float32 [2, 2, 1024], replicated
- grad_norm_biases: float32 [2, 4, 1024], replicated
- grad_head_gains: float32 [2, 1024], P(None, 'tp')
- grad_head_biases: float32 [2, 3, 1024], P(None, None, 'tp')
- grad_hidden_gains: float32 [2, 2730], P(None, 'tp')
- grad_hidden_biases: float32 [2, 3, 2730], P(None, None, 'tp')
Inputs may be any that keep to these rules, and one draw needn't show every extreme that they name: `key_mask`: exactly one image, drawn from the seed, is all zeros; every other image has 1 on exactly 1025 rows, among them its first and its last row, the others at drawn places, and 0 on the rest. `grid_pos`: in each image the rows where a nonempty image's key_mask would be 1, other than the class token, hold every patch of the 32 x 32 grid once, in a drawn order; the class token and pad rows hold 0. `class_index`: the class token lies on one of an image's real rows.
All inputs are finite; a program needn't handle non-finite values.
Results may differ from a plain program's by a relative error of at most 0.018.
Values may be sent and summed in bfloat16 or wider, within the bound.
A program may use at most 256 MiB of HBM per device.

v0:
```python
import jax
import jax.numpy as jnp
from jax import lax
from jax.sharding import PartitionSpec as P

FF = 2730
HEAD_DIM = 64


norm_epsilon = 1e-06
rotary_base = 10000.0
masked_score = -10000.0


def rotary_tables(positions, not_class):
    quarter = HEAD_DIM // 4
    frequency = rotary_base ** (-jnp.arange(quarter, dtype=jnp.float32) / quarter)
    angles = (
        jnp.transpose(positions).astype(jnp.float32)[:, :, None]
        * frequency
        * not_class[:, None, None]
    )
    return (jnp.cos(angles), jnp.sin(angles))


def rotate(values, cosine, sine, direction):
    row_count, head_count, head_dim = values.shape
    paired = values.reshape(row_count, head_count, 2, 2, head_dim // 4)
    first_half = paired[:, :, :, 0]
    second_half = paired[:, :, :, 1]
    cos_rows = cosine[:, None]
    sin_rows = sine[:, None] * direction
    turned = jnp.stack(
        [
            first_half * cos_rows - second_half * sin_rows,
            second_half * cos_rows + first_half * sin_rows,
        ],
        axis=3,
    )
    return turned.reshape(row_count, head_count, head_dim)


def local_norm(values, gain_vec, shift_vec):
    center = values - jnp.mean(values, axis=-1, keepdims=True)
    spread = jnp.mean(center * center, axis=-1, keepdims=True)
    inv_spread = lax.rsqrt(spread + norm_epsilon)
    unit_rows = center * inv_spread
    return (unit_rows * gain_vec + shift_vec, unit_rows, inv_spread)


def local_norm_back(upstream, unit_rows, inv_spread, gain_vec):
    weighted = upstream * gain_vec
    return inv_spread * (
        weighted
        - jnp.mean(weighted, axis=-1, keepdims=True)
        - unit_rows * jnp.mean(weighted * unit_rows, axis=-1, keepdims=True)
    )


def row_totals(first_part, second_part):
    return lax.psum(
        (jnp.sum(first_part, axis=-1, keepdims=True), jnp.sum(second_part, axis=-1, keepdims=True)),
        "tp",
    )


def split_norm(values, gain_vec, shift_vec, full_width):
    sum_first, sum_second = row_totals(values, values * values)
    row_mean = sum_first / full_width
    inv_spread = lax.rsqrt(sum_second / full_width - row_mean * row_mean + norm_epsilon)
    unit_rows = (values - row_mean) * inv_spread
    return (unit_rows * gain_vec + shift_vec, unit_rows, inv_spread)


def split_norm_back(upstream, unit_rows, inv_spread, gain_vec, full_width):
    weighted = upstream * gain_vec
    sum_first, sum_second = row_totals(weighted, weighted * unit_rows)
    return inv_spread * (weighted - sum_first / full_width - unit_rows * (sum_second / full_width))


def tensor_sum(partial_value):
    return lax.psum(partial_value.astype(jnp.bfloat16), "tp").astype(jnp.float32)


def tensor_back(partial_value):
    return lax.psum(partial_value.astype(jnp.bfloat16), "tp").astype(jnp.float32)


def fetch_weights(layer_index, input_weight, output_weight, gate_up_weight, down_weight):
    return (
        lax.all_gather(input_weight[layer_index], ("dp", "ctx"), axis=0, tiled=True),
        lax.all_gather(output_weight[layer_index], ("dp", "ctx"), axis=0, tiled=True),
        lax.all_gather(gate_up_weight[layer_index], ("dp", "ctx"), axis=0, tiled=True),
        lax.all_gather(down_weight[layer_index], ("dp", "ctx"), axis=0, tiled=True),
    )


def masked_scores(queries, key_heads, valid_keys):
    raw_scores = jnp.einsum("qhe,khe->hqk", queries, key_heads, preferred_element_type=jnp.float32)
    return jnp.where(valid_keys[None, None, :] > 0, raw_scores * HEAD_DIM ** (-0.5), masked_score)


def attend_forward(block_items):
    queries, keys_all, values_all, valid_keys = block_items
    key_count = keys_all.shape[0]
    head_count = queries.shape[1]
    key_heads = keys_all.reshape(key_count, head_count, HEAD_DIM)
    value_heads = values_all.reshape(key_count, head_count, HEAD_DIM)
    scores = masked_scores(queries, key_heads, valid_keys)
    row_max = jnp.max(scores, axis=-1, keepdims=True)
    exp_scores = jnp.exp(scores - row_max)
    row_total = jnp.sum(exp_scores, axis=-1, keepdims=True)
    attn_probs = (exp_scores / row_total).astype(jnp.bfloat16)
    attended = jnp.einsum(
        "hqk,khe->qhe", attn_probs, value_heads, preferred_element_type=jnp.float32
    )
    return (
        attended.reshape(queries.shape[0], head_count * HEAD_DIM),
        (row_max + jnp.log(row_total))[:, :, 0],
    )


def attend_backward(block_items):
    queries, keys_all, values_all, valid_keys, log_total, grad_out = block_items
    key_count = keys_all.shape[0]
    head_count = queries.shape[1]
    key_heads = keys_all.reshape(key_count, head_count, HEAD_DIM)
    value_heads = values_all.reshape(key_count, head_count, HEAD_DIM)
    scores = masked_scores(queries, key_heads, valid_keys)
    probs_full = jnp.exp(scores - log_total[:, :, None])
    probs_low = probs_full.astype(jnp.bfloat16)
    grad_probs = jnp.einsum(
        "qhe,khe->hqk", grad_out, value_heads, preferred_element_type=jnp.float32
    )
    row_dot = jnp.sum(probs_full * grad_probs, axis=-1, keepdims=True)
    grad_raw = jnp.where(
        valid_keys[None, None, :] > 0, HEAD_DIM ** (-0.5) * probs_full * (grad_probs - row_dot), 0.0
    ).astype(jnp.bfloat16)
    grad_queries = jnp.einsum(
        "hqk,khe->qhe", grad_raw, key_heads, preferred_element_type=jnp.float32
    )
    grad_keys = jnp.einsum("hqk,qhe->khe", grad_raw, queries, preferred_element_type=jnp.float32)
    grad_values = jnp.einsum(
        "hqk,qhe->khe", probs_low, grad_out, preferred_element_type=jnp.float32
    )
    local_rows = queries.shape[0]
    return (
        grad_queries.reshape(local_rows, head_count * HEAD_DIM),
        grad_keys.reshape(key_count, head_count * HEAD_DIM),
        grad_values.reshape(key_count, head_count * HEAD_DIM),
    )


def contract_rows(left, right):
    return lax.dot_general(
        left, right, (((0,), (0,)), ((), ())), preferred_element_type=jnp.float32
    )


def contract_cols(left, right):
    return lax.dot_general(
        left, right, (((1,), (1,)), ((), ())), preferred_element_type=jnp.float32
    )


def on_device(
    tokens_in,
    cotangent,
    key_mask,
    grid_pos,
    class_index,
    input_weight,
    output_weight,
    gate_up_weight,
    down_weight,
    norm_gains,
    norm_biases,
    head_gains,
    head_biases,
    hidden_gains,
    hidden_biases,
):
    images, rows_dev, model_width = tokens_in.shape
    row_count = images * rows_dev
    dim_local = head_gains.shape[1]
    heads_local = dim_local // HEAD_DIM
    hidden_local = hidden_gains.shape[1]
    layer_count = input_weight.shape[0]
    first_row = lax.axis_index("ctx") * rows_dev
    places = first_row + jnp.arange(rows_dev, dtype=jnp.int32)
    not_class = (places[None, :] != class_index[:, None]).astype(jnp.float32).reshape(row_count)
    cosine, sine = rotary_tables(grid_pos.reshape(2, row_count), not_class)
    row_keep = key_mask.astype(jnp.float32).reshape(row_count, 1)
    key_keep = key_mask.astype(jnp.bfloat16)
    gains_norm = norm_gains.astype(jnp.float32)
    biases_norm = norm_biases.astype(jnp.float32)
    gains_head = head_gains.astype(jnp.float32)
    biases_head = head_biases.astype(jnp.float32)
    gains_hidden = hidden_gains.astype(jnp.float32)
    biases_hidden = hidden_biases.astype(jnp.float32)
    hidden_state = tokens_in.astype(jnp.float32).reshape(row_count, model_width) * row_keep
    saved_layers = []
    for layer_index in range(layer_count):
        layer_mats = fetch_weights(
            layer_index, input_weight, output_weight, gate_up_weight, down_weight
        )
        mat_in, mat_out, mat_gate_up, mat_down = layer_mats
        normed, unit_one, spread_one = local_norm(
            hidden_state, gains_norm[layer_index, 0], biases_norm[layer_index, 0]
        )
        normed_low = normed.astype(jnp.bfloat16)
        projected = jnp.dot(
            normed_low,
            mat_in.reshape(model_width, 3 * dim_local),
            preferred_element_type=jnp.float32,
        ).reshape(row_count, 3, dim_local)
        queries = projected[:, 0] + biases_head[layer_index, 0]
        keys_proj = projected[:, 1]
        values_proj = projected[:, 2] + biases_head[layer_index, 1]
        query_low = rotate(
            queries.reshape(row_count, heads_local, HEAD_DIM), cosine, sine, 1.0
        ).astype(jnp.bfloat16)
        key_low = rotate(
            keys_proj.reshape(row_count, heads_local, HEAD_DIM), cosine, sine, 1.0
        ).astype(jnp.bfloat16)
        value_low = values_proj.astype(jnp.bfloat16)
        keys_all, values_all, valid_all = (
            lax.all_gather(key_low.reshape(images, rows_dev, dim_local), "ctx", axis=1, tiled=True),
            lax.all_gather(
                value_low.reshape(images, rows_dev, dim_local), "ctx", axis=1, tiled=True
            ),
            lax.all_gather(key_keep, "ctx", axis=1, tiled=True),
        )
        query_blocks = query_low.reshape(images, rows_dev, heads_local, HEAD_DIM)
        attended, log_total = lax.map(
            attend_forward, (query_blocks, keys_all, values_all, valid_all)
        )
        attended = attended.reshape(row_count, dim_local)
        head_normed, unit_two, spread_two = split_norm(
            attended, gains_head[layer_index], biases_head[layer_index, 2], model_width
        )
        head_low = head_normed.astype(jnp.bfloat16)
        branch = tensor_sum(contract_cols(head_low, mat_out))
        hidden_mid = hidden_state + row_keep * (branch + biases_norm[layer_index, 2])
        normed_two, unit_three, spread_three = local_norm(
            hidden_mid, gains_norm[layer_index, 1], biases_norm[layer_index, 1]
        )
        normed_two_low = normed_two.astype(jnp.bfloat16)
        gate_up = jnp.dot(
            normed_two_low,
            mat_gate_up.reshape(model_width, 2 * hidden_local),
            preferred_element_type=jnp.float32,
        ).reshape(row_count, 2, hidden_local)
        gate_pre = gate_up[:, 0] + biases_hidden[layer_index, 0]
        up_pre = gate_up[:, 1] + biases_hidden[layer_index, 1]
        inner_act = jax.nn.silu(gate_pre) * up_pre
        inner_normed, unit_four, spread_four = split_norm(
            inner_act, gains_hidden[layer_index], biases_hidden[layer_index, 2], FF
        )
        inner_low = inner_normed.astype(jnp.bfloat16)
        down_out = tensor_sum(contract_cols(inner_low, mat_down))
        hidden_state = hidden_mid + row_keep * (down_out + biases_norm[layer_index, 3])
        held_mats = None
        saved_layers.append(
            (
                held_mats,
                normed_low,
                unit_one,
                spread_one,
                query_blocks,
                keys_all,
                values_all,
                valid_all,
                log_total,
                unit_two,
                spread_two,
                head_low,
                unit_three,
                spread_three,
                normed_two_low,
                gate_pre,
                up_pre,
                unit_four,
                spread_four,
                inner_low,
            )
        )
    activations = hidden_state.reshape(images, rows_dev, model_width).astype(jnp.bfloat16)
    upstream = cotangent.astype(jnp.float32).reshape(row_count, model_width)
    mat_grads = [None] * layer_count
    vector_parts = [None] * layer_count
    for layer_index in reversed(range(layer_count)):
        (
            held_mats,
            normed_low,
            unit_one,
            spread_one,
            query_blocks,
            keys_all,
            values_all,
            valid_all,
            log_total,
            unit_two,
            spread_two,
            head_low,
            unit_three,
            spread_three,
            normed_two_low,
            gate_pre,
            up_pre,
            unit_four,
            spread_four,
            inner_low,
        ) = saved_layers[layer_index]
        mat_in, mat_out, mat_gate_up, mat_down = fetch_weights(
            layer_index, input_weight, output_weight, gate_up_weight, down_weight
        )
        grad_down = row_keep * upstream
        grad_bias_down = jnp.sum(grad_down, axis=0)
        grad_down_low = grad_down.astype(jnp.bfloat16)
        grad_mat_down = contract_rows(grad_down_low, inner_low)
        grad_inner_normed = jnp.dot(grad_down_low, mat_down, preferred_element_type=jnp.float32)
        grad_gain_hidden = jnp.sum(grad_inner_normed * unit_four, axis=0)
        grad_shift_hidden = jnp.sum(grad_inner_normed, axis=0)
        grad_inner = split_norm_back(
            grad_inner_normed, unit_four, spread_four, gains_hidden[layer_index], FF
        )
        sigmoid_gate = jax.nn.sigmoid(gate_pre)
        grad_up = grad_inner * gate_pre * sigmoid_gate
        grad_gate = grad_inner * up_pre * sigmoid_gate * (1.0 + gate_pre * (1.0 - sigmoid_gate))
        grad_gate_up_low = (
            jnp.stack([grad_gate, grad_up], axis=1)
            .astype(jnp.bfloat16)
            .reshape(row_count, 2 * hidden_local)
        )
        grad_mat_gate_up = contract_rows(normed_two_low, grad_gate_up_low).reshape(
            model_width, 2, hidden_local
        )
        grad_normed_two = tensor_back(
            contract_cols(grad_gate_up_low, mat_gate_up.reshape(model_width, 2 * hidden_local))
        )
        grad_gain_two = jnp.sum(grad_normed_two * unit_three, axis=0)
        grad_shift_two = jnp.sum(grad_normed_two, axis=0)
        upstream = upstream + local_norm_back(
            grad_normed_two, unit_three, spread_three, gains_norm[layer_index, 1]
        )
        grad_branch = row_keep * upstream
        grad_bias_out = jnp.sum(grad_branch, axis=0)
        grad_branch_low = grad_branch.astype(jnp.bfloat16)
        grad_mat_out = contract_rows(grad_branch_low, head_low)
        grad_head = jnp.dot(grad_branch_low, mat_out, preferred_element_type=jnp.float32)
        grad_gain_head = jnp.sum(grad_head * unit_two, axis=0)
        grad_shift_head = jnp.sum(grad_head, axis=0)
        grad_attended = split_norm_back(
            grad_head, unit_two, spread_two, gains_head[layer_index], model_width
        )
        grad_att_low = grad_attended.astype(jnp.bfloat16).reshape(
            images, rows_dev, heads_local, HEAD_DIM
        )
        grad_query_rot, grad_keys_all, grad_values_all = lax.map(
            attend_backward,
            (query_blocks, keys_all, values_all, valid_all, log_total, grad_att_low),
        )
        grad_keys_rot, grad_values = (
            lax.psum_scatter(
                grad_keys_all.astype(jnp.bfloat16), "ctx", scatter_dimension=1, tiled=True
            ).astype(jnp.float32),
            lax.psum_scatter(
                grad_values_all.astype(jnp.bfloat16), "ctx", scatter_dimension=1, tiled=True
            ).astype(jnp.float32),
        )
        grad_queries = rotate(
            grad_query_rot.reshape(row_count, heads_local, HEAD_DIM), cosine, sine, -1.0
        ).reshape(row_count, dim_local)
        grad_keys = rotate(
            grad_keys_rot.reshape(row_count, heads_local, HEAD_DIM), cosine, sine, -1.0
        ).reshape(row_count, dim_local)
        grad_values = grad_values.reshape(row_count, dim_local)
        grad_proj_low = (
            jnp.stack([grad_queries, grad_keys, grad_values], axis=1)
            .astype(jnp.bfloat16)
            .reshape(row_count, 3 * dim_local)
        )
        grad_mat_in = contract_rows(normed_low, grad_proj_low).reshape(model_width, 3, dim_local)
        grad_normed_one = tensor_back(
            contract_cols(grad_proj_low, mat_in.reshape(model_width, 3 * dim_local))
        )
        grad_gain_one = jnp.sum(grad_normed_one * unit_one, axis=0)
        grad_shift_one = jnp.sum(grad_normed_one, axis=0)
        upstream = upstream + local_norm_back(
            grad_normed_one, unit_one, spread_one, gains_norm[layer_index, 0]
        )
        mat_grads[layer_index] = (
            lax.psum_scatter(grad_mat_in, ("dp", "ctx"), scatter_dimension=0, tiled=True),
            lax.psum_scatter(grad_mat_out, ("dp", "ctx"), scatter_dimension=0, tiled=True),
            lax.psum_scatter(grad_mat_gate_up, ("dp", "ctx"), scatter_dimension=0, tiled=True),
            lax.psum_scatter(grad_mat_down, ("dp", "ctx"), scatter_dimension=0, tiled=True),
        )
        vector_parts[layer_index] = (
            jnp.stack([grad_gain_one, grad_gain_two]),
            jnp.stack([grad_shift_one, grad_shift_two, grad_bias_out, grad_bias_down]),
            grad_gain_head,
            jnp.stack(
                [jnp.sum(grad_queries, axis=0), jnp.sum(grad_values, axis=0), grad_shift_head]
            ),
            grad_gain_hidden,
            jnp.stack([jnp.sum(grad_gate, axis=0), jnp.sum(grad_up, axis=0), grad_shift_hidden]),
        )
    input_grad = (row_keep * upstream).reshape(images, rows_dev, model_width)
    stacked_vectors = tuple(
        (
            jnp.stack([vector_parts[index][member] for index in range(layer_count)])
            for member in range(6)
        )
    )
    summed_vectors = lax.psum(
        (
            stacked_vectors[0],
            stacked_vectors[1],
            stacked_vectors[2],
            stacked_vectors[3],
            stacked_vectors[4],
            stacked_vectors[5],
        ),
        ("dp", "ctx"),
    )
    grad_input_weight = jnp.stack([mat_grads[index][0] for index in range(layer_count)])
    grad_output_weight = jnp.stack([mat_grads[index][1] for index in range(layer_count)])
    grad_gate_up_weight = jnp.stack([mat_grads[index][2] for index in range(layer_count)])
    grad_down_weight = jnp.stack([mat_grads[index][3] for index in range(layer_count)])
    return (
        activations,
        input_grad,
        grad_input_weight,
        grad_output_weight,
        grad_gate_up_weight,
        grad_down_weight,
        summed_vectors[0],
        summed_vectors[1],
        summed_vectors[2],
        summed_vectors[3],
        summed_vectors[4],
        summed_vectors[5],
    )


def solution(mesh):
    return jax.shard_map(
        on_device,
        mesh=mesh,
        in_specs=(
            P("dp", "ctx", None),
            P("dp", "ctx", None),
            P("dp", "ctx"),
            P(None, "dp", "ctx"),
            P("dp"),
            P(None, ("dp", "ctx"), None, "tp"),
            P(None, ("dp", "ctx"), "tp"),
            P(None, ("dp", "ctx"), None, "tp"),
            P(None, ("dp", "ctx"), "tp"),
            P(),
            P(),
            P(None, "tp"),
            P(None, None, "tp"),
            P(None, "tp"),
            P(None, None, "tp"),
        ),
        out_specs=(
            P("dp", "ctx", None),
            P("dp", "ctx", None),
            P(None, ("dp", "ctx"), None, "tp"),
            P(None, ("dp", "ctx"), "tp"),
            P(None, ("dp", "ctx"), None, "tp"),
            P(None, ("dp", "ctx"), "tp"),
            P(),
            P(),
            P(None, "tp"),
            P(None, None, "tp"),
            P(None, "tp"),
            P(None, None, "tp"),
        ),
        check_vma=False,
    )
```

profile of v0, /device:TPU:0, one launch (start us, length us, event | category | flops | bytes accessed | tf_op | source)
XLA Modules:
  0.0 2527.9 jit_solution(4947003350529639438)
XLA Ops:
  16.5 65.2 %all-gather.29.cloned.1.call-done = bf16[1,1024,3,512]{3,1,2,0:T(8,128)(2,1)} async-done(((bf16[1,64,3,512]{3,1,2,0:T(8,128)(2,1)}), bf16[1,1024,3,512]{3,1,2,0:T(8,128)(2,1)}) %all-gather.29.cloned.1.call-update) | async-done | bytes 3145744 | tf_op jit(solution)/shard_map/all_gather | solution.py:91
  114.6 20.1 all-gather.23.cloned.1.call-done
  189.5 39.1 %all-gather.31.cloned.1.call-done = bf16[1,1024,512]{2,1,0:T(8,128)(2,1)} async-done(((bf16[1,64,512]{2,1,0:T(8,128)(2,1)}), bf16[1,1024,512]{2,1,0:T(8,128)(2,1)}) %all-gather.31.cloned.1.call-update) | async-done | bytes 1048592 | tf_op jit(solution)/shard_map/all_gather | solution.py:92
  253.1 91.4 %all-gather.33.cloned.1.call-done = bf16[1,1024,2,1365]{3,2,0,1:T(2,128)(2,1)} async-done(((bf16[1,64,2,1365]{3,2,0,1:T(2,128)(2,1)}), bf16[1,1024,2,1365]{3,2,0,1:T(2,128)(2,1)}) %all-gather.33.cloned.1.call-update) | async-done | bytes 5591056 | tf_op jit(solution)/shard_map/all_gather | solution.py:93
  384.3 28.2 %all-gather.35.cloned.1.call-done = bf16[1,1024,1365]{2,1,0:T(8,128)(2,1)} async-done(((bf16[1,64,1365]{2,1,0:T(8,128)(2,1)}), bf16[1,1024,1365]{2,1,0:T(8,128)(2,1)}) %all-gather.35.cloned.1.call-update) | async-done | bytes 2795536 | tf_op jit(solution)/shard_map/all_gather | solution.py:94
  418.4 64.5 %all-gather.37.cloned.1.call-done = bf16[1,1024,3,512]{3,1,2,0:T(8,128)(2,1)} async-done(((bf16[1,64,3,512]{3,1,2,0:T(8,128)(2,1)}), bf16[1,1024,3,512]{3,1,2,0:T(8,128)(2,1)}) %all-gather.37.cloned.1.call-update) | async-done | bytes 3145744 | tf_op jit(solution)/shard_map/all_gather | solution.py:91
  529.4 18.8 all-gather.25.cloned.1.call-done
  554.3 29.4 %all-gather.27.cloned.1.call-done = bf16[1,1032,512]{2,0,1:T(2,128)(2,1)} async-done(((bf16[1,516,512]{2,0,1:T(2,128)(2,1)}), bf16[1,1032,512]{2,0,1:T(2,128)(2,1)}) %all-gather.27.cloned.1.call-update) | async-done | bytes 1056784 | tf_op jit(solution)/shard_map/all_gather | solution.py:228
  645.7 87.5 %all-gather.41.cloned.1.call-done = bf16[1,1024,2,1365]{3,2,0,1:T(2,128)(2,1)} async-done(((bf16[1,64,2,1365]{3,2,0,1:T(2,128)(2,1)}), bf16[1,1024,2,1365]{3,2,0,1:T(2,128)(2,1)}) %all-gather.41.cloned.1.call-update) | async-done | bytes 5591056 | tf_op jit(solution)/shard_map/all_gather | solution.py:93
  787.7 36.4 %all-gather.43.cloned.1.call-done = bf16[1,1024,1365]{2,1,0:T(8,128)(2,1)} async-done(((bf16[1,64,1365]{2,1,0:T(8,128)(2,1)}), bf16[1,1024,1365]{2,1,0:T(8,128)(2,1)}) %all-gather.43.cloned.1.call-update) | async-done | bytes 2795536 | tf_op jit(solution)/shard_map/all_gather | solution.py:94
  883.9 25.6 %fusion.71 = bf16[8,64,1032]{2,1,0:T(8,128)(2,1)} fusion(bf16[516,8,64]{0,2,1:T(8,128)(2,1)} %bitcast.477, f32[8,516,1032]{2,1,0:T(8,128)} %get-tuple-element.313, bf16[516,8,64]{0,2,1:T(8,128)(2,1)S(1)} %bitcast.463, bf16[1032,8,64]{0,2,1:T(8,128)(2,1)} %bitcast.483, f32[8,516]{1,0:T(8,128)S(1)} %log_add_fusion.1, pred[1032]{0:T(1024)(128)(4,1)S(1)} %copy-done.111), kind=kOutput, calls=%fused_computation.65 | convolution fusion | flops 1670491136 | bytes 20228232 | tf_op jit(solution)/shard_map/while/body/eval_jaxpr/hqk,qhe->khe/dot_general | solution.py:142
  921.2 30.0 %fusion = bf16[520,512]{1,0:T(8,128)(2,1)} fusion(bf16[1,1032,512]{2,1,0:T(8,128)(2,1)} %copy.108), kind=kCustom, calls=%all-reduce-scatter | all-reduce-scatter fusion | flops 532481 | bytes 1589760
  954.7 22.6 fusion.35
  1075.0 22.5 fusion.66
  1111.2 29.8 %fusion.1 = bf16[520,512]{1,0:T(8,128)(2,1)} fusion(bf16[1,1032,512]{2,1,0:T(8,128)(2,1)} %copy.113), kind=kCustom, calls=%all-reduce-scatter.1 | all-reduce-scatter fusion | flops 532481 | bytes 1589760
  1144.3 22.8 fusion.45
  1331.9 76.3 %reduce-scatter.23.cloned.1.call-done = f32[64,512]{1,0:T(8,128)} async-done(((f32[1024,512]{1,0:T(8,128)}), f32[64,512]{1,0:T(8,128)}) %reduce-scatter.23.cloned.1.call-update) | async-done | bytes 131088 | tf_op jit(solution)/shard_map/reduce_scatter | solution.py:395
  1408.3 80.0 %reduce-scatter.21.cloned.1.call-done = f32[64,512]{1,0:T(8,128)} async-done(((f32[1024,512]{1,0:T(8,128)}), f32[64,512]{1,0:T(8,128)}) %reduce-scatter.21.cloned.1.call-update) | async-done | bytes 131088 | tf_op jit(solution)/shard_map/reduce_scatter | solution.py:395
  1489.9 123.9 %reduce-scatter.31.cloned.1.call-done = f32[64,1365]{1,0:T(8,128)} async-done(((f32[1024,1365]{1,0:T(8,128)}), f32[64,1365]{1,0:T(8,128)}) %reduce-scatter.31.cloned.1.call-update) | async-done | bytes 349456 | tf_op jit(solution)/shard_map/reduce_scatter | solution.py:397
  1613.8 129.2 %reduce-scatter.29.cloned.1.call-done = f32[64,1365]{1,0:T(8,128)} async-done(((f32[1024,1365]{1,0:T(8,128)}), f32[64,1365]{1,0:T(8,128)}) %reduce-scatter.29.cloned.1.call-update) | async-done | bytes 349456 | tf_op jit(solution)/shard_map/reduce_scatter | solution.py:397
  1745.0 137.4 %reduce-scatter.19.cloned.1.call-done = f32[64,3,512]{2,0,1:T(8,128)} async-done(((f32[1024,3,512]{2,0,1:T(8,128)}), f32[64,3,512]{2,0,1:T(8,128)}) %reduce-scatter.19.cloned.1.call-update) | async-done | bytes 393232 | tf_op jit(solution)/shard_map/reduce_scatter | solution.py:394
  1882.4 139.8 %reduce-scatter.17.cloned.1.call-done = f32[64,3,512]{2,0,1:T(8,128)} async-done(((f32[1024,3,512]{2,0,1:T(8,128)}), f32[64,3,512]{2,0,1:T(8,128)}) %reduce-scatter.17.cloned.1.call-update) | async-done | bytes 393232 | tf_op jit(solution)/shard_map/reduce_scatter | solution.py:394
  2024.3 242.4 %reduce-scatter.27.cloned.1.call-done = f32[64,2,1365]{2,0,1:T(8,128)} async-done(((f32[1024,2,1365]{2,0,1:T(8,128)}), f32[64,2,1365]{2,0,1:T(8,128)}) %reduce-scatter.27.cloned.1.call-update) | async-done | bytes 698896 | tf_op jit(solution)/shard_map/reduce_scatter | solution.py:396
  2266.7 247.7 %reduce-scatter.25.cloned.1.call-done = f32[64,2,1365]{2,0,1:T(8,128)} async-done(((f32[1024,2,1365]{2,0,1:T(8,128)}), f32[64,2,1365]{2,0,1:T(8,128)}) %reduce-scatter.25.cloned.1.call-update) | async-done | bytes 698896 | tf_op jit(solution)/shard_map/reduce_scatter | solution.py:396
  (637 shorter events, 697.7 us)
Async XLA Ops:
  9.2 125.6 %all-gather.23.cloned.1.call-start = ((), (), s32[]{:S(2)}) async-start(), calls=%async_computation.9 | async-start | bytes 3170304 | tf_op jit(solution)/shard_map/all_gather | solution.py:228
  106.1 122.6 %all-gather.31.cloned.1.call-start = ((), (), s32[]{:S(2)}) async-start(), calls=%async_computation.27 | async-start | bytes 1114112 | tf_op jit(solution)/shard_map/all_gather | solution.py:92
  106.8 143.5 %all-reduce.28.cloned.1.call-start = ((), (), s32[]{:S(2)}) async-start(), calls=%async_computation.10 | async-start | bytes 2129920 | tf_op jit(solution)/shard_map/psum | solution.py:82
  231.8 112.8 %all-gather.33.cloned.1.call-start = ((), (), s32[]{:S(2)}) async-start(), calls=%async_computation.28 | async-start | bytes 6127616 | tf_op jit(solution)/shard_map/all_gather | solution.py:93
  233.2 179.3 %all-gather.35.cloned.1.call-start = ((), (), s32[]{:S(2)}) async-start(), calls=%async_computation.29 | async-start | bytes 3063808 | tf_op jit(solution)/shard_map/all_gather | solution.py:94
  235.1 247.9 %all-gather.37.cloned.1.call-start = ((), (), s32[]{:S(2)}) async-start(), calls=%async_computation.30 | async-start | bytes 3342336 | tf_op jit(solution)/shard_map/all_gather | solution.py:91
  235.8 268.9 %all-reduce.30.cloned.1.call-start = ((), (), s32[]{:S(2)}) async-start(), calls=%async_computation.11 | async-start | bytes 2129920 | tf_op jit(solution)/shard_map/psum | solution.py:82
  418.1 130.1 %all-gather.25.cloned.1.call-start = ((), (), s32[]{:S(2)}) async-start(), calls=%async_computation.12 | async-start | bytes 3170304 | tf_op jit(solution)/shard_map/all_gather | solution.py:229
  526.8 114.8 %all-gather.39.cloned.1.call-start = ((), (), s32[]{:S(2)}) async-start(), calls=%async_computation.31 | async-start | bytes 1114112 | tf_op jit(solution)/shard_map/all_gather | solution.py:92
  527.4 205.8 %all-gather.41.cloned.1.call-start = ((), (), s32[]{:S(2)}) async-start(), calls=%async_computation.32 | async-start | bytes 6127616 | tf_op jit(solution)/shard_map/all_gather | solution.py:93
  528.1 247.0 %all-reduce.32.cloned.1.call-start = ((), (), s32[]{:S(2)}) async-start(), calls=%async_computation.14 | async-start | bytes 2129920 | tf_op jit(solution)/shard_map/psum | solution.py:82
  644.6 179.5 %all-gather.43.cloned.1.call-start = ((), (), s32[]{:S(2)}) async-start(), calls=%async_computation.33 | async-start | bytes 3063808 | tf_op jit(solution)/shard_map/all_gather | solution.py:94
  645.2 223.0 %all-reduce.34.cloned.1.call-start = ((), (), s32[]{:S(2)}) async-start(), calls=%async_computation.15 | async-start | bytes 2129920 | tf_op jit(solution)/shard_map/psum | solution.py:86
  849.4 133.1 %all-reduce.40.cloned.1.call-start = ((), (), s32[]{:S(2)}) async-start(), calls=%async_computation.34 | async-start | bytes 2359296
  1036.9 141.8 %all-reduce.42.cloned.1.call-start = ((), (), s32[]{:S(2)}) async-start(), calls=%async_computation.35 | async-start | bytes 2359296
  1189.0 140.2 %all-reduce.44.cloned.1.call-start = ((), (), s32[]{:S(2)}) async-start(), calls=%async_computation.36 | async-start | bytes 251904 | tf_op jit(solution)/shard_map/psum | solution.py:416
  1215.3 193.0 %reduce-scatter.23.cloned.1.call-start = ((), (), s32[]{:S(2)}) async-start(), calls=%async_computation.21 | async-start | bytes 2228224 | tf_op jit(solution)/shard_map/reduce_scatter | solution.py:395
  1219.9 268.4 %reduce-scatter.21.cloned.1.call-start = ((), (), s32[]{:S(2)}) async-start(), calls=%async_computation.20 | async-start | bytes 2228224 | tf_op jit(solution)/shard_map/reduce_scatter | solution.py:395
  1224.4 389.5 %reduce-scatter.31.cloned.1.call-start = ((), (), s32[]{:S(2)}) async-start(), calls=%async_computation.25 | async-start | bytes 6127616 | tf_op jit(solution)/shard_map/reduce_scatter | solution.py:397
  1233.7 509.3 %reduce-scatter.29.cloned.1.call-start = ((), (), s32[]{:S(2)}) async-start(), calls=%async_computation.24 | async-start | bytes 6127616 | tf_op jit(solution)/shard_map/reduce_scatter | solution.py:397
  1242.2 640.2 %reduce-scatter.19.cloned.1.call-start = ((), (), s32[]{:S(2)}) async-start(), calls=%async_computation.19 | async-start | bytes 6684672 | tf_op jit(solution)/shard_map/reduce_scatter | solution.py:394
  1249.9 772.3 %reduce-scatter.17.cloned.1.call-start = ((), (), s32[]{:S(2)}) async-start(), calls=%async_computation.18 | async-start | bytes 6684672 | tf_op jit(solution)/shard_map/reduce_scatter | solution.py:394
  1256.9 1009.8 %reduce-scatter.27.cloned.1.call-start = ((), (), s32[]{:S(2)}) async-start(), calls=%async_computation.23 | async-start | bytes 12255232 | tf_op jit(solution)/shard_map/reduce_scatter | solution.py:396
  1288.4 1226.1 %reduce-scatter.25.cloned.1.call-start = ((), (), s32[]{:S(2)}) async-start(), calls=%async_computation.22 | async-start | bytes 12255232 | tf_op jit(solution)/shard_map/reduce_scatter | solution.py:396
  (165 other events, 6299.2 us)
Sparse Core Ops, SparseCore 0:
  11.4 70.2 all-gather.28
  102.2 32.4 all-gather.22
  136.8 33.2 all-gather.20
  173.3 55.2 all-gather.30
  253.8 90.6 all-gather.32
  348.2 64.2 all-gather.34
  416.3 66.6 all-gather.36
  513.7 34.4 all-gather.24
  550.3 33.2 all-gather.26
  586.3 55.2 all-gather.38
  644.9 88.2 all-gather.40
  757.0 67.0 all-gather.42
  921.3 53.8 all-reduce.39
  1111.3 53.7 all-reduce.41
  1189.0 21.6 all-reduce.45
  1218.2 107.8 all-reduce.43
  1328.4 79.8 reduce-scatter.22
  1410.4 77.7 reduce-scatter.20
  1490.6 123.2 reduce-scatter.30
  1616.0 126.9 reduce-scatter.28
  1745.2 137.1 reduce-scatter.18
  1884.7 137.4 reduce-scatter.16
  2024.5 242.1 reduce-scatter.26
  2268.9 245.5 reduce-scatter.24
  (6 shorter events, 114.2 us)
where the time goes:
time: 2540 us; the launch traced here: 2530 us
  waiting for transfers between devices  1770 us (70%)
  matrix products  287 us (11%)
  local copies, waits for them, and re-layouts  242 us (10%)
  other arithmetic  114 us (4%)
  blocking collectives  85.8 us (3%)
    reduce_scatter x2, waiting for transfers between devices, on_device(): lax.psum_scatter(grad_mat_gate_up, ('dp', 'ctx'), scatter_dimension=0, ti...  490 us
    reduce_scatter x2, waiting for transfers between devices, on_device(): lax.psum_scatter(grad_mat_in, ('dp', 'ctx'), scatter_dimension=0, tiled=T...  277 us
    reduce_scatter x2, waiting for transfers between devices, on_device(): lax.psum_scatter(grad_mat_down, ('dp', 'ctx'), scatter_dimension=0, tiled...  253 us
    all_gather x2, waiting for transfers between devices, fetch_weights(): lax.all_gather(gate_up_weight[layer_index], ('dp', 'ctx'), axis=0, tiled=...  179 us
    reduce_scatter x2, waiting for transfers between devices, on_device(): lax.psum_scatter(grad_mat_out, ('dp', 'ctx'), scatter_dimension=0, tiled=...  156 us
    all_gather x2, waiting for transfers between devices, fetch_weights(): lax.all_gather(input_weight[layer_index], ('dp', 'ctx'), axis=0, tiled=True)  130 us
    unnamed x3, blocking collectives  65.2 us
    all_gather x2, waiting for transfers between devices, fetch_weights(): lax.all_gather(down_weight[layer_index], ('dp', 'ctx'), axis=0, tiled=True)  64.6 us
  transfers between devices with their start and end apart: 32, of which 26 were waited for; matrix products, arithmetic and copies ran while one was open for 19% of the time, Pallas kernels for 0%

commit v1 on v0

--- a/solution.py
+++ b/solution.py
@@ -1,6 +1,10 @@
+import functools
+
 import jax
 import jax.numpy as jnp
 from jax import lax
+from jax.experimental import pallas as pl
+from jax.experimental.pallas import tpu as pltpu
 from jax.sharding import PartitionSpec as P
 
 FF = 2730
@@ -444,9 +448,556 @@
     )
 
 
+MESH=pl.DeviceIdType.MESH
+RB=64
+
+class Where:
+    def __init__(self):
+        self.dp=lax.axis_index("dp"); self.x=lax.axis_index("ctx"); self.c=lax.axis_index("tp")
+        self.z=self.dp//2; self.y=self.dp%2
+    def nx(self): return (self.dp,1-self.x,self.c)
+    def ny(self): return (self.z*2+1-self.y,self.x,self.c)
+    def up(self): return ((self.z+1)*2+self.y,self.x,self.c)
+    def dn(self): return ((self.z-1)*2+self.y,self.x,self.c)
+
+def greet(w):
+    bar=pltpu.get_barrier_semaphore()
+    def sig(dev): pl.semaphore_signal(bar,inc=1,device_id=dev,device_id_type=MESH)
+    sig(w.nx()); sig(w.ny())
+    @pl.when(w.z<3)
+    def _(): sig(w.up())
+    @pl.when(w.z>0)
+    def _(): sig(w.dn())
+    pl.semaphore_wait(bar,2+(w.z<3).astype(jnp.int32)+(w.z>0).astype(jnp.int32))
+
+class Gather:
+    def __init__(self,w,order,src,out,r0,nr,ssem,rsem,own_sem):
+        self.w,self.order,self.src,self.out,self.r0,self.nr=w,order,src,out,r0,nr
+        self.ssem,self.rsem=ssem,rsem
+        self.pending=[]
+    def rows(self,zz,yy,xx):
+        return pl.ds(pl.multiple_of(((zz*2+yy)*2+xx)*RB+self.r0,16),self.nr)
+    def here(self,zz,yy,xx,own=False):
+        return self.src.at[pl.ds(self.r0,self.nr)] if own else self.out.at[self.rows(zz,yy,xx)]
+    def copy(self,zz,yy,xx,dev,s,r,own=False):
+        return pltpu.make_async_remote_copy(src_ref=self.here(zz,yy,xx,own),dst_ref=self.out.at[self.rows(zz,yy,xx)],
+            send_sem=self.ssem.at[s],recv_sem=self.rsem.at[r],device_id=dev,device_id_type=MESH)
+    def send(self,cond,*a,**k):
+        self.pending.append((cond,a,k))
+        if cond is None: self.copy(*a,**k).start()
+        else:
+            @pl.when(cond)
+            def _(): self.copy(*a,**k).start()
+    def finish_sends(self):
+        for cond,a,k in self.pending:
+            if cond is None: self.copy(*a,**k).wait_send()
+            else:
+                @pl.when(cond)
+                def _(a=a,k=k): self.copy(*a,**k).wait_send()
+    def arrived(self,zz,yy,xx,r):
+        self.copy(zz,yy,xx,self.w.nx(),0,r).wait_recv()
+
+class GatherZ(Gather):
+    def pq(self,zz,pself):
+        w=self.w
+        if self.order=="zyx": return (zz,w.y if pself else 1-w.y,w.x)
+        return (zz,w.y,w.x if pself else 1-w.x)
+    def pdev(self): return self.w.ny() if self.order=="zyx" else self.w.nx()
+    def qdev(self): return self.w.nx() if self.order=="zyx" else self.w.ny()
+    def qcoord(self,zz,pself):
+        w=self.w
+        if self.order=="zyx": return (zz,w.y if pself else 1-w.y,1-w.x)
+        return (zz,1-w.y,w.x if pself else 1-w.x)
+    def emit(self,cond,zz,k,own=False):
+        b=self.pq(zz,True)
+        w=self.w
+        if k<4:
+            c=(w.z<3) if cond is None else jnp.logical_and(cond,w.z<3)
+            self.send(c,*b,w.up(),k,zz,own=own)
+        if k==0 or k>=4:
+            c=(w.z>0) if cond is None else jnp.logical_and(cond,w.z>0)
+            self.send(c,*b,w.dn(),7+(k if k==0 else k-3),zz,own=own)
+        self.send(cond,*b,self.pdev(),11+k,4+zz,own=own)
+        self.send(cond,*b,self.qdev(),18+k,8+zz*2,own=own)
+    def rounds(self):
+        w=self.w
+        self.emit(None,w.z,0,own=True)
+        yield
+        for k in (1,2,3,4):
+            if k<4:
+                for kk,zz,cond in ((k,w.z-k,w.z>=k),(k+3,w.z+k,w.z+k<=3)):
+                    @pl.when(cond)
+                    def _(zz=zz): self.arrived(*self.pq(zz,True),zz)
+                    self.emit(cond,zz,kk)
+            for kk,zz,cond in (((0,w.z,None),) if k==1 else ((k-1,w.z-k+1,w.z>=k-1),(k+2,w.z+k-1,w.z+k-1<=3))):
+                b=self.pq(zz,False)
+                def go(zz=zz,b=b): self.arrived(*b,4+zz)
+                if cond is None: go()
+                else: pl.when(cond)(go)
+                self.send(cond,*b,self.qdev(),25+kk,8+zz*2+1)
+            yield
+    def finish(self):
+        for zz in range(4):
+            for pself in (True,False):
+                self.arrived(*self.qcoord(zz,pself),8+zz*2+(0 if pself else 1))
+        self.finish_sends()
+    NS,NR=32,16
+
+class GatherX(Gather):
+    NS,NR=3+4*7,19
+    def blk(self,zz,j):
+        w=self.w
+        return (zz,w.y if j<2 else 1-w.y,w.x if j%2==0 else 1-w.x)
+    def vert(self,cond,zz,j,k,own=False):
+        w=self.w; b=self.blk(zz,j)
+        if k<4:
+            c=(w.z<3) if cond is None else jnp.logical_and(cond,w.z<3)
+            self.send(c,*b,w.up(),3+j*7+k if k else 3+j*7,3+zz*4+j,own=own)
+        if k==0 or k>=4:
+            c=(w.z>0) if cond is None else jnp.logical_and(cond,w.z>0)
+            self.send(c,*b,w.dn(),3+j*7+(k if k>=4 else 3),3+zz*4+j,own=own)
+    def rounds(self):
+        w=self.w
+        self.send(None,*self.blk(w.z,0),w.nx(),0,0,own=True)
+        self.send(None,*self.blk(w.z,0),w.ny(),1,1,own=True)
+        self.vert(None,w.z,0,0,own=True)
+        yield
+        b=self.blk(w.z,1); self.arrived(*b,0)
+        self.send(None,*b,w.ny(),2,2)
+        self.vert(None,w.z,1,0)
+        self.arrived(*self.blk(w.z,2),1)
+        self.vert(None,w.z,2,0)
+        yield
+        self.arrived(*self.blk(w.z,3),2)
+        self.vert(None,w.z,3,0)
+        yield
+        for k in (1,2,3):
+            for j in range(4):
+                for kk,zz,cond in ((k,w.z-k,w.z>=k),(k+3,w.z+k,w.z+k<=3)):
+                    @pl.when(cond)
+                    def _(zz=zz,j=j): self.arrived(*self.blk(zz,j),3+zz*4+j)
+                    if k<3: self.vert(cond,zz,j,kk)
+                if j%2==1: yield
+    def finish(self):
+        self.finish_sends()
+
+def interleave(gens):
+    gens=list(gens)
+    while gens:
+        for g in list(gens):
+            try: next(g)
+            except StopIteration: gens.remove(g)
+
+def ag_kernel(nz,nx,*refs):
+    n=nz+nx
+    srcs,outs=refs[:n],refs[n:2*n]; sems=refs[2*n:]
+    w=Where()
+    greet(w)
+    parts=[];i=0
+    me=(w.dp*2+w.x)*RB
+    locs=[]
+    for a in range(n):
+        lc=pltpu.make_async_copy(srcs[a],outs[a].at[pl.ds(pl.multiple_of(me,16),RB)],sems[-1].at[a]); lc.start(); locs.append(lc)
+        if a<nz:
+            parts.append(GatherZ(w,"zyx",srcs[a],outs[a],0,32,sems[i],sems[i+1],None)); i+=2
+            parts.append(GatherZ(w,"zxy",srcs[a],outs[a],32,32,sems[i],sems[i+1],None)); i+=2
+        else:
+            parts.append(GatherX(w,"xyz",srcs[a],outs[a],0,64,sems[i],sems[i+1],None)); i+=2
+    interleave([p.rounds() for p in parts])
+    for p in parts: p.finish()
+    for lc in locs: lc.wait()
+
+def all_gather(zs,xs,cid):
+    arrs=list(zs)+list(xs)
+    sems=[]
+    for a in range(len(arrs)):
+        if a<len(zs): sems+=[pltpu.SemaphoreType.DMA((GatherZ.NS,)),pltpu.SemaphoreType.DMA((GatherZ.NR,))]*2
+        else: sems+=[pltpu.SemaphoreType.DMA((GatherX.NS,)),pltpu.SemaphoreType.DMA((GatherX.NR,))]
+    sems.append(pltpu.SemaphoreType.DMA((len(arrs),)))
+    return pl.pallas_call(functools.partial(ag_kernel,len(zs),len(xs)),
+        out_shape=[jax.ShapeDtypeStruct((16*RB,a.shape[1]),a.dtype) for a in arrs],
+        in_specs=[pl.BlockSpec(memory_space=pl.ANY)]*len(arrs),
+        out_specs=[pl.BlockSpec(memory_space=pl.ANY)]*len(arrs),
+        scratch_shapes=sems,
+        compiler_params=pltpu.CompilerParams(collective_id=cid,has_side_effects=True),name=f"gather{cid}")(*arrs)
+
+
+ZORD=(3,0,2,1)
+class Scatter:
+    def __init__(self,w,order,src,out,r0,nr,ssem,rsem,lsem,own,bufs):
+        self.w,self.order,self.src,self.out,self.r0,self.nr=w,order,src,out,r0,nr
+        self.ssem,self.rsem,self.lsem,self.own=ssem,rsem,lsem,own
+        self.bufs=bufs
+        self.pending=[]
+    def rows(self,zz,yy,xx):
+        return pl.ds(pl.multiple_of(((zz*2+yy)*2+xx)*RB+self.r0,16),self.nr)
+    def send(self,cond,src,dst,dev,s,r):
+        mk=lambda: pltpu.make_async_remote_copy(src_ref=src,dst_ref=dst,send_sem=self.ssem.at[s],recv_sem=self.rsem.at[r],device_id=dev,device_id_type=MESH)
+        self.pending.append((cond,mk))
+        if cond is None: mk().start()
+        else: pl.when(cond)(lambda: mk().start())
+    def wait(self,cond,dst,r):
+        def go(): pltpu.make_async_remote_copy(src_ref=dst,dst_ref=dst,send_sem=self.ssem.at[0],recv_sem=self.rsem.at[r],device_id=self.w.nx(),device_id_type=MESH).wait_recv()
+        if cond is None: go()
+        else: pl.when(cond)(go)
+    def finish(self):
+        for cond,mk in self.pending:
+            if cond is None: mk().wait_send()
+            else: pl.when(cond)(lambda mk=mk: mk().wait_send())
+    def total(self,dst,terms,extra=()):
+        def strip(i,_):
+            s=pl.ds(pl.multiple_of(i*16,16),16)
+            t=terms[0][s].astype(jnp.float32)
+            for r in terms[1:]: t=t+r[s].astype(jnp.float32)
+            dst[s]=t.astype(dst.dtype)
+            return 0
+        lax.fori_loop(0,self.nr//16,strip,0)
+
+class ScatterZ(Scatter):
+    NS,NR=16,20
+    def mine(self,zz,pself):
+        w=self.w
+        if self.order=="zyx": return (zz,w.y if pself else 1-w.y,w.x)
+        return (zz,w.y,w.x if pself else 1-w.x)
+    def theirs(self,zz,pself):
+        w=self.w
+        if self.order=="zyx": return (zz,w.y if pself else 1-w.y,1-w.x)
+        return (zz,1-w.y,w.x if pself else 1-w.x)
+    def rounds(self):
+        w=self.w; rq,rp,ru,rd=self.bufs
+        pdev=w.ny() if self.order=="zyx" else w.nx()
+        qdev=w.nx() if self.order=="zyx" else w.ny()
+        self.loc=[]
+        for zz in ZORD:
+            for k in (1,0):
+                self.send(None,self.src.at[self.rows(*self.theirs(zz,k==0))],rq.at[zz*2+k],qdev,zz*2+k,zz*2+k)
+            for k in (1,0):
+                c=pltpu.make_async_copy(self.src.at[self.rows(*self.mine(zz,k==0))],self.own.at[zz*2+k],self.lsem.at[zz*2+k]); c.start(); self.loc.append((zz*2+k,c))
+        loc=dict(self.loc)
+        yield
+        for zz in ZORD:
+            i=zz*2+1
+            loc[i].wait(); self.wait(None,rq.at[i],i)
+            self.total(rq.at[i],[self.own.at[i],rq.at[i]])
+            self.send(None,rq.at[i],rp.at[zz],pdev,8+zz,8+zz)
+            yield
+        for zz in ZORD:
+            i=zz*2
+            loc[i].wait(); self.wait(None,rq.at[i],i)
+            self.wait(None,rp.at[zz],8+zz)
+            base=[self.own.at[i],rq.at[i],rp.at[zz]]
+            if zz>0:
+                @pl.when(w.z==0)
+                def _(): self.total(rp.at[zz],base)
+                @pl.when(jnp.logical_and(w.z>0,w.z<zz))
+                def _():
+                    self.wait(None,ru.at[zz],12+zz)
+                    self.total(rp.at[zz],base+[ru.at[zz]])
+                self.send(w.z<zz,rp.at[zz],ru.at[zz],w.up(),12+zz,12+zz)
+            if zz<3:
+                @pl.when(w.z==3)
+                def _(): self.total(rp.at[zz],base)
+                @pl.when(jnp.logical_and(w.z<3,w.z>zz))
+                def _():
+                    self.wait(None,rd.at[zz],16+zz)
+                    self.total(rp.at[zz],base+[rd.at[zz]])
+                self.send(w.z>zz,rp.at[zz],rd.at[zz],w.dn(),12+zz,16+zz)
+            yield
+        o=self.out.at[pl.ds(self.r0,self.nr)]
+        for zz in range(4):
+            base=[self.own.at[zz*2],rq.at[zz*2],rp.at[zz]]
+            if zz>0: base=base+[ru.at[zz]]
+            if zz<3: base=base+[rd.at[zz]]
+            @pl.when(w.z==zz)
+            def _():
+                if zz>0: self.wait(None,ru.at[zz],12+zz)
+                if zz<3: self.wait(None,rd.at[zz],16+zz)
+                self.total(o,base)
+        yield
+
+class ScatterX(Scatter):
+    NS,NR=19,35
+    def blk(self,zz,j):
+        w=self.w
+        return (zz,w.y if j<2 else 1-w.y,w.x if j%2==0 else 1-w.x)
+    def rounds(self):
+        w=self.w; ru,rd,ry,rx=self.bufs
+        loc={}
+        for zz in ZORD:
+            for j in (3,2,1,0):
+                i=zz*4+j
+                c=pltpu.make_async_copy(self.src.at[self.rows(*self.blk(zz,j))],self.own.at[i],self.lsem.at[i]); c.start(); loc[i]=c
+        for j in (3,2,1,0):
+            for zz in ZORD:
+                i=zz*4+j
+                if zz>0: self.send(w.z==0,self.src.at[self.rows(*self.blk(zz,j))],ru.at[i],w.up(),i,i)
+                if zz<3: self.send(w.z==3,self.src.at[self.rows(*self.blk(zz,j))],rd.at[i],w.dn(),i,16+i)
+        for i in loc: loc[i].wait()
+        yield
+        for j in (3,2,1,0):
+            for zz in ZORD:
+                i=zz*4+j
+                if zz>1:
+                    cu=jnp.logical_and(w.z>0,w.z<zz)
+                    @pl.when(cu)
+                    def _():
+                        self.wait(None,ru.at[i],i)
+                        self.total(ru.at[i],[self.own.at[i],ru.at[i]])
+                    self.send(cu,ru.at[i],ru.at[i],w.up(),i,i)
+                if zz<2:
+                    cd=jnp.logical_and(w.z<3,w.z>zz)
+                    @pl.when(cd)
+                    def _():
+                        self.wait(None,rd.at[i],16+i)
+                        self.total(rd.at[i],[self.own.at[i],rd.at[i]])
+                    self.send(cd,rd.at[i],rd.at[i],w.dn(),i,16+i)
+            yield
+        def zsum(j,dst,extra):
+            for zz in range(4):
+                i=zz*4+j
+                t=[self.own.at[i]]
+                if zz>0: t.append(ru.at[i])
+                if zz<3: t.append(rd.at[i])
+                @pl.when(w.z==zz)
+                def _():
+                    if zz>0: self.wait(None,ru.at[i],i)
+                    if zz<3: self.wait(None,rd.at[i],16+i)
+                    self.total(dst,t+extra)
+        sy=self.bufs_stage
+        for j in (3,2):
+            k=j-2
+            zsum(j,sy.at[k],[])
+            self.send(None,sy.at[k],ry.at[k],w.ny(),16+k,32+k)
+        yield
+        self.wait(None,ry.at[1],33)
+        zsum(1,sy.at[2],[ry.at[1]])
+        self.send(None,sy.at[2],rx.at[0],w.nx(),18,34)
+        yield
+        self.wait(None,ry.at[0],32)
+        self.wait(None,rx.at[0],34)
+        zsum(0,self.out.at[pl.ds(self.r0,self.nr)],[ry.at[0],rx.at[0]])
+        yield
+
+def rs_kernel(nz,nx,*refs):
+    n=nz+nx
+    srcs,outs=refs[:n],refs[n:2*n]; sc=list(refs[2*n:])
+    w=Where(); greet(w)
+    parts=[]
+    for a in range(n):
+        if a<nz:
+            for h,o in ((0,"zyx"),(1,"zxy")):
+                ss,rs,ls,own,rq,rp,ru,rd=[sc.pop(0) for _ in range(8)]
+                parts.append(ScatterZ(w,o,srcs[a],outs[a],h*32,32,ss,rs,ls,own,(rq,rp,ru,rd)))
+        else:
+            ss,rs,ls,own,ru,rd,ry,rx,st=[sc.pop(0) for _ in range(9)]
+            p=ScatterX(w,"xyz",srcs[a],outs[a],0,64,ss,rs,ls,own,(ru,rd,ry,rx)); p.bufs_stage=st
+            parts.append(p)
+    interleave([p.rounds() for p in parts])
+    for p in parts: p.finish()
+
+def reduce_scatter(zs,xs,cid):
+    arrs=list(zs)+list(xs); sc=[]
+    D=pltpu.SemaphoreType.DMA; V=lambda *s: pltpu.VMEM(s,jnp.bfloat16)
+    for a,v in enumerate(arrs):
+        C=v.shape[1]
+        if a<len(zs):
+            for _ in range(2): sc+=[D((ScatterZ.NS,)),D((ScatterZ.NR,)),D((8,)),V(8,32,C),V(8,32,C),V(4,32,C),V(4,32,C),V(4,32,C)]
+        else: sc+=[D((ScatterX.NS,)),D((ScatterX.NR,)),D((16,)),V(16,64,C),V(16,64,C),V(16,64,C),V(2,64,C),V(1,64,C),V(3,64,C)]
+    return pl.pallas_call(functools.partial(rs_kernel,len(zs),len(xs)),
+        out_shape=[jax.ShapeDtypeStruct((RB,v.shape[1]),jnp.float32) for v in arrs],
+        in_specs=[pl.BlockSpec(memory_space=pl.ANY)]*len(arrs),
+        out_specs=[pl.BlockSpec(memory_space=pltpu.VMEM)]*len(arrs),
+        scratch_shapes=sc,
+        compiler_params=pltpu.CompilerParams(collective_id=cid,has_side_effects=True,vmem_limit_bytes=56*2**20),name=f"scatter{cid}")(*arrs)
+
+
+HP = 1408
+XPERM = [(0, 1), (1, 0)]
+
+
+def swap_tp(v):
+    return lax.ppermute(v, "tp", XPERM)
+
+
+def swap_ctx(v):
+    return lax.ppermute(v, "ctx", XPERM)
+
+
+def pair_sum(partial):
+    low = partial.astype(jnp.bfloat16)
+    return low.astype(jnp.float32) + swap_tp(low).astype(jnp.float32)
+
+
+def pair_totals(first, second):
+    both = jnp.stack([jnp.sum(first, axis=-1), jnp.sum(second, axis=-1)])
+    both = both + swap_tp(both)
+    return both[0][:, None], both[1][:, None]
+
+
+def cut_norm(values, gain_vec, shift_vec, full_width):
+    s1, s2 = pair_totals(values, values * values)
+    mean = s1 / full_width
+    inv = lax.rsqrt(s2 / full_width - mean * mean + norm_epsilon)
+    unit = (values - mean) * inv
+    return unit * gain_vec + shift_vec, unit, inv
+
+
+def cut_norm_back(upstream, unit, inv, gain_vec, full_width):
+    weighted = upstream * gain_vec
+    s1, s2 = pair_totals(weighted, weighted * unit)
+    return inv * (weighted - s1 / full_width - unit * (s2 / full_width))
+
+
+def fast_device(
+    tokens_in,
+    cotangent,
+    key_mask,
+    grid_pos,
+    class_index,
+    input_weight,
+    output_weight,
+    gate_up_weight,
+    down_weight,
+    norm_gains,
+    norm_biases,
+    head_gains,
+    head_biases,
+    hidden_gains,
+    hidden_biases,
+):
+    _, rows, model_width = tokens_in.shape
+    dim = head_gains.shape[1]
+    heads = dim // HEAD_DIM
+    hidden = hidden_gains.shape[1]
+    layers = input_weight.shape[0]
+    pad = HP - hidden
+    f32 = jnp.float32
+    bf = jnp.bfloat16
+    places = lax.axis_index("ctx") * rows + jnp.arange(rows, dtype=jnp.int32)
+    not_class = (places != class_index[0]).astype(f32)
+    cosine, sine = rotary_tables(grid_pos.reshape(2, rows), not_class)
+    keep = key_mask.astype(f32).reshape(rows, 1)
+    keep_low = key_mask.astype(bf).reshape(rows)
+    valid_all = jnp.concatenate([keep_low, swap_ctx(keep_low)])
+    gn = norm_gains.astype(f32)
+    bn = norm_biases.astype(f32)
+    gh = head_gains.astype(f32)
+    bh = head_biases.astype(f32)
+    gf = jnp.pad(hidden_gains.astype(f32), ((0, 0), (0, pad)))
+    bfb = jnp.pad(hidden_biases.astype(f32), ((0, 0), (0, 0), (0, pad)))
+    gu = jnp.pad(gate_up_weight, ((0, 0), (0, 0), (0, 0), (0, pad)))
+    first = jnp.concatenate(
+        [
+            input_weight.reshape(layers, RB, 3 * dim),
+            output_weight,
+            gu.reshape(layers, RB, 2 * HP),
+        ],
+        axis=2,
+    )
+    second = jnp.pad(down_weight, ((0, 0), (0, 0), (0, pad)))
+    mats = []
+    for l in range(layers):
+        big, small = all_gather([first[l]], [second[l]], l)
+        mats.append((big[:, : 3 * dim], big[:, 3 * dim : 4 * dim], big[:, 4 * dim :], small))
+    h = tokens_in.astype(f32).reshape(rows, model_width) * keep
+    saved = []
+    for l in range(layers):
+        w_in, w_out, w_gu, w_dn = mats[l]
+        n1, unit1, inv1 = local_norm(h, gn[l, 0], bn[l, 0])
+        n1 = n1.astype(bf)
+        proj = jnp.dot(n1, w_in, preferred_element_type=f32)
+        q = rotate((proj[:, :dim] + bh[l, 0]).reshape(rows, heads, HEAD_DIM), cosine, sine, 1.0)
+        k = rotate(proj[:, dim : 2 * dim].reshape(rows, heads, HEAD_DIM), cosine, sine, 1.0)
+        q = q.astype(bf)
+        k = k.astype(bf).reshape(rows, dim)
+        v = (proj[:, 2 * dim :] + bh[l, 1]).astype(bf)
+        k_all = jnp.concatenate([k, swap_ctx(k)])
+        v_all = jnp.concatenate([v, swap_ctx(v)])
+        att, log_total = attend_forward((q, k_all, v_all, valid_all))
+        u, unit2, inv2 = cut_norm(att, gh[l], bh[l, 2], model_width)
+        u = u.astype(bf)
+        branch = pair_sum(contract_cols(u, w_out))
+        h = h + keep * (branch + bn[l, 2])
+        n2, unit3, inv3 = local_norm(h, gn[l, 1], bn[l, 1])
+        n2 = n2.astype(bf)
+        both = jnp.dot(n2, w_gu, preferred_element_type=f32)
+        gate = both[:, :HP] + bfb[l, 0]
+        up = both[:, HP:] + bfb[l, 1]
+        zn, unit4, inv4 = cut_norm(jax.nn.silu(gate) * up, gf[l], bfb[l, 2], FF)
+        zn = zn.astype(bf)
+        h = h + keep * (pair_sum(contract_cols(zn, w_dn)) + bn[l, 3])
+        saved.append(
+            (n1, unit1, inv1, q, k_all, v_all, log_total, unit2, inv2, u, unit3, inv3, n2, gate, up, unit4, inv4, zn)
+        )
+    activations = h.astype(bf).reshape(1, rows, model_width)
+    g = cotangent.astype(f32).reshape(rows, model_width)
+    mat_grads = [None] * layers
+    vectors = [None] * layers
+    for l in reversed(range(layers)):
+        (n1, unit1, inv1, q, k_all, v_all, log_total, unit2, inv2, u, unit3, inv3, n2, gate, up, unit4, inv4, zn) = saved[l]
+        w_in, w_out, w_gu, w_dn = mats[l]
+        e = keep * g
+        d_bias_down = jnp.sum(e, axis=0)
+        el = e.astype(bf)
+        d_down = contract_rows(el, zn).astype(bf)
+        ezn = jnp.dot(el, w_dn, preferred_element_type=f32)
+        d_gain_hidden = jnp.sum(ezn * unit4, axis=0)
+        d_shift_hidden = jnp.sum(ezn, axis=0)
+        ez = cut_norm_back(ezn, unit4, inv4, gf[l], FF)
+        sg = jax.nn.sigmoid(gate)
+        eu = ez * gate * sg
+        eg = ez * up * sg * (1.0 + gate * (1.0 - sg))
+        egu = jnp.concatenate([eg.astype(bf), eu.astype(bf)], axis=1)
+        d_gu = contract_rows(n2, egu).astype(bf)
+        en2 = pair_sum(contract_cols(egu, w_gu))
+        d_gain2 = jnp.sum(en2 * unit3, axis=0)
+        d_shift2 = jnp.sum(en2, axis=0)
+        g = g + local_norm_back(en2, unit3, inv3, gn[l, 1])
+        e = keep * g
+        d_bias_out = jnp.sum(e, axis=0)
+        el = e.astype(bf)
+        d_out = contract_rows(el, u).astype(bf)
+        ehead = jnp.dot(el, w_out, preferred_element_type=f32)
+        d_gain_head = jnp.sum(ehead * unit2, axis=0)
+        d_shift_head = jnp.sum(ehead, axis=0)
+        eo = cut_norm_back(ehead, unit2, inv2, gh[l], model_width)
+        eo = eo.astype(bf).reshape(rows, heads, HEAD_DIM)
+        dq, dk_all, dv_all = attend_backward((q, k_all, v_all, valid_all, log_total, eo))
+        dk = dk_all[:rows] + swap_ctx(dk_all[rows:].astype(bf)).astype(f32)
+        dv = dv_all[:rows] + swap_ctx(dv_all[rows:].astype(bf)).astype(f32)
+        dq = rotate(dq.reshape(rows, heads, HEAD_DIM), cosine, sine, -1.0).reshape(rows, dim)
+        dk = rotate(dk.reshape(rows, heads, HEAD_DIM), cosine, sine, -1.0).reshape(rows, dim)
+        ep = jnp.concatenate([dq.astype(bf), dk.astype(bf), dv.astype(bf)], axis=1)
+        d_in = contract_rows(n1, ep).astype(bf)
+        en1 = pair_sum(contract_cols(ep, w_in))
+        d_gain1 = jnp.sum(en1 * unit1, axis=0)
+        d_shift1 = jnp.sum(en1, axis=0)
+        g = g + local_norm_back(en1, unit1, inv1, gn[l, 0])
+        mat_grads[l] = reduce_scatter([jnp.concatenate([d_in, d_out, d_gu], axis=1)], [d_down], 2 + l)
+        vectors[l] = (
+            jnp.stack([d_gain1, d_gain2]),
+            jnp.stack([d_shift1, d_shift2, d_bias_out, d_bias_down]),
+            d_gain_head,
+            jnp.stack([jnp.sum(dq, axis=0), jnp.sum(dv, axis=0), d_shift_head]),
+            d_gain_hidden[:hidden],
+            jnp.stack([jnp.sum(eg, axis=0), jnp.sum(eu, axis=0), d_shift_hidden])[:, :hidden],
+        )
+    input_grad = (keep * g).reshape(1, rows, model_width)
+    stacked = tuple(jnp.stack([vectors[l][i] for l in range(layers)]) for i in range(6))
+    summed = lax.psum(stacked, ("dp", "ctx"))
+    bigs = [mat_grads[l][0] for l in range(layers)]
+    g_in = jnp.stack([b[:, : 3 * dim].reshape(RB, 3, dim) for b in bigs])
+    g_out = jnp.stack([b[:, 3 * dim : 4 * dim] for b in bigs])
+    g_gu = jnp.stack([b[:, 4 * dim :].reshape(RB, 2, HP)[:, :, :hidden] for b in bigs])
+    g_dn = jnp.stack([mat_grads[l][1][:, :hidden] for l in range(layers)])
+    return (activations, input_grad, g_in, g_out, g_gu, g_dn) + summed
+
+
 def solution(mesh):
+    sizes = dict(mesh.shape)
+    fits = sizes == {"dp": 8, "ctx": 2, "tp": 2}
     return jax.shard_map(
-        on_device,
+        fast_device if fits else on_device,
         mesh=mesh,
         in_specs=(
             P("dp", "ctx", None),

time: 2540 us -> 1080 us (0.43)
  waiting for transfers between devices: 1770 us -> 136 us
  Pallas kernels: 0 us -> 471 us
  local copies, waits for them, and re-layouts: 242 us -> 91.4 us
  blocking collectives: 85.8 us -> 0 us
  matrix products: 287 us -> 233 us
    reduce_scatter x8 -> x0, waiting for transfers between devices: 1180 us -> none  [the longest x2 490 us: on_device(): lax.psum_scatter(grad_mat_gate_up, ('dp', 'ctx'), scatter_dimension=0, ti...]
    all_gather x12 -> x0, waiting for transfers between devices: 511 us -> none  [the longest x2 179 us: fetch_weights(): lax.all_gather(gate_up_weight[layer_index], ('dp', 'ctx'), axis=0, tiled=...]
    pallas_call x0 -> x4, Pallas kernels: none -> 471 us  [the longest x2 243 us: reduce_scatter(): pl.pallas_call(functools.partial(rs_kernel, len(zs), len(xs)), out_shape=...]
    unnamed x3 -> x0, blocking collectives: 65.2 us -> none
    all_gather x8 -> x0, local copies, waits for them, and re-layouts: 60.1 us -> none  [the longest x2 29.9 us: fetch_weights(): lax.all_gather(gate_up_weight[layer_index], ('dp', 'ctx'), axis=0, tiled=...]
    reshape x6, local copies, waits for them, and re-layouts: 45.3 us -> 7.99 us  [the longest x2 4.78 us: fast_device(): b[:, 4 * dim:].reshape(RB, 2, HP)[:, :, :hidden]]
    ppermute x0 -> x25, waiting for transfers between devices: none -> 29 us  [the longest x9 25.1 us: swap_ctx(): return lax.ppermute(v, 'ctx', XPERM)]
    dot_general x4 -> x0, local copies, waits for them, and re-layouts: 27.3 us -> none  [the longest x2 15.2 us: contract_rows(): lax.dot_general(left, right, (((0,), (0,)), ((), ())), preferred_element_...]
  transfers between devices with their start and end apart: 32 -> 26, of which waited for: 26 -> 10; matrix products, arithmetic and copies ran while one was open for 19% -> 17% of each run, Pallas kernels for 0% -> 21%
where the time goes in v1:
time: 1080 us; the launch traced here: 1070 us
  Pallas kernels  471 us (44%)
  matrix products  233 us (22%)
  waiting for transfers between devices  136 us (13%)
  other arithmetic  106 us (10%)
  local copies, waits for them, and re-layouts  91.4 us (8%)
  between operations  17.7 us (2%)
  starting transfers between devices  16.2 us (2%)
    pallas_call x2, Pallas kernels, reduce_scatter(): pl.pallas_call(functools.partial(rs_kernel, len(zs), len(xs)), out_shape=...  243 us
    pallas_call x2, Pallas kernels, all_gather(): pl.pallas_call(functools.partial(ag_kernel, len(zs), len(xs)), out_shape=...  228 us
    psum x1, waiting for transfers between devices, fast_device(): summed = lax.psum(stacked, ('dp', 'ctx'))  107 us
    dot_general x2, matrix products, attend_backward(): jnp.einsum('hqk,khe->qhe', grad_raw, key_heads, preferred_element_type=jn...  46 us
    dot_general x2, matrix products, attend_backward(): jnp.einsum('hqk,qhe->khe', grad_raw, queries, preferred_element_type=jnp....  45 us
    dot_general x8, matrix products, contract_rows(): lax.dot_general(left, right, (((0,), (0,)), ((), ())), preferred_element_...  33.6 us
    dot_general x8, matrix products, contract_cols(): lax.dot_general(left, right, (((1,), (1,)), ((), ())), preferred_element_...  25.4 us
    ppermute x9, waiting for transfers between devices, swap_ctx(): return lax.ppermute(v, 'ctx', XPERM)  25.1 us
  transfers between devices with their start and end apart: 26, of which 10 were waited for; matrix products, arithmetic and copies ran while one was open for 17% of the time, Pallas kernels for 21%

profile of v1, /device:TPU:0, one launch (start us, length us, event | category | flops | bytes accessed | tf_op | source)
XLA Modules:
  0.0 1072.1 jit_solution(16703252333652349725)
XLA Ops:
  20.2 113.6 %gather0.1 = (bf16[1024,4864]{1,0:T(8,128)(2,1)}, bf16[1024,1408]{1,0:T(8,128)(2,1)}) custom-call(bf16[64,4864]{1,0:T(8,128)(2,1)} %get-tuple-element.183.refs_0_, bf16[64,1408]{1,0:T(8,128)(2,1)} %get-tuple-element.185.refs_1_), custom_call_target="tpu_custom_call" | custom-call | tf_op jit(solution)/shard_map/gather0/pallas_call | solution.py:617
  149.1 5.8 collective-permute-done
  163.2 11.0 %fusion.215 = (f32[8,516]{1,0:T(8,128)S(1)}, f32[8,516,1032]{2,1,0:T(8,128)}) fusion(bf16[516,8,64]{0,2,1:T(8,128)(2,1)} %bitcast.232, bf16[516,8,64]{0,2,1:T(8,128)(2,1)S(1)} %bitcast.230, bf16[516,8,64]{0,2,1:T(8,128)(2,1)S(1)} %bitcast.209, pred[1032]{0:T(1024)(128)(4,1)S(1)} %maximum_compare_fusion), kind=kOutput, calls=%fused_computation.406 | convolution fusion | flops 560182016 | bytes 18643080 | tf_op jit(solution)/shard_map/qhe,khe->hqk/dot_general | solution.py:103
  174.2 9.5 fusion.8
  183.7 9.1 fusion.124
  201.5 6.4 fusion.52
  214.8 114.7 %gather1.1 = (bf16[1024,4864]{1,0:T(8,128)(2,1)}, bf16[1024,1408]{1,0:T(8,128)(2,1)}) custom-call(bf16[64,4864]{1,0:T(8,128)(2,1)} %get-tuple-element.182.refs_0_, bf16[64,1408]{1,0:T(8,128)(2,1)} %get-tuple-element.184.refs_1_), custom_call_target="tpu_custom_call" | custom-call | tf_op jit(solution)/shard_map/gather1/pallas_call | solution.py:617
  343.2 9.9 collective-permute-done.7
  355.9 5.5 collective-permute-done.8
  362.8 8.3 fusion.216
  371.1 9.5 fusion.9
  380.6 9.0 fusion.123
  398.0 6.1 fusion.48
  425.3 6.9 convolution_convert_fusion
  443.7 22.6 %fusion.59 = f32[1032,8,64]{0,2,1:T(8,128)} fusion(bf16[516,8,64]{0,2,1:T(8,128)(2,1)S(1)} %bitcast.237, f32[8,516,1032]{2,1,0:T(8,128)} %get-tuple-element.218, bf16[516,8,64]{0,2,1:T(8,128)(2,1)} %bitcast.241, bf16[1032,8,64]{0,2,1:T(8,128)(2,1)} %bitcast.251, f32[8,516]{1,0:T(8,128)} %log_add_fusion.1, pred[1032]{0:T(1024)(128)(4,1)S(1)} %copy-done.96), kind=kOutput, calls=%fused_computation.51 | convolution fusion | flops 1669962752 | bytes 21285000 | tf_op jit(solution)/shard_map/hqk,qhe->khe/dot_general | solution.py:146
  469.4 8.7 fusion.64
  484.3 23.0 %fusion.33 = f32[8,64,516]{2,1,0:T(8,128)} fusion(f32[8,516,1032]{2,1,0:T(8,128)} %get-tuple-element.218, bf16[516,8,64]{0,2,1:T(8,128)(2,1)} %bitcast.243, bf16[1032,8,64]{0,2,1:T(8,128)(2,1)} %bitcast.252, f32[8,516]{1,0:T(8,128)} %log_add_fusion.1, pred[1032]{0:T(1024)(128)(4,1)S(1)} %copy-done.96, bf16[516,8,64]{0,2,1:T(8,128)(2,1)} %bitcast.235, ...), kind=kOutput, calls=%fused_computation.33 | convolution fusion | flops 1672076288 | bytes 20756616 | tf_op jit(solution)/shard_map/hqk,khe->qhe/dot_general | solution.py:143
  531.4 115.4 %scatter3.1 = (f32[64,4864]{1,0:T(8,128)}, f32[64,1408]{1,0:T(8,128)}) custom-call(bf16[1024,4864]{1,0:T(8,128)(2,1)} %pad_maximum_fusion.1.refs_0_, bf16[1024,1408]{1,0:T(8,128)(2,1)} %convolution_convert_fusion.4.refs_1_), custom_call_target="tpu_custom_call" | custom-call | tf_op jit(solution)/shard_map/scatter3/pallas_call | solution.py:806
  684.6 7.0 convolution_convert_fusion.1
  703.0 22.4 %fusion.54 = f32[1032,8,64]{0,2,1:T(8,128)} fusion(bf16[516,8,64]{0,2,1:T(8,128)(2,1)S(1)} %bitcast.233, f32[8,516,1032]{2,1,0:T(8,128)} %get-tuple-element.214, bf16[516,8,64]{0,2,1:T(8,128)(2,1)} %bitcast.238, bf16[1032,8,64]{0,2,1:T(8,128)(2,1)} %bitcast.248, f32[8,516]{1,0:T(8,128)S(1)} %copy-done.50, pred[1032]{0:T(1024)(128)(4,1)S(1)} %copy-done.96), kind=kOutput, calls=%fused_computation.50 | convolution fusion | flops 1669962752 | bytes 21285000 | tf_op jit(solution)/shard_map/hqk,qhe->khe/dot_general | solution.py:146
  729.6 8.7 fusion.67
  744.5 23.0 %fusion.43 = f32[8,64,516]{2,1,0:T(8,128)} fusion(f32[8,516,1032]{2,1,0:T(8,128)} %get-tuple-element.214, bf16[516,8,64]{0,2,1:T(8,128)(2,1)} %bitcast.240, bf16[1032,8,64]{0,2,1:T(8,128)(2,1)} %bitcast.249, f32[8,516]{1,0:T(8,128)S(1)} %copy-done.50, pred[1032]{0:T(1024)(128)(4,1)S(1)} %copy-done.96, bf16[516,8,64]{0,2,1:T(8,128)(2,1)} %bitcast.231, ...), kind=kOutput, calls=%fused_computation.35 | convolution fusion | flops 1672076288 | bytes 20756616 | tf_op jit(solution)/shard_map/hqk,khe->qhe/dot_general | solution.py:143
  789.5 127.6 %scatter2.1 = (f32[64,4864]{1,0:T(8,128)}, f32[64,1408]{1,0:T(8,128)}) custom-call(bf16[1024,4864]{1,0:T(8,128)(2,1)} %pad_maximum_fusion.refs_0_, bf16[1024,1408]{1,0:T(8,128)(2,1)} %convolution_convert_fusion.5.refs_1_), custom_call_target="tpu_custom_call" | custom-call | tf_op jit(solution)/shard_map/scatter2/pallas_call | solution.py:806
  949.6 107.3 %all-reduce.7.cloned.1.call-done = (f32[2,2,1024]{2,1,0:T(2,128)}, f32[2,4,1024]{2,1,0:T(4,128)}, f32[2,512]{1,0:T(2,128)}, f32[2,3,512]{2,1,0:T(4,128)}, f32[2,1365]{1,0:T(2,128)}, /*index=5*/f32[2,3,1365]{2,1,0:T(4,128)}) async-done(((f32[2,2,1024]{2,1,0:T(2,128)}, f32[2,4,1024]{2,1,0:T(4,128)}, f32[2,512]{1,0:T(2,128)}, f32[2,3,512]{2,1,0:T(4,128)}, f32[2,1365]{1,0:T(2,128)}, ...) | async-done | bytes 109232 | tf_op jit(solution)/shard_map/psum | solution.py:987
  (590 shorter events, 263.7 us)
Async XLA Ops:
  7.2 1049.6 %all-reduce.7.cloned.1.call-start = ((), (), s32[]{:S(2)}) async-start(), calls=%async_computation | async-start | bytes 251904 | tf_op jit(solution)/shard_map/psum | solution.py:987
  8.1 141.0 %collective-permute-start.1 = (bf16[516]{0:T(1024)(128)(2,1)S(1)}, bf16[516]{0:T(1024)(128)(2,1)S(1)}, u32[]{:S(2)}, u32[]{:S(2)}) collective-permute-start(bf16[516]{0:T(1024)(128)(2,1)S(1)} %convert_reduce_fusion), channel_id=1, source_target_pairs={{0,2},{2,0},{1,3},{3,1},{4,6},{6,4},{5,7},{7,5},{8,10},{10,8},{9,1... | collective-permute-start | bytes 3104 | tf_op jit(solution)/shard_map/ppermute | solution.py:823
  139.6 15.4 %collective-permute-start = (bf16[516,512]{1,0:T(8,128)(2,1)}, bf16[516,512]{1,0:T(8,128)(2,1)}, u32[]{:S(2)}, u32[]{:S(2)}) collective-permute-start(bf16[516,512]{1,0:T(8,128)(2,1)} %get-tuple-element.159), channel_id=1, source_target_pairs={{0,2},{2,0},{1,3},{3,1},{4,6},{6,4},{5,7},{7,5},{8,10},{10,8},{9,1... | collective-permute-start | bytes 1585160 | tf_op jit(solution)/shard_map/ppermute | solution.py:823
  145.8 16.1 %collective-permute-start.2 = (bf16[516,512]{1,0:T(8,128)(2,1)}, bf16[516,512]{1,0:T(8,128)(2,1)}, u32[]{:S(2)}, u32[]{:S(2)}) collective-permute-start(bf16[516,512]{1,0:T(8,128)(2,1)} %copy.81), channel_id=1, source_target_pairs={{0,2},{2,0},{1,3},{3,1},{4,6},{6,4},{5,7},{7,5},{8,10},{10,8},{9,1... | collective-permute-start | bytes 1585160 | tf_op jit(solution)/shard_map/ppermute | solution.py:823
  192.9 2.1 collective-permute-start.3
  197.4 2.9 collective-permute-start.4
  214.4 115.2 %collective-permute-start.6 = (bf16[516,1024]{1,0:T(8,128)(2,1)S(1)}, bf16[516,1024]{1,0:T(8,128)(2,1)}, u32[]{:S(2)}, u32[]{:S(2)}) collective-permute-start(bf16[516,1024]{1,0:T(8,128)(2,1)S(1)} %convolution_convert_fusion.7), channel_id=1, source_target_pairs={{0,1},{1,0},{2,3},{3,2},{4,5},{5,4},{6,7},{7,6},{8,9},{9,8},{10,11... | collective-permute-start | bytes 3170312 | tf_op jit(solution)/shard_map/ppermute | solution.py:819
  337.9 15.2 %collective-permute-start.7 = (bf16[516,512]{1,0:T(8,128)(2,1)S(1)}, bf16[516,512]{1,0:T(8,128)(2,1)}, u32[]{:S(2)}, u32[]{:S(2)}) collective-permute-start(bf16[516,512]{1,0:T(8,128)(2,1)S(1)} %get-tuple-element.156), channel_id=1, source_target_pairs={{0,2},{2,0},{1,3},{3,1},{4,6},{6,4},{5,7},{7,5},{8,10},{10,8},{9,1... | collective-permute-start | bytes 1585160 | tf_op jit(solution)/shard_map/ppermute | solution.py:823
  339.8 21.6 %collective-permute-start.8 = (bf16[516,512]{1,0:T(8,128)(2,1)}, bf16[516,512]{1,0:T(8,128)(2,1)}, u32[]{:S(2)}, u32[]{:S(2)}) collective-permute-start(bf16[516,512]{1,0:T(8,128)(2,1)} %copy.87), channel_id=1, source_target_pairs={{0,2},{2,0},{1,3},{3,1},{4,6},{6,4},{5,7},{7,5},{8,10},{10,8},{9,1... | collective-permute-start | bytes 1585160 | tf_op jit(solution)/shard_map/ppermute | solution.py:823
  389.8 1.4 collective-permute-start.9
  393.8 2.9 collective-permute-start.10
  409.1 2.5 collective-permute-start.13
  419.6 12.6 %collective-permute-start.14 = (bf16[516,1024]{1,0:T(8,128)(2,1)S(1)}, bf16[516,1024]{1,0:T(8,128)(2,1)S(1)}, u32[]{:S(2)}, u32[]{:S(2)}) collective-permute-start(bf16[516,1024]{1,0:T(8,128)(2,1)S(1)} %fusion.120), channel_id=1, source_target_pairs={{0,1},{1,0},{2,3},{3,2},{4,5},{5,4},{6,7},{7,6},{8,9},{9,8},{10,11... | collective-permute-start | bytes 3170312 | tf_op jit(solution)/shard_map/ppermute | solution.py:819
  425.0 8.9 collective-permute-start.12
  437.9 2.4 collective-permute-start.15
  468.9 38.5 %collective-permute-start.16 = (bf16[516,512]{1,0:T(8,128)(2,1)}, bf16[516,512]{1,0:T(8,128)(2,1)}, u32[]{:S(2)}, u32[]{:S(2)}) collective-permute-start(bf16[516,512]{1,0:T(8,128)(2,1)} %copy.91), channel_id=1, source_target_pairs={{0,2},{2,0},{1,3},{3,1},{4,6},{6,4},{5,7},{7,5},{8,10},{10,8},{9,1... | collective-permute-start | bytes 1585160 | tf_op jit(solution)/shard_map/ppermute | solution.py:823
  482.8 30.5 %collective-permute-start.17 = (bf16[516,512]{1,0:T(8,128)(2,1)}, bf16[516,512]{1,0:T(8,128)(2,1)}, u32[]{:S(2)}, u32[]{:S(2)}) collective-permute-start(bf16[516,512]{1,0:T(8,128)(2,1)} %copy.93), channel_id=1, source_target_pairs={{0,2},{2,0},{1,3},{3,1},{4,6},{6,4},{5,7},{7,5},{8,10},{10,8},{9,1... | collective-permute-start | bytes 1585160 | tf_op jit(solution)/shard_map/ppermute | solution.py:823
  652.3 8.9 collective-permute-start.18
  674.3 1.8 collective-permute-start.19
  683.8 7.8 collective-permute-start.20
  698.3 1.4 collective-permute-start.21
  728.1 39.4 %collective-permute-start.22 = (bf16[516,512]{1,0:T(8,128)(2,1)}, bf16[516,512]{1,0:T(8,128)(2,1)}, u32[]{:S(2)}, u32[]{:S(2)}) collective-permute-start(bf16[516,512]{1,0:T(8,128)(2,1)} %copy.96), channel_id=1, source_target_pairs={{0,2},{2,0},{1,3},{3,1},{4,6},{6,4},{5,7},{7,5},{8,10},{10,8},{9,1... | collective-permute-start | bytes 1585160 | tf_op jit(solution)/shard_map/ppermute | solution.py:823
  743.9 28.8 %collective-permute-start.23 = (bf16[516,512]{1,0:T(8,128)(2,1)}, bf16[516,512]{1,0:T(8,128)(2,1)}, u32[]{:S(2)}, u32[]{:S(2)}) collective-permute-start(bf16[516,512]{1,0:T(8,128)(2,1)} %copy.98), channel_id=1, source_target_pairs={{0,2},{2,0},{1,3},{3,1},{4,6},{6,4},{5,7},{7,5},{8,10},{10,8},{9,1... | collective-permute-start | bytes 1585160 | tf_op jit(solution)/shard_map/ppermute | solution.py:823
  919.9 18.6 %collective-permute-start.24 = (bf16[516,1024]{1,0:T(8,128)(2,1)}, bf16[516,1024]{1,0:T(8,128)(2,1)}, u32[]{:S(2)}, u32[]{:S(2)}) collective-permute-start(bf16[516,1024]{1,0:T(8,128)(2,1)} %fusion.111), channel_id=1, source_target_pairs={{0,1},{1,0},{2,3},{3,2},{4,5},{5,4},{6,7},{7,6},{8,9},{9,8},{10,11... | collective-permute-start | bytes 3170312 | tf_op jit(solution)/shard_map/ppermute | solution.py:819
  (153 other events, 3383.2 us)
Sparse Core Ops, SparseCore 0:
  943.6 113.1 all-reduce.6

commit v2 on v1

--- a/solution.py
+++ b/solution.py
@@ -448,7 +448,8 @@
     )
 
 
-MESH=pl.DeviceIdType.MESH
+MESH = pl.DeviceIdType.MESH
+
 RB=64
 
 class Where:
@@ -581,46 +582,6 @@
     def finish(self):
         self.finish_sends()
 
-def interleave(gens):
-    gens=list(gens)
-    while gens:
-        for g in list(gens):
-            try: next(g)
-            except StopIteration: gens.remove(g)
-
-def ag_kernel(nz,nx,*refs):
-    n=nz+nx
-    srcs,outs=refs[:n],refs[n:2*n]; sems=refs[2*n:]
-    w=Where()
-    greet(w)
-    parts=[];i=0
-    me=(w.dp*2+w.x)*RB
-    locs=[]
-    for a in range(n):
-        lc=pltpu.make_async_copy(srcs[a],outs[a].at[pl.ds(pl.multiple_of(me,16),RB)],sems[-1].at[a]); lc.start(); locs.append(lc)
-        if a<nz:
-            parts.append(GatherZ(w,"zyx",srcs[a],outs[a],0,32,sems[i],sems[i+1],None)); i+=2
-            parts.append(GatherZ(w,"zxy",srcs[a],outs[a],32,32,sems[i],sems[i+1],None)); i+=2
-        else:
-            parts.append(GatherX(w,"xyz",srcs[a],outs[a],0,64,sems[i],sems[i+1],None)); i+=2
-    interleave([p.rounds() for p in parts])
-    for p in parts: p.finish()
-    for lc in locs: lc.wait()
-
-def all_gather(zs,xs,cid):
-    arrs=list(zs)+list(xs)
-    sems=[]
-    for a in range(len(arrs)):
-        if a<len(zs): sems+=[pltpu.SemaphoreType.DMA((GatherZ.NS,)),pltpu.SemaphoreType.DMA((GatherZ.NR,))]*2
-        else: sems+=[pltpu.SemaphoreType.DMA((GatherX.NS,)),pltpu.SemaphoreType.DMA((GatherX.NR,))]
-    sems.append(pltpu.SemaphoreType.DMA((len(arrs),)))
-    return pl.pallas_call(functools.partial(ag_kernel,len(zs),len(xs)),
-        out_shape=[jax.ShapeDtypeStruct((16*RB,a.shape[1]),a.dtype) for a in arrs],
-        in_specs=[pl.BlockSpec(memory_space=pl.ANY)]*len(arrs),
-        out_specs=[pl.BlockSpec(memory_space=pl.ANY)]*len(arrs),
-        scratch_shapes=sems,
-        compiler_params=pltpu.CompilerParams(collective_id=cid,has_side_effects=True),name=f"gather{cid}")(*arrs)
-
 
 ZORD=(3,0,2,1)
 class Scatter:
@@ -654,7 +615,7 @@
         lax.fori_loop(0,self.nr//16,strip,0)
 
 class ScatterZ(Scatter):
-    NS,NR=16,20
+    NS,NR=16,17
     def mine(self,zz,pself):
         w=self.w
         if self.order=="zyx": return (zz,w.y if pself else 1-w.y,w.x)
@@ -664,7 +625,7 @@
         if self.order=="zyx": return (zz,w.y if pself else 1-w.y,1-w.x)
         return (zz,1-w.y,w.x if pself else 1-w.x)
     def rounds(self):
-        w=self.w; rq,rp,ru,rd=self.bufs
+        w=self.w; rq,rp,ru=self.bufs
         pdev=w.ny() if self.order=="zyx" else w.nx()
         qdev=w.nx() if self.order=="zyx" else w.ny()
         self.loc=[]
@@ -699,29 +660,31 @@
                 def _(): self.total(rp.at[zz],base)
                 @pl.when(jnp.logical_and(w.z<3,w.z>zz))
                 def _():
-                    self.wait(None,rd.at[zz],16+zz)
-                    self.total(rp.at[zz],base+[rd.at[zz]])
-                self.send(w.z>zz,rp.at[zz],rd.at[zz],w.dn(),12+zz,16+zz)
+                    self.wait(None,ru.at[zz],12+zz)
+                    self.total(rp.at[zz],base+[ru.at[zz]])
+                to=jnp.where(w.z-1==zz,4,zz)
+                self.send(w.z>zz,rp.at[zz],ru.at[to],w.dn(),12+zz,12+to)
             yield
         o=self.out.at[pl.ds(self.r0,self.nr)]
         for zz in range(4):
             base=[self.own.at[zz*2],rq.at[zz*2],rp.at[zz]]
             if zz>0: base=base+[ru.at[zz]]
-            if zz<3: base=base+[rd.at[zz]]
+            if zz<3: base=base+[ru.at[4]]
             @pl.when(w.z==zz)
             def _():
                 if zz>0: self.wait(None,ru.at[zz],12+zz)
-                if zz<3: self.wait(None,rd.at[zz],16+zz)
+                if zz<3: self.wait(None,ru.at[4],16)
                 self.total(o,base)
         yield
 
 class ScatterX(Scatter):
-    NS,NR=19,35
+    NS,NR=19,23
     def blk(self,zz,j):
         w=self.w
         return (zz,w.y if j<2 else 1-w.y,w.x if j%2==0 else 1-w.x)
     def rounds(self):
-        w=self.w; ru,rd,ry,rx=self.bufs
+        w=self.w; ru,ry,rx=self.bufs
+        down=lambda zz,j: jnp.where(w.z-1==zz,16+j,zz*4+j)
         loc={}
         for zz in ZORD:
             for j in (3,2,1,0):
@@ -731,7 +694,7 @@
             for zz in ZORD:
                 i=zz*4+j
                 if zz>0: self.send(w.z==0,self.src.at[self.rows(*self.blk(zz,j))],ru.at[i],w.up(),i,i)
-                if zz<3: self.send(w.z==3,self.src.at[self.rows(*self.blk(zz,j))],rd.at[i],w.dn(),i,16+i)
+                if zz<3: self.send(w.z==3,self.src.at[self.rows(*self.blk(zz,j))],ru.at[down(zz,j)],w.dn(),i,down(zz,j))
         for i in loc: loc[i].wait()
         yield
         for j in (3,2,1,0):
@@ -748,104 +711,898 @@
                     cd=jnp.logical_and(w.z<3,w.z>zz)
                     @pl.when(cd)
                     def _():
-                        self.wait(None,rd.at[i],16+i)
-                        self.total(rd.at[i],[self.own.at[i],rd.at[i]])
-                    self.send(cd,rd.at[i],rd.at[i],w.dn(),i,16+i)
+                        self.wait(None,ru.at[i],i)
+                        self.total(ru.at[i],[self.own.at[i],ru.at[i]])
+                    self.send(cd,ru.at[i],ru.at[down(zz,j)],w.dn(),i,down(zz,j))
             yield
         def zsum(j,dst,extra):
             for zz in range(4):
                 i=zz*4+j
                 t=[self.own.at[i]]
                 if zz>0: t.append(ru.at[i])
-                if zz<3: t.append(rd.at[i])
+                if zz<3: t.append(ru.at[16+j])
                 @pl.when(w.z==zz)
                 def _():
                     if zz>0: self.wait(None,ru.at[i],i)
-                    if zz<3: self.wait(None,rd.at[i],16+i)
+                    if zz<3: self.wait(None,ru.at[16+j],16+j)
                     self.total(dst,t+extra)
         sy=self.bufs_stage
         for j in (3,2):
             k=j-2
             zsum(j,sy.at[k],[])
-            self.send(None,sy.at[k],ry.at[k],w.ny(),16+k,32+k)
+            self.send(None,sy.at[k],ry.at[k],w.ny(),16+k,20+k)
         yield
-        self.wait(None,ry.at[1],33)
+        self.wait(None,ry.at[1],21)
         zsum(1,sy.at[2],[ry.at[1]])
-        self.send(None,sy.at[2],rx.at[0],w.nx(),18,34)
+        self.send(None,sy.at[2],rx.at[0],w.nx(),18,22)
         yield
-        self.wait(None,ry.at[0],32)
-        self.wait(None,rx.at[0],34)
+        self.wait(None,ry.at[0],20)
+        self.wait(None,rx.at[0],22)
         zsum(0,self.out.at[pl.ds(self.r0,self.nr)],[ry.at[0],rx.at[0]])
         yield
 
-def rs_kernel(nz,nx,*refs):
-    n=nz+nx
-    srcs,outs=refs[:n],refs[n:2*n]; sc=list(refs[2*n:])
-    w=Where(); greet(w)
-    parts=[]
-    for a in range(n):
-        if a<nz:
-            for h,o in ((0,"zyx"),(1,"zxy")):
-                ss,rs,ls,own,rq,rp,ru,rd=[sc.pop(0) for _ in range(8)]
-                parts.append(ScatterZ(w,o,srcs[a],outs[a],h*32,32,ss,rs,ls,own,(rq,rp,ru,rd)))
+
+F32 = jnp.float32
+BF = jnp.bfloat16
+DMA = pltpu.SemaphoreType.DMA
+EPS = 1e-06
+
+
+class Bag:
+    pass
+
+
+def step_all(gens):
+    gens = list(gens)
+    while gens:
+        for g in list(gens):
+            try:
+                next(g)
+            except StopIteration:
+                gens.remove(g)
+                continue
+            yield
+
+
+def drive(compute, comm, ratio):
+    comm_live = True
+    for _ in compute:
+        for _ in range(ratio):
+            if comm_live:
+                try:
+                    next(comm)
+                except StopIteration:
+                    comm_live = False
+    for _ in comm:
+        pass
+
+
+class GatherSet:
+    def __init__(self, parts, names):
+        self.parts, self.names = parts, names
+
+    def scratch(self):
+        out = []
+        for name, cols, kind in self.parts:
+            if kind == "z":
+                out += [DMA((GatherZ.NS,)), DMA((GatherZ.NR,))] * 2
+            else:
+                out += [DMA((GatherX.NS,)), DMA((GatherX.NR,))]
+        return out + [DMA((len(self.names),))]
+
+    def start(self, w, srcs, outs, sems):
+        sems = list(sems)
+        me = pl.multiple_of((w.dp * 2 + w.x) * RB, 16)
+        self.locs = []
+        for i, name in enumerate(self.names):
+            c = pltpu.make_async_copy(srcs[name], outs[name].at[pl.ds(me, RB)], sems[-1].at[i])
+            c.start()
+            self.locs.append(c)
+        self.live = []
+        for name, cols, kind in self.parts:
+            s, o = srcs[name], outs[name]
+            if cols is not None:
+                s, o = s.at[:, cols[0] : cols[1]], o.at[:, cols[0] : cols[1]]
+            if kind == "z":
+                for r0, order in ((0, "zyx"), (32, "zxy")):
+                    self.live.append(GatherZ(w, order, s, o, r0, 32, sems.pop(0), sems.pop(0), None))
+            else:
+                self.live.append(GatherX(w, "xyz", s, o, 0, 64, sems.pop(0), sems.pop(0), None))
+        return step_all([p.rounds() for p in self.live])
+
+    def finish(self):
+        for p in self.live:
+            p.finish()
+        for c in self.locs:
+            c.wait()
+
+
+class VecSum:
+    def __init__(self, w, src, out, st, rv, ss, rs):
+        self.w, self.src, self.out, self.st, self.rv, self.ss, self.rs = w, src, out, st, rv, ss, rs
+
+    def mk(self, src, k, dev, send):
+        return pltpu.make_async_remote_copy(
+            src_ref=src, dst_ref=self.rv.at[k], send_sem=self.ss.at[send], recv_sem=self.rs.at[k],
+            device_id=dev, device_id_type=MESH)
+
+    def rounds(self):
+        w = self.w
+        st, rv = self.st, self.rv
+        even = w.z % 2 == 0
+        odd = w.z % 2 == 1
+        mid = jnp.logical_and(w.z > 0, w.z < 3)
+        self.mk(self.src, 0, w.nx(), 0).start()
+        yield
+        self.mk(self.src, 0, w.nx(), 0).wait_recv()
+        st[0] = self.src[...] + rv[0]
+        self.mk(st.at[0], 1, w.ny(), 1).start()
+        yield
+        self.mk(self.src, 1, w.ny(), 1).wait_recv()
+        st[1] = st[0] + rv[1]
+        pl.when(even)(lambda: self.mk(st.at[1], 2, w.up(), 2).start())
+        pl.when(odd)(lambda: self.mk(st.at[1], 2, w.dn(), 2).start())
+        yield
+        self.mk(self.src, 2, w.nx(), 2).wait_recv()
+        st[2] = st[1] + rv[2]
+        pl.when(w.z == 1)(lambda: self.mk(st.at[2], 3, w.up(), 3).start())
+        pl.when(w.z == 2)(lambda: self.mk(st.at[2], 3, w.dn(), 3).start())
+        yield
+
+        @pl.when(mid)
+        def _():
+            self.mk(self.src, 3, w.nx(), 3).wait_recv()
+            st[3] = st[2] + rv[3]
+            self.out[...] = st[3]
+
+        pl.when(w.z == 1)(lambda: self.mk(st.at[3], 4, w.dn(), 4).start())
+        pl.when(w.z == 2)(lambda: self.mk(st.at[3], 4, w.up(), 4).start())
+        yield
+
+        @pl.when(jnp.logical_not(mid))
+        def _():
+            self.mk(self.src, 4, w.nx(), 4).wait_recv()
+            self.out[...] = rv[4]
+
+        yield
+
+    def finish(self):
+        w = self.w
+        self.mk(self.src, 0, w.nx(), 0).wait_send()
+        self.mk(self.src, 0, w.nx(), 1).wait_send()
+        self.mk(self.src, 0, w.nx(), 2).wait_send()
+
+        @pl.when(jnp.logical_and(w.z > 0, w.z < 3))
+        def _():
+            self.mk(self.src, 0, w.nx(), 3).wait_send()
+            self.mk(self.src, 0, w.nx(), 4).wait_send()
+
+
+class ScatterSet:
+    def __init__(self, parts, names, widths):
+        self.parts, self.names, self.widths = parts, names, widths
+
+    def scratch(self):
+        V = lambda *s: pltpu.VMEM(s, BF)
+        sc = []
+        for name, cols, kind in self.parts:
+            C = self.widths[name] if cols is None else cols[1] - cols[0]
+            if kind == "z":
+                for _ in range(2):
+                    sc += [DMA((ScatterZ.NS,)), DMA((ScatterZ.NR,)), DMA((8,))]
+                    sc += [V(8, 32, C), V(8, 32, C), V(4, 32, C), V(5, 32, C)]
+            else:
+                sc += [DMA((ScatterX.NS,)), DMA((ScatterX.NR,)), DMA((16,))]
+                sc += [V(16, 64, C), V(20, 64, C), V(2, 64, C), V(1, 64, C), V(3, 64, C)]
+        sc += [pltpu.VMEM((4, 8, HP), F32), pltpu.VMEM((5, 8, HP), F32), DMA((5,)), DMA((5,))]
+        return sc
+
+    def start(self, w, srcs, outs, vec, vec_out, sc):
+        sc = list(sc)
+        self.live = []
+        for name, cols, kind in self.parts:
+            s, o = srcs[name], outs[name]
+            if cols is not None:
+                s, o = s.at[:, cols[0] : cols[1]], o.at[:, cols[0] : cols[1]]
+            if kind == "z":
+                for r0, order in ((0, "zyx"), (32, "zxy")):
+                    ss, rs, ls, own, rq, rp, ru = [sc.pop(0) for _ in range(7)]
+                    self.live.append(ScatterZ(w, order, s, o, r0, 32, ss, rs, ls, own, (rq, rp, ru)))
+            else:
+                ss, rs, ls, own, ru, ry, rx, st = [sc.pop(0) for _ in range(8)]
+                p = ScatterX(w, "xyz", s, o, 0, 64, ss, rs, ls, own, (ru, ry, rx))
+                p.bufs_stage = st
+                self.live.append(p)
+        st, rv, ss, rs = sc
+        self.live.append(VecSum(w, vec, vec_out, st, rv, ss, rs))
+        return step_all([p.rounds() for p in self.live])
+
+    def finish(self):
+        for p in self.live:
+            p.finish()
+
+
+AT_G = GatherSet([("in", None, "z"), ("out", None, "x")], ["in", "out"])
+FF_G = GatherSet([("gu", None, "z"), ("dn", (0, 512), "z"), ("dn", (512, 1408), "x")], ["gu", "dn"])
+
+
+def at_scatter():
+    return ScatterSet([("in", None, "z"), ("out", None, "x")], ["in", "out"], {"in": 1536, "out": 512})
+
+
+def ff_scatter():
+    return ScatterSet(
+        [("gu", None, "z"), ("dn", (0, 512), "z"), ("dn", (512, 1408), "x")], ["gu", "dn"], {"gu": 2816, "dn": 1408}
+    )
+
+
+def rows16(n, fn, step=176):
+    def body(i, _):
+        fn(pl.ds(pl.multiple_of(i * step, 16), step))
+        return 0
+
+    lax.fori_loop(0, n // step, body, 0)
+
+
+def unit_of(x, width):
+    mean = jnp.sum(x, axis=-1, keepdims=True) / width
+    c = x - mean
+    inv = lax.rsqrt(jnp.sum(c * c, axis=-1, keepdims=True) / width + EPS)
+    return c * inv, inv
+
+
+def dot_nn(a, b):
+    return jnp.dot(a, b, preferred_element_type=F32)
+
+
+def dot_nt(a, b):
+    return lax.dot_general(a, b, (((1,), (1,)), ((), ())), preferred_element_type=F32)
+
+
+def dot_tn(a, b):
+    return lax.dot_general(a, b, (((0,), (0,)), ((), ())), preferred_element_type=F32)
+
+
+def tiles(n, size=256):
+    return [(a, min(size, n - a)) for a in range(0, n, size)]
+
+
+def fold8(x):
+    return jnp.sum(x.reshape(x.shape[0] // 8, 8, x.shape[1]), axis=0)
+
+
+def wide(x, n):
+    return jnp.concatenate([x] * (-(-n // 128)), axis=1)[:, :n]
+
+
+def two_cols(a, b):
+    lane = lax.broadcasted_iota(jnp.int32, (a.shape[0], 128), 1)
+    return jnp.where(lane == 0, a, jnp.where(lane == 1, b, 0.0))
+
+
+def turn(x, cos, sin):
+    lane = lax.broadcasted_iota(jnp.int32, x.shape, 1)
+    other = jnp.where((lane // 16) % 2 == 0, pltpu.roll(x, 112, 1), pltpu.roll(x, 16, 1))
+    return x * cos + other * sin
+
+
+def head_lanes(x, t):
+    lane = lax.broadcasted_iota(jnp.int32, x.shape, 1)
+    return jnp.where(lane // 64 == t, x, jnp.zeros_like(x))
+
+
+class Peer:
+    def __init__(self, dev, ss, rs):
+        self.dev, self.ss, self.rs, self.open = dev, ss, rs, []
+
+    def mk(self, src, dst, k):
+        return pltpu.make_async_remote_copy(
+            src_ref=src, dst_ref=dst, send_sem=self.ss.at[k], recv_sem=self.rs.at[k], device_id=self.dev, device_id_type=MESH)
+
+    def send(self, src, dst, k):
+        c = self.mk(src, dst, k)
+        c.start()
+        self.open.append(c)
+
+    def recv(self, dst, k):
+        self.mk(dst, dst, k).wait_recv()
+
+    def finish(self):
+        for c in self.open:
+            c.wait_send()
+
+
+def greet_all(w, links):
+    bar = pltpu.get_barrier_semaphore()
+
+    def sig(dev):
+        pl.semaphore_signal(bar, inc=1, device_id=dev, device_id_type=MESH)
+
+    sig((w.dp, w.x, 1 - w.c))
+    n = jnp.int32(1)
+    if links != "core":
+        sig(w.nx())
+        n = n + 1
+    if links == "all":
+        sig(w.ny())
+        pl.when(w.z < 3)(lambda: sig(w.up()))
+        pl.when(w.z > 0)(lambda: sig(w.dn()))
+        n = n + 1 + (w.z < 3).astype(jnp.int32) + (w.z > 0).astype(jnp.int32)
+    pl.semaphore_wait(bar, n)
+
+
+def run_kernel(body, name, cid, ins, outs, scratch, extra=()):
+    iname, oname, sname = list(ins), list(outs), list(scratch)
+
+    def kernel(*refs):
+        b = Bag()
+        ni, no, ns = len(iname), len(oname), len(sname)
+        for n, r in zip(iname + oname + sname, refs):
+            setattr(b, n, r)
+        b.extra = refs[ni + no + ns :]
+        body(b)
+
+    res = pl.pallas_call(
+        kernel,
+        out_shape=[jax.ShapeDtypeStruct(outs[n][0], outs[n][1]) for n in oname],
+        in_specs=[pl.BlockSpec(memory_space=ins[n][1]) for n in iname],
+        out_specs=[pl.BlockSpec(memory_space=outs[n][2]) for n in oname],
+        scratch_shapes=[scratch[n] for n in sname] + list(extra),
+        compiler_params=pltpu.CompilerParams(collective_id=cid, has_side_effects=True, vmem_limit_bytes=62 * 2**20),
+        name=name,
+    )(*[ins[n][0] for n in iname])
+    return dict(zip(oname, res))
+
+
+VM = pltpu.VMEM
+ANY = pl.ANY
+
+
+def gather_first(srcs, gset, cid):
+    names = gset.names
+
+    def body(b):
+        w = Where()
+        greet(w)
+        g = gset.start(w, {n: getattr(b, "s_" + n) for n in names}, {n: getattr(b, "w_" + n) for n in names}, b.extra)
+        for _ in g:
+            pass
+        gset.finish()
+
+    return run_kernel(
+        body, "gather", cid,
+        {"s_" + n: (srcs[n], ANY) for n in names},
+        {"w_" + n: ((16 * RB, srcs[n].shape[1]), BF, ANY) for n in names},
+        {}, gset.scratch())
+
+
+def attend_body(b, w, R, core, side):
+    hp = b.h.shape[1]
+    rows16(R, lambda s: norm_store(b.n, s, b.h[s], b.vn[0:1, :], b.vn[1:2, :]))
+    yield
+    D = 512
+    for j in range(2):
+        kt = dot_nn(b.n[...], b.w_in[:, D + 256 * j : D + 256 * j + 256])
+        for hf in range(2):
+            l = slice(256 * j + 128 * hf, 256 * j + 128 * hf + 128)
+            b.k[0:R, l] = (turn(kt[:, 128 * hf : 128 * hf + 128], b.cos[...], b.sin[...]) * b.keep[...]).astype(BF)
+        l = slice(256 * j, 256 * j + 256)
+        side.send(b.k.at[pl.ds(0, R), l], b.k.at[pl.ds(R, R), l], 2 * j)
+        vt = dot_nn(b.n[...], b.w_in[:, 2 * D + 256 * j : 2 * D + 256 * j + 256]) + b.vh[2:3, l]
+        b.v[0:R, l] = vt.astype(BF)
+        side.send(b.v.at[pl.ds(0, R), l], b.v.at[pl.ds(R, R), l], 2 * j + 1)
+        yield
+    for j in range(2):
+        qt = dot_nn(b.n[...], b.w_in[:, 256 * j : 256 * j + 256]) + b.vh[1:2, 256 * j : 256 * j + 256]
+        for hf in range(2):
+            l = slice(256 * j + 128 * hf, 256 * j + 128 * hf + 128)
+            b.q[:, l] = (turn(qt[:, 128 * hf : 128 * hf + 128], b.cos[...], b.sin[...]) * 0.125).astype(BF)
+    yield
+    S = 176
+    for p in range(4):
+        l = slice(128 * p, 128 * p + 128)
+        if p % 2 == 0:
+            j = p // 2
+            lj = slice(256 * j, 256 * j + 256)
+            side.recv(b.k.at[pl.ds(R, R), lj], 2 * j)
+            side.recv(b.v.at[pl.ds(R, R), lj], 2 * j + 1)
+        kp = b.k[:, l]
+        vT = b.v[:, l].T
+        halves = []
+        for t in range(2):
+            b.s[...] = dot_nt(kp, head_lanes(b.q[:, l], t))
+
+            def top(i, m):
+                r = pl.ds(pl.multiple_of(i * S, 16), S)
+                x = b.s[r] + wide(b.fill[r], R)
+                return jnp.maximum(m, jnp.max(x.reshape(S // 8, 8, R), axis=0))
+
+            m = lax.fori_loop(0, 2 * R // S, top, jnp.full((8, R), -3.0e38, F32))
+            m = jnp.max(m, axis=0, keepdims=True)
+
+            def expo(i, acc):
+                r = pl.ds(pl.multiple_of(i * S, 16), S)
+                x = jnp.exp(b.s[r] + wide(b.fill[r], R) - m)
+                b.p[r] = x.astype(BF)
+                return acc + jnp.sum(x.reshape(S // 8, 8, R), axis=0)
+
+            tot = lax.fori_loop(0, 2 * R // S, expo, jnp.zeros((8, R), F32))
+            tot = jnp.sum(tot, axis=0, keepdims=True)
+            halves.append(dot_nn(vT[64 * t : 64 * t + 64], b.p[...]) / tot)
+            b.lse[2 * p + t : 2 * p + t + 1, :] = m + jnp.log(tot)
+            yield
+        b.o[:, l] = jnp.concatenate(halves, axis=0).T
+
+    def stats(s):
+        x = b.o[s]
+        b.stat[s] = two_cols(jnp.sum(x, axis=-1, keepdims=True), jnp.sum(x * x, axis=-1, keepdims=True))
+
+    rows16(R, stats)
+    core.send(b.stat, b.rstat, 0)
+    core.recv(b.rstat, 0)
+
+    def unit(s):
+        t = b.stat[s] + b.rstat[s]
+        mean = t[:, 0:1] / hp
+        inv = lax.rsqrt(t[:, 1:2] / hp - mean * mean + EPS)
+        b.st[s] = two_cols(mean, inv)
+        b.u[s] = ((b.o[s] - mean) * inv * b.vh[0:1, :] + b.vh[3:4, :]).astype(BF)
+
+    rows16(R, unit)
+    yield
+    for d in range(4):
+        l = slice(256 * d, 256 * d + 256)
+        b.part[:, l] = dot_nt(b.u[...], b.w_out[256 * d : 256 * d + 256, :]).astype(BF)
+        core.send(b.part.at[:, l], b.rpart.at[:, l], 1 + d)
+        if d % 2 == 1:
+            yield
+    for d in range(4):
+        l = slice(256 * d, 256 * d + 256)
+        core.recv(b.rpart.at[:, l], 1 + d)
+
+    def close(s):
+        x = b.part[s].astype(F32) + b.rpart[s].astype(F32) + b.vn[4:5, :]
+        b.hm[s] = b.h[s] + wide(b.keep[s], x.shape[1]) * x
+
+    rows16(R, close)
+    yield
+
+
+def norm_store(dst, s, x, gain, bias):
+    dst[s] = (unit_of(x, x.shape[1])[0] * gain + bias).astype(BF)
+
+
+def forward_attend(h, tabs, wts, vn, vh, srcs, gset, cid):
+    R, D = h.shape
+
+    def body(b):
+        w = Where()
+        greet_all(w, "all")
+        names = gset.names
+        comm = gset.start(w, {n: getattr(b, "s_" + n) for n in names}, {n: getattr(b, "g_" + n) for n in names}, b.extra)
+        core = Peer((w.dp, w.x, 1 - w.c), b.cs, b.cr)
+        side = Peer(w.nx(), b.xs, b.xr)
+        next(comm)
+        drive(attend_body(b, w, R, core, side), comm, 2)
+        gset.finish()
+        core.finish()
+        side.finish()
+
+    ins = {"h": (h, VM), "keep": (tabs["keep"], VM), "fill": (tabs["fill"], VM), "cos": (tabs["cos"], VM),
+           "sin": (tabs["sin"], VM), "w_in": (wts["in"], VM), "w_out": (wts["out"], VM), "vn": (vn, VM), "vh": (vh, VM)}
+    ins.update({"s_" + n: (srcs[n], ANY) for n in gset.names})
+    outs = {"hm": ((R, D), F32, VM), "q": ((R, 512), BF, VM), "k": ((2 * R, 512), BF, VM), "v": ((2 * R, 512), BF, VM),
+            "lse": ((8, R), F32, VM), "o": ((R, 512), F32, VM), "st": ((R, 128), F32, VM)}
+    outs.update({"g_" + n: ((16 * RB, srcs[n].shape[1]), BF, ANY) for n in gset.names})
+    scratch = {"n": pltpu.VMEM((R, D), BF), "s": pltpu.VMEM((2 * R, R), F32), "p": pltpu.VMEM((2 * R, R), BF),
+               "u": pltpu.VMEM((R, 512), BF), "part": pltpu.VMEM((R, D), BF), "rpart": pltpu.VMEM((R, D), BF),
+               "stat": pltpu.VMEM((R, 128), F32), "rstat": pltpu.VMEM((R, 128), F32),
+               "cs": DMA((5,)), "cr": DMA((5,)), "xs": DMA((4,)), "xr": DMA((4,))}
+    return run_kernel(body, "attend", cid, ins, outs, scratch, gset.scratch())
+
+
+def hidden_body(b, w, R, core):
+    rows16(R, lambda s: norm_store(b.n, s, b.hm[s], b.vn[2:3, :], b.vn[3:4, :]))
+    yield
+    for i, (a, n) in enumerate(tiles(HP)):
+        b.gate[:, a : a + n] = dot_nn(b.n[...], b.w_gu[:, a : a + n]) + b.vf[1:2, a : a + n]
+        b.up[:, a : a + n] = dot_nn(b.n[...], b.w_gu[:, HP + a : HP + a + n]) + b.vf[2:3, a : a + n]
+        if i % 2 == 1:
+            yield
+
+    def stats(s):
+        g = b.gate[s]
+        z = g * jax.nn.sigmoid(g) * b.up[s]
+        b.z[s] = z
+        b.stat[s] = two_cols(jnp.sum(z, axis=-1, keepdims=True), jnp.sum(z * z, axis=-1, keepdims=True))
+
+    rows16(R, stats)
+    core.send(b.stat, b.rstat, 0)
+    core.recv(b.rstat, 0)
+    yield
+
+    def unit(s):
+        t = b.stat[s] + b.rstat[s]
+        mean = t[:, 0:1] / FF
+        inv = lax.rsqrt(t[:, 1:2] / FF - mean * mean + EPS)
+        b.st[s] = two_cols(mean, inv)
+        b.zn[s] = ((b.z[s] - mean) * inv * b.vf[0:1, :] + b.vf[3:4, :]).astype(BF)
+
+    rows16(R, unit)
+    yield
+    for d in range(4):
+        l = slice(256 * d, 256 * d + 256)
+        b.part[:, l] = dot_nt(b.zn[...], b.w_dn[256 * d : 256 * d + 256, :]).astype(BF)
+        core.send(b.part.at[:, l], b.rpart.at[:, l], 1 + d)
+        if d % 2 == 1:
+            yield
+    for d in range(4):
+        l = slice(256 * d, 256 * d + 256)
+        core.recv(b.rpart.at[:, l], 1 + d)
+
+    def close(s):
+        x = b.part[s].astype(F32) + b.rpart[s].astype(F32) + b.vn[5:6, :]
+        b.ho[s] = b.hm[s] + wide(b.keep[s], x.shape[1]) * x
+
+    rows16(R, close)
+    yield
+
+
+def forward_hidden(hm, tabs, wts, vn, vf, srcs, gset, cid):
+    R, D = hm.shape
+
+    def body(b):
+        w = Where()
+        greet_all(w, "all" if gset else "core")
+        core = Peer((w.dp, w.x, 1 - w.c), b.cs, b.cr)
+        comp = hidden_body(b, w, R, core)
+        if gset:
+            names = gset.names
+            comm = gset.start(w, {n: getattr(b, "s_" + n) for n in names}, {n: getattr(b, "g_" + n) for n in names}, b.extra)
+            next(comm)
+            drive(comp, comm, 2)
+            gset.finish()
         else:
-            ss,rs,ls,own,ru,rd,ry,rx,st=[sc.pop(0) for _ in range(9)]
-            p=ScatterX(w,"xyz",srcs[a],outs[a],0,64,ss,rs,ls,own,(ru,rd,ry,rx)); p.bufs_stage=st
-            parts.append(p)
-    interleave([p.rounds() for p in parts])
-    for p in parts: p.finish()
-
-def reduce_scatter(zs,xs,cid):
-    arrs=list(zs)+list(xs); sc=[]
-    D=pltpu.SemaphoreType.DMA; V=lambda *s: pltpu.VMEM(s,jnp.bfloat16)
-    for a,v in enumerate(arrs):
-        C=v.shape[1]
-        if a<len(zs):
-            for _ in range(2): sc+=[D((ScatterZ.NS,)),D((ScatterZ.NR,)),D((8,)),V(8,32,C),V(8,32,C),V(4,32,C),V(4,32,C),V(4,32,C)]
-        else: sc+=[D((ScatterX.NS,)),D((ScatterX.NR,)),D((16,)),V(16,64,C),V(16,64,C),V(16,64,C),V(2,64,C),V(1,64,C),V(3,64,C)]
-    return pl.pallas_call(functools.partial(rs_kernel,len(zs),len(xs)),
-        out_shape=[jax.ShapeDtypeStruct((RB,v.shape[1]),jnp.float32) for v in arrs],
-        in_specs=[pl.BlockSpec(memory_space=pl.ANY)]*len(arrs),
-        out_specs=[pl.BlockSpec(memory_space=pltpu.VMEM)]*len(arrs),
-        scratch_shapes=sc,
-        compiler_params=pltpu.CompilerParams(collective_id=cid,has_side_effects=True,vmem_limit_bytes=56*2**20),name=f"scatter{cid}")(*arrs)
+            for _ in comp:
+                pass
+        core.finish()
+
+    ins = {"hm": (hm, VM), "keep": (tabs["keep"], VM), "w_gu": (wts["gu"], VM), "w_dn": (wts["dn"], VM), "vn": (vn, VM), "vf": (vf, VM)}
+    outs = {"ho": ((R, D), F32, VM), "gate": ((R, HP), F32, VM), "up": ((R, HP), F32, VM), "st": ((R, 128), F32, VM)}
+    if gset:
+        ins.update({"s_" + n: (srcs[n], ANY) for n in gset.names})
+        outs.update({"g_" + n: ((16 * RB, srcs[n].shape[1]), BF, ANY) for n in gset.names})
+    scratch = {"n": pltpu.VMEM((R, D), BF), "z": pltpu.VMEM((R, HP), F32), "zn": pltpu.VMEM((R, HP), BF),
+               "part": pltpu.VMEM((R, D), BF), "rpart": pltpu.VMEM((R, D), BF),
+               "stat": pltpu.VMEM((R, 128), F32), "rstat": pltpu.VMEM((R, 128), F32), "cs": DMA((5,)), "cr": DMA((5,))}
+    return run_kernel(body, "hidden", cid, ins, outs, scratch, gset.scratch() if gset else ())
+
+
+def add8(acc, x):
+    acc[...] = acc[...] + fold8(x)
+
+
+def put_vec(b, row, acc, n):
+    b.vec[row : row + 1, 0:n] = jnp.sum(acc[...], axis=0, keepdims=True)
+
+
+def close_back(b, s, x, gain, acc_gain, acc_shift):
+    e = b.part[s].astype(F32) + b.rpart[s].astype(F32)
+    unit, inv = unit_of(x, x.shape[1])
+    add8(acc_gain, e * unit)
+    add8(acc_shift, e)
+    wt = e * gain
+    n = x.shape[1]
+    m1 = jnp.sum(wt, axis=-1, keepdims=True) / n
+    m2 = jnp.sum(wt * unit, axis=-1, keepdims=True) / n
+    b.go[s] = b.g[s] + inv * (wt - m1 - unit * m2)
+
+
+def hidden_back_body(b, w, R, core):
+    D = b.g.shape[1]
+    for a in (b.a0, b.a1, b.a2, b.a3, b.a4, b.a5, b.a6, b.vec):
+        a[...] = jnp.zeros_like(a)
+
+    def unit4(s):
+        g = b.gate[s]
+        sg = jax.nn.sigmoid(g)
+        return (g * sg * b.up[s] - b.st[s, 0:1]) * b.st[s, 1:2], g, sg
+
+    def first(s):
+        e = wide(b.keep[s], D) * b.g[s]
+        b.el[s] = e.astype(BF)
+        add8(b.a2, e)
+        norm_store(b.n, s, b.go[s], b.vn[2:3, :], b.vn[3:4, :])
+        b.zn[s] = (unit4(s)[0] * b.vf[0:1, :] + b.vf[3:4, :]).astype(BF)
+
+    rows16(R, first)
+    yield
+    for i, (a, n) in enumerate(tiles(HP)):
+        b.ez[:, a : a + n] = dot_nn(b.el[...], b.w_dn[:, a : a + n])
+        if i % 3 == 2:
+            yield
+
+    def second(s):
+        u = unit4(s)[0]
+        e = b.ez[s]
+        wt = e * b.vf[0:1, :]
+        add8(b.a3, e * u)
+        add8(b.a6, e)
+        b.stat[s] = two_cols(jnp.sum(wt, axis=-1, keepdims=True), jnp.sum(wt * u, axis=-1, keepdims=True))
+
+    rows16(R, second)
+    core.send(b.stat, b.rstat, 0)
+    b.xT[...] = b.el[...].T
+    yield
+    for i, (a, n) in enumerate(tiles(HP)):
+        b.d_dn[:, a : a + n] = dot_nn(b.xT[...], b.zn[:, a : a + n]).astype(BF)
+        if i % 3 == 2:
+            yield
+    core.recv(b.rstat, 0)
+
+    def third(s):
+        u, g, sg = unit4(s)
+        t = (b.stat[s] + b.rstat[s]) / FF
+        ez = b.st[s, 1:2] * (b.ez[s] * b.vf[0:1, :] - t[:, 0:1] - u * t[:, 1:2])
+        eg = ez * b.up[s] * sg * (1.0 + g * (1.0 - sg))
+        eu = ez * g * sg
+        add8(b.a4, eg)
+        add8(b.a5, eu)
+        b.egu[s, 0:HP] = eg.astype(BF)
+        b.egu[s, HP : 2 * HP] = eu.astype(BF)
+
+    rows16(R, third, 48)
+    yield
+    for d in range(4):
+        l = slice(256 * d, 256 * d + 256)
+        b.part[:, l] = dot_nt(b.egu[...], b.w_gu[256 * d : 256 * d + 256, :]).astype(BF)
+        core.send(b.part.at[:, l], b.rpart.at[:, l], 1 + d)
+        yield
+    b.xT[...] = b.n[...].T
+    for i, (a, n) in enumerate(tiles(2 * HP)):
+        b.d_gu[:, a : a + n] = dot_nn(b.xT[...], b.egu[:, a : a + n]).astype(BF)
+        if i % 3 == 2:
+            yield
+    for d in range(4):
+        l = slice(256 * d, 256 * d + 256)
+        core.recv(b.rpart.at[:, l], 1 + d)
+    rows16(R, lambda s: close_back(b, s, b.go[s], b.vn[2:3, :], b.a0, b.a1))
+    for row, acc, n in ((0, b.a0, D), (1, b.a1, D), (2, b.a2, D), (3, b.a3, HP), (4, b.a4, HP), (5, b.a5, HP), (6, b.a6, HP)):
+        put_vec(b, row, acc, n)
+    yield
+
+
+def attend_back_body(b, w, R, core, side):
+    D = b.g.shape[1]
+    hp = D
+    for a in (b.a0, b.a1, b.a2, b.a3, b.a4, b.a5, b.a6, b.vec):
+        a[...] = jnp.zeros_like(a)
+
+    def first(s):
+        e = wide(b.keep[s], D) * b.g[s]
+        b.el[s] = e.astype(BF)
+        add8(b.a2, e)
+        norm_store(b.n, s, b.go[s], b.vn[0:1, :], b.vn[1:2, :])
+        u = (b.o[s] - b.st[s, 0:1]) * b.st[s, 1:2]
+        b.u[s] = (u * b.vh[0:1, :] + b.vh[3:4, :]).astype(BF)
+
+    rows16(R, first)
+    yield
+    for a, n in tiles(512):
+        b.dq[:, a : a + n] = dot_nn(b.el[...], b.w_out[:, a : a + n])
+
+    def second(s):
+        u = (b.o[s] - b.st[s, 0:1]) * b.st[s, 1:2]
+        e = b.dq[s]
+        wt = e * b.vh[0:1, :]
+        add8(b.a3, e * u)
+        add8(b.a6, e)
+        b.stat[s] = two_cols(jnp.sum(wt, axis=-1, keepdims=True), jnp.sum(wt * u, axis=-1, keepdims=True))
+
+    rows16(R, second)
+    core.send(b.stat, b.rstat, 0)
+    b.xT[...] = b.el[...].T
+    yield
+    for a, n in tiles(512):
+        b.d_out[:, a : a + n] = dot_nn(b.xT[...], b.u[:, a : a + n]).astype(BF)
+    yield
+    core.recv(b.rstat, 0)
+
+    def third(s):
+        u = (b.o[s] - b.st[s, 0:1]) * b.st[s, 1:2]
+        t = (b.stat[s] + b.rstat[s]) / hp
+        b.eo[s] = (b.st[s, 1:2] * (b.dq[s] * b.vh[0:1, :] - t[:, 0:1] - u * t[:, 1:2])).astype(BF)
+
+    rows16(R, third, 48)
+    yield
+    S = 176
+    for p in range(4):
+        l = slice(128 * p, 128 * p + 128)
+        kp = b.k[:, l]
+        vp = b.v[:, l]
+        kT = kp.T
+        dk, dv, dqs = None, None, []
+        for t in range(2):
+            qt = head_lanes(b.q[:, l], t)
+            ot = head_lanes(b.eo[:, l], t)
+            b.s[...] = dot_nt(kp, qt)
+            b.dp[...] = dot_nt(vp, ot)
+            lse = b.lse[2 * p + t : 2 * p + t + 1, :]
+
+            def expo(i, acc):
+                r = pl.ds(pl.multiple_of(i * S, 16), S)
+                x = jnp.exp(b.s[r] + wide(b.fill[r], R) - lse)
+                b.s[r] = x
+                b.p[r] = x.astype(BF)
+                return acc + jnp.sum((x * b.dp[r]).reshape(S // 8, 8, R), axis=0)
+
+            tot = lax.fori_loop(0, 2 * R // S, expo, jnp.zeros((8, R), F32))
+            tot = jnp.sum(tot, axis=0, keepdims=True)
+
+            def grad(i, _):
+                r = pl.ds(pl.multiple_of(i * S, 16), S)
+                b.ds[r] = (b.s[r] * (b.dp[r] - tot)).astype(BF)
+                return 0
+
+            lax.fori_loop(0, 2 * R // S, grad, 0)
+            yield
+            v1 = dot_nn(b.p[...], ot)
+            k1 = dot_nn(b.ds[...], qt)
+            dqs.append(dot_nn(kT[64 * t : 64 * t + 64], b.ds[...]))
+            dv = v1 if t == 0 else dv + v1
+            dk = k1 if t == 0 else dk + k1
+            yield
+        dk = jnp.where(b.fill[:, 0:1] == 0.0, dk, 0.0)
+        b.dq[:, l] = jnp.concatenate(dqs, axis=0).T * 0.125
+        b.dk[:, l] = dk[:R]
+        b.dv[:, l] = dv[:R]
+        l2 = slice(512 + 128 * p, 640 + 128 * p)
+        b.ep[:, l] = dk[R:].astype(BF)
+        b.ep[:, l2] = dv[R:].astype(BF)
+        side.send(b.ep.at[:, l], b.rk.at[:, l], 2 * p)
+        side.send(b.ep.at[:, l2], b.rv.at[:, l], 2 * p + 1)
+    yield
+    side.finish()
+    for p in range(4):
+        l = slice(128 * p, 128 * p + 128)
+        side.recv(b.rk.at[:, l], 2 * p)
+        side.recv(b.rv.at[:, l], 2 * p + 1)
+
+        def last(s):
+            cos, sin = b.cos[s], -b.sin[s]
+            eq = turn(b.dq[s, l], cos, sin)
+            ek = turn(b.dk[s, l] + b.rk[s, l].astype(F32), cos, sin)
+            ev = b.dv[s, l] + b.rv[s, l].astype(F32)
+            b.a4[:, l] = b.a4[:, l] + fold8(eq)
+            b.a5[:, l] = b.a5[:, l] + fold8(ev)
+            b.ep[s, l] = eq.astype(BF)
+            b.ep[s, 512 + 128 * p : 640 + 128 * p] = ek.astype(BF)
+            b.ep[s, 1024 + 128 * p : 1152 + 128 * p] = ev.astype(BF)
+
+        rows16(R, last)
+    yield
+    for d in range(4):
+        l = slice(256 * d, 256 * d + 256)
+        b.part[:, l] = dot_nt(b.ep[...], b.w_in[256 * d : 256 * d + 256, :]).astype(BF)
+        core.send(b.part.at[:, l], b.rpart.at[:, l], 1 + d)
+        if d % 2 == 1:
+            yield
+    b.xT[...] = b.n[...].T
+    for i, (a, n) in enumerate(tiles(1536)):
+        b.d_in[:, a : a + n] = dot_nn(b.xT[...], b.ep[:, a : a + n]).astype(BF)
+        if i % 3 == 2:
+            yield
+    for d in range(4):
+        l = slice(256 * d, 256 * d + 256)
+        core.recv(b.rpart.at[:, l], 1 + d)
+    rows16(R, lambda s: close_back(b, s, b.go[s], b.vn[0:1, :], b.a0, b.a1))
+    for row, acc, n in ((0, b.a0, D), (1, b.a1, D), (2, b.a2, D), (3, b.a3, 512), (4, b.a4, 512), (5, b.a5, 512), (6, b.a6, 512)):
+        put_vec(b, row, acc, n)
+    yield
+
+
+def scatter_args(sset, grads, vec):
+    ins = {"s_" + n: (grads[n], ANY) for n in sset.names}
+    ins["s_vec"] = (vec, VM)
+    outs = {"r_" + n: ((RB, grads[n].shape[1]), F32, VM) for n in sset.names}
+    outs["r_vec"] = ((8, HP), F32, VM)
+    return ins, outs
+
+
+def scatter_start(sset, w, b):
+    n = sset.names
+    return sset.start(w, {i: getattr(b, "s_" + i) for i in n}, {i: getattr(b, "r_" + i) for i in n}, b.s_vec, b.r_vec, b.extra)
+
+
+def backward_hidden(g, fw, hm, tabs, wts, vn, vf, sset, grads, vec, cid):
+    R, D = g.shape
+
+    def body(b):
+        w = Where()
+        greet_all(w, "all" if sset else "core")
+        core = Peer((w.dp, w.x, 1 - w.c), b.cs, b.cr)
+        load = pltpu.make_async_copy(b.hm, b.go, b.ls.at[0])
+        load.start()
+        comp = hidden_back_body(b, w, R, core)
+        if sset:
+            comm = scatter_start(sset, w, b)
+            for _ in sset.live:
+                next(comm)
+            load.wait()
+            drive(comp, comm, 2)
+            sset.finish()
+        else:
+            load.wait()
+            for _ in comp:
+                pass
+        core.finish()
+
+    ins = {"g": (g, VM), "keep": (tabs["keep"], VM), "hm": (hm, ANY), "gate": (fw["gate"], VM), "up": (fw["up"], VM), "st": (fw["st"], VM),
+           "w_gu": (wts["gu"], VM), "w_dn": (wts["dn"], VM), "vn": (vn, VM), "vf": (vf, VM)}
+    outs = {"go": ((R, D), F32, VM), "d_gu": ((D, 2 * HP), BF, VM), "d_dn": ((D, HP), BF, VM), "vec": ((8, HP), F32, VM)}
+    extra = ()
+    if sset:
+        i2, o2 = scatter_args(sset, grads, vec)
+        ins.update(i2)
+        outs.update(o2)
+        extra = sset.scratch()
+    acc = lambda n: pltpu.VMEM((8, n), F32)
+    scratch = {"el": pltpu.VMEM((R, D), BF), "xT": pltpu.VMEM((D, R), BF), "n": pltpu.VMEM((R, D), BF), "ez": pltpu.VMEM((R, HP), F32),
+               "zn": pltpu.VMEM((R, HP), BF), "egu": pltpu.VMEM((R, 2 * HP), BF), "part": pltpu.VMEM((R, D), BF), "rpart": pltpu.VMEM((R, D), BF),
+               "stat": pltpu.VMEM((R, 128), F32), "rstat": pltpu.VMEM((R, 128), F32), "cs": DMA((5,)), "cr": DMA((5,)), "ls": DMA((1,)),
+               "a0": acc(D), "a1": acc(D), "a2": acc(D), "a3": acc(HP), "a4": acc(HP), "a5": acc(HP), "a6": acc(HP)}
+    return run_kernel(body, "hidden_back", cid, ins, outs, scratch, extra)
+
+
+def backward_attend(g, fw, h, tabs, wts, vn, vh, sset, grads, vec, cid):
+    R, D = g.shape
+
+    def body(b):
+        w = Where()
+        greet_all(w, "all")
+        core = Peer((w.dp, w.x, 1 - w.c), b.cs, b.cr)
+        side = Peer(w.nx(), b.xs, b.xr)
+        load = pltpu.make_async_copy(b.h, b.go, b.ls.at[0])
+        load.start()
+        comm = scatter_start(sset, w, b)
+        for _ in sset.live:
+            next(comm)
+        load.wait()
+        drive(attend_back_body(b, w, R, core, side), comm, 2)
+        sset.finish()
+        core.finish()
+
+    ins = {"g": (g, VM), "keep": (tabs["keep"], VM), "h": (h, ANY), "fill": (tabs["fill"], VM), "cos": (tabs["cos"], VM), "sin": (tabs["sin"], VM),
+           "o": (fw["o"], VM), "st": (fw["st"], VM), "q": (fw["q"], VM), "k": (fw["k"], VM), "v": (fw["v"], VM), "lse": (fw["lse"], VM),
+           "w_in": (wts["in"], VM), "w_out": (wts["out"], VM), "vn": (vn, VM), "vh": (vh, VM)}
+    outs = {"go": ((R, D), F32, VM), "d_in": ((D, 1536), BF, VM), "d_out": ((D, 512), BF, VM), "vec": ((8, HP), F32, VM)}
+    i2, o2 = scatter_args(sset, grads, vec)
+    ins.update(i2)
+    outs.update(o2)
+    acc = lambda n: pltpu.VMEM((8, n), F32)
+    B = lambda *s: pltpu.VMEM(s, BF)
+    F = lambda *s: pltpu.VMEM(s, F32)
+    scratch = {"el": B(R, D), "xT": B(D, R), "n": B(R, D), "u": B(R, 512), "eo": B(R, 512), "s": F(2 * R, R), "dp": F(2 * R, R),
+               "p": B(2 * R, R), "ds": B(2 * R, R), "dq": F(R, 512), "dk": F(R, 512), "dv": F(R, 512),
+               "rk": B(R, 512), "rv": B(R, 512), "ep": B(R, 1536), "part": B(R, D), "rpart": B(R, D), "stat": F(R, 128), "rstat": F(R, 128),
+               "cs": DMA((5,)), "cr": DMA((5,)), "ls": DMA((1,)), "xs": DMA((8,)), "xr": DMA((8,)),
+               "a0": acc(D), "a1": acc(D), "a2": acc(D), "a3": acc(512), "a4": acc(512), "a5": acc(512), "a6": acc(512)}
+    return run_kernel(body, "attend_back", cid, ins, outs, scratch, sset.scratch())
+
+
+def scatter_last(sset, grads, vec, cid):
+    def body(b):
+        w = Where()
+        greet(w)
+        for _ in scatter_start(sset, w, b):
+            pass
+        sset.finish()
+
+    ins, outs = scatter_args(sset, grads, vec)
+    return run_kernel(body, "scatter", cid, ins, outs, {}, sset.scratch())
 
 
 HP = 1408
-XPERM = [(0, 1), (1, 0)]
-
-
-def swap_tp(v):
-    return lax.ppermute(v, "tp", XPERM)
-
-
-def swap_ctx(v):
-    return lax.ppermute(v, "ctx", XPERM)
-
-
-def pair_sum(partial):
-    low = partial.astype(jnp.bfloat16)
-    return low.astype(jnp.float32) + swap_tp(low).astype(jnp.float32)
-
-
-def pair_totals(first, second):
-    both = jnp.stack([jnp.sum(first, axis=-1), jnp.sum(second, axis=-1)])
-    both = both + swap_tp(both)
-    return both[0][:, None], both[1][:, None]
-
-
-def cut_norm(values, gain_vec, shift_vec, full_width):
-    s1, s2 = pair_totals(values, values * values)
-    mean = s1 / full_width
-    inv = lax.rsqrt(s2 / full_width - mean * mean + norm_epsilon)
-    unit = (values - mean) * inv
-    return unit * gain_vec + shift_vec, unit, inv
-
-
-def cut_norm_back(upstream, unit, inv, gain_vec, full_width):
-    weighted = upstream * gain_vec
-    s1, s2 = pair_totals(weighted, weighted * unit)
-    return inv * (weighted - s1 / full_width - unit * (s2 / full_width))
 
 
 def fast_device(
@@ -865,132 +1622,88 @@
     hidden_gains,
     hidden_biases,
 ):
-    _, rows, model_width = tokens_in.shape
+    _, rows, width = tokens_in.shape
     dim = head_gains.shape[1]
-    heads = dim // HEAD_DIM
     hidden = hidden_gains.shape[1]
     layers = input_weight.shape[0]
     pad = HP - hidden
-    f32 = jnp.float32
-    bf = jnp.bfloat16
+    R = -(-rows // 16) * 16
+    more = R - rows
     places = lax.axis_index("ctx") * rows + jnp.arange(rows, dtype=jnp.int32)
-    not_class = (places != class_index[0]).astype(f32)
+    not_class = (places != class_index[0]).astype(F32)
     cosine, sine = rotary_tables(grid_pos.reshape(2, rows), not_class)
-    keep = key_mask.astype(f32).reshape(rows, 1)
-    keep_low = key_mask.astype(bf).reshape(rows)
-    valid_all = jnp.concatenate([keep_low, swap_ctx(keep_low)])
-    gn = norm_gains.astype(f32)
-    bn = norm_biases.astype(f32)
-    gh = head_gains.astype(f32)
-    bh = head_biases.astype(f32)
-    gf = jnp.pad(hidden_gains.astype(f32), ((0, 0), (0, pad)))
-    bfb = jnp.pad(hidden_biases.astype(f32), ((0, 0), (0, 0), (0, pad)))
+    c0, c1, s0, s1 = cosine[:, 0], cosine[:, 1], sine[:, 0], sine[:, 1]
+    low = lambda a: jnp.pad(a, ((0, more), (0, 0)))
+    keep = low(key_mask.astype(F32).reshape(rows, 1))
+    fill = jnp.where(jnp.arange(R)[:, None] < rows, (keep - 1.0) * 10000.0, -1.0e30)
+    other = lax.ppermute(fill[:, 0], "ctx", [(0, 1), (1, 0)])[:, None]
+    tabs = {
+        "keep": jnp.broadcast_to(keep, (R, 128)),
+        "fill": jnp.broadcast_to(jnp.concatenate([fill, other]), (2 * R, 128)),
+        "cos": low(jnp.concatenate([c0, c0, c1, c1] * 2, axis=1)),
+        "sin": low(jnp.concatenate([-s0, s0, -s1, s1] * 2, axis=1)),
+    }
+    gn = norm_gains.astype(F32)
+    bn = norm_biases.astype(F32)
+    gh = head_gains.astype(F32)[:, None]
+    bh = head_biases.astype(F32)
+    vh = jnp.pad(jnp.concatenate([gh, bh], axis=1), ((0, 0), (0, 4), (0, 0)))
+    vn = jnp.stack([gn[:, 0], bn[:, 0], gn[:, 1], bn[:, 1], bn[:, 2], bn[:, 3]], axis=1)
+    vn = jnp.pad(vn, ((0, 0), (0, 2), (0, 0)))
+    vf = jnp.concatenate([hidden_gains.astype(F32)[:, None], hidden_biases.astype(F32)], axis=1)
+    vf = jnp.pad(vf, ((0, 0), (0, 4), (0, pad)))
     gu = jnp.pad(gate_up_weight, ((0, 0), (0, 0), (0, 0), (0, pad)))
-    first = jnp.concatenate(
-        [
-            input_weight.reshape(layers, RB, 3 * dim),
-            output_weight,
-            gu.reshape(layers, RB, 2 * HP),
-        ],
-        axis=2,
-    )
-    second = jnp.pad(down_weight, ((0, 0), (0, 0), (0, pad)))
-    mats = []
+    dn = jnp.pad(down_weight, ((0, 0), (0, 0), (0, pad)))
+    at_src = [{"in": input_weight[l].reshape(RB, 3 * dim), "out": output_weight[l]} for l in range(layers)]
+    ff_src = [{"gu": gu[l].reshape(RB, 2 * HP), "dn": dn[l]} for l in range(layers)]
+    grab = lambda d, names: {n: d["g_" + n] for n in names}
+    h = low(tokens_in.astype(F32).reshape(rows, width)) * keep
+    first = gather_first(at_src[0], AT_G, 0)
+    at_w = {0: {n: first["w_" + n] for n in AT_G.names}}
+    ff_w, hs, hms, at_f, ff_f = {}, {}, {}, {}, {}
     for l in range(layers):
-        big, small = all_gather([first[l]], [second[l]], l)
-        mats.append((big[:, : 3 * dim], big[:, 3 * dim : 4 * dim], big[:, 4 * dim :], small))
-    h = tokens_in.astype(f32).reshape(rows, model_width) * keep
-    saved = []
-    for l in range(layers):
-        w_in, w_out, w_gu, w_dn = mats[l]
-        n1, unit1, inv1 = local_norm(h, gn[l, 0], bn[l, 0])
-        n1 = n1.astype(bf)
-        proj = jnp.dot(n1, w_in, preferred_element_type=f32)
-        q = rotate((proj[:, :dim] + bh[l, 0]).reshape(rows, heads, HEAD_DIM), cosine, sine, 1.0)
-        k = rotate(proj[:, dim : 2 * dim].reshape(rows, heads, HEAD_DIM), cosine, sine, 1.0)
-        q = q.astype(bf)
-        k = k.astype(bf).reshape(rows, dim)
-        v = (proj[:, 2 * dim :] + bh[l, 1]).astype(bf)
-        k_all = jnp.concatenate([k, swap_ctx(k)])
-        v_all = jnp.concatenate([v, swap_ctx(v)])
-        att, log_total = attend_forward((q, k_all, v_all, valid_all))
-        u, unit2, inv2 = cut_norm(att, gh[l], bh[l, 2], model_width)
-        u = u.astype(bf)
-        branch = pair_sum(contract_cols(u, w_out))
-        h = h + keep * (branch + bn[l, 2])
-        n2, unit3, inv3 = local_norm(h, gn[l, 1], bn[l, 1])
-        n2 = n2.astype(bf)
-        both = jnp.dot(n2, w_gu, preferred_element_type=f32)
-        gate = both[:, :HP] + bfb[l, 0]
-        up = both[:, HP:] + bfb[l, 1]
-        zn, unit4, inv4 = cut_norm(jax.nn.silu(gate) * up, gf[l], bfb[l, 2], FF)
-        zn = zn.astype(bf)
-        h = h + keep * (pair_sum(contract_cols(zn, w_dn)) + bn[l, 3])
-        saved.append(
-            (n1, unit1, inv1, q, k_all, v_all, log_total, unit2, inv2, u, unit3, inv3, n2, gate, up, unit4, inv4, zn)
-        )
-    activations = h.astype(bf).reshape(1, rows, model_width)
-    g = cotangent.astype(f32).reshape(rows, model_width)
-    mat_grads = [None] * layers
-    vectors = [None] * layers
+        hs[l] = h
+        at_f[l] = forward_attend(h, tabs, at_w[l], vn[l], vh[l], ff_src[l], FF_G, 1 + 2 * l)
+        ff_w[l] = grab(at_f[l], FF_G.names)
+        hms[l] = at_f[l]["hm"]
+        nxt = l + 1 < layers
+        ff_f[l] = forward_hidden(hms[l], tabs, ff_w[l], vn[l], vf[l], at_src[l + 1] if nxt else None, AT_G if nxt else None, 2 + 2 * l)
+        if nxt:
+            at_w[l + 1] = grab(ff_f[l], AT_G.names)
+        h = ff_f[l]["ho"]
+    activations = h[:rows].astype(BF).reshape(1, rows, width)
+    g = low(cotangent.astype(F32).reshape(rows, width))
+    got = {}
+    grads, vec, cid = None, None, 2 * layers + 1
     for l in reversed(range(layers)):
-        (n1, unit1, inv1, q, k_all, v_all, log_total, unit2, inv2, u, unit3, inv3, n2, gate, up, unit4, inv4, zn) = saved[l]
-        w_in, w_out, w_gu, w_dn = mats[l]
-        e = keep * g
-        d_bias_down = jnp.sum(e, axis=0)
-        el = e.astype(bf)
-        d_down = contract_rows(el, zn).astype(bf)
-        ezn = jnp.dot(el, w_dn, preferred_element_type=f32)
-        d_gain_hidden = jnp.sum(ezn * unit4, axis=0)
-        d_shift_hidden = jnp.sum(ezn, axis=0)
-        ez = cut_norm_back(ezn, unit4, inv4, gf[l], FF)
-        sg = jax.nn.sigmoid(gate)
-        eu = ez * gate * sg
-        eg = ez * up * sg * (1.0 + gate * (1.0 - sg))
-        egu = jnp.concatenate([eg.astype(bf), eu.astype(bf)], axis=1)
-        d_gu = contract_rows(n2, egu).astype(bf)
-        en2 = pair_sum(contract_cols(egu, w_gu))
-        d_gain2 = jnp.sum(en2 * unit3, axis=0)
-        d_shift2 = jnp.sum(en2, axis=0)
-        g = g + local_norm_back(en2, unit3, inv3, gn[l, 1])
-        e = keep * g
-        d_bias_out = jnp.sum(e, axis=0)
-        el = e.astype(bf)
-        d_out = contract_rows(el, u).astype(bf)
-        ehead = jnp.dot(el, w_out, preferred_element_type=f32)
-        d_gain_head = jnp.sum(ehead * unit2, axis=0)
-        d_shift_head = jnp.sum(ehead, axis=0)
-        eo = cut_norm_back(ehead, unit2, inv2, gh[l], model_width)
-        eo = eo.astype(bf).reshape(rows, heads, HEAD_DIM)
-        dq, dk_all, dv_all = attend_backward((q, k_all, v_all, valid_all, log_total, eo))
-        dk = dk_all[:rows] + swap_ctx(dk_all[rows:].astype(bf)).astype(f32)
-        dv = dv_all[:rows] + swap_ctx(dv_all[rows:].astype(bf)).astype(f32)
-        dq = rotate(dq.reshape(rows, heads, HEAD_DIM), cosine, sine, -1.0).reshape(rows, dim)
-        dk = rotate(dk.reshape(rows, heads, HEAD_DIM), cosine, sine, -1.0).reshape(rows, dim)
-        ep = jnp.concatenate([dq.astype(bf), dk.astype(bf), dv.astype(bf)], axis=1)
-        d_in = contract_rows(n1, ep).astype(bf)
-        en1 = pair_sum(contract_cols(ep, w_in))
-        d_gain1 = jnp.sum(en1 * unit1, axis=0)
-        d_shift1 = jnp.sum(en1, axis=0)
-        g = g + local_norm_back(en1, unit1, inv1, gn[l, 0])
-        mat_grads[l] = reduce_scatter([jnp.concatenate([d_in, d_out, d_gu], axis=1)], [d_down], 2 + l)
-        vectors[l] = (
-            jnp.stack([d_gain1, d_gain2]),
-            jnp.stack([d_shift1, d_shift2, d_bias_out, d_bias_down]),
-            d_gain_head,
-            jnp.stack([jnp.sum(dq, axis=0), jnp.sum(dv, axis=0), d_shift_head]),
-            d_gain_hidden[:hidden],
-            jnp.stack([jnp.sum(eg, axis=0), jnp.sum(eu, axis=0), d_shift_hidden])[:, :hidden],
-        )
-    input_grad = (keep * g).reshape(1, rows, model_width)
-    stacked = tuple(jnp.stack([vectors[l][i] for l in range(layers)]) for i in range(6))
-    summed = lax.psum(stacked, ("dp", "ctx"))
-    bigs = [mat_grads[l][0] for l in range(layers)]
-    g_in = jnp.stack([b[:, : 3 * dim].reshape(RB, 3, dim) for b in bigs])
-    g_out = jnp.stack([b[:, 3 * dim : 4 * dim] for b in bigs])
-    g_gu = jnp.stack([b[:, 4 * dim :].reshape(RB, 2, HP)[:, :, :hidden] for b in bigs])
-    g_dn = jnp.stack([mat_grads[l][1][:, :hidden] for l in range(layers)])
-    return (activations, input_grad, g_in, g_out, g_gu, g_dn) + summed
+        sset = at_scatter() if grads else None
+        r = backward_hidden(g, ff_f[l], hms[l], tabs, ff_w[l], vn[l], vf[l], sset, grads, vec, cid)
+        if grads:
+            got["at", l + 1] = r
+        g, vec, grads = r["go"], r["vec"], {"gu": r["d_gu"], "dn": r["d_dn"]}
+        r = backward_attend(g, at_f[l], hs[l], tabs, at_w[l], vn[l], vh[l], ff_scatter(), grads, vec, cid + 1)
+        got["ff", l] = r
+        g, vec, grads = r["go"], r["vec"], {"in": r["d_in"], "out": r["d_out"]}
+        cid += 2
+    got["at", 0] = scatter_last(at_scatter(), grads, vec, cid)
+    input_grad = (keep * g)[:rows].reshape(1, rows, width)
+    L = range(layers)
+    va = jnp.stack([got["at", l]["r_vec"] for l in L])
+    vff = jnp.stack([got["ff", l]["r_vec"] for l in L])
+    return (
+        activations,
+        input_grad,
+        jnp.stack([got["at", l]["r_in"].reshape(RB, 3, dim) for l in L]),
+        jnp.stack([got["at", l]["r_out"] for l in L]),
+        jnp.stack([got["ff", l]["r_gu"].reshape(RB, 2, HP)[:, :, :hidden] for l in L]),
+        jnp.stack([got["ff", l]["r_dn"][:, :hidden] for l in L]),
+        jnp.stack([va[:, 0, :width], vff[:, 0, :width]], axis=1),
+        jnp.stack([va[:, 1, :width], vff[:, 1, :width], va[:, 2, :width], vff[:, 2, :width]], axis=1),
+        va[:, 3, :dim],
+        va[:, 4:7, :dim],
+        vff[:, 3, :hidden],
+        vff[:, 4:7, :hidden],
+    )
 
 
 def solution(mesh):

time: 1080 us -> 871 us (0.81)
  Pallas kernels: 471 us -> 814 us
  matrix products: 233 us -> 0 us
  waiting for transfers between devices: 136 us -> 0.01 us
  other arithmetic: 106 us -> 15.1 us
  local copies, waits for them, and re-layouts: 91.4 us -> 29.9 us
  between operations: 17.7 us -> 2.08 us
  starting transfers between devices: 16.2 us -> 3 us
    pallas_call x4 -> x10, Pallas kernels: 471 us -> 814 us  [run_kernel(): pl.pallas_call(kernel, out_shape=[jax.ShapeDtypeStruct(outs[n][0], outs[n...]
    dot_general x34 -> x0, matrix products: 233 us -> none  [the longest x2 46 us: attend_backward(): jnp.einsum('hqk,khe->qhe', grad_raw, key_heads, preferred_element_type=jn...]
    psum x1 -> x0, waiting for transfers between devices: 107 us -> none  [fast_device(): summed = lax.psum(stacked, ('dp', 'ctx'))]
    reduce_sum x24 -> x0, other arithmetic: 52.6 us -> none  [the longest x2 18.9 us: attend_forward(): row_total = jnp.sum(exp_scores, axis=-1, keepdims=True)]
    ppermute x25 -> x1, waiting for transfers between devices: 29 us -> 0.01 us  [fast_device(): other = lax.ppermute(fill[:, 0], 'ctx', [(0, 1), (1, 0)])[:, None]]
    slice x21 -> x7, local copies, waits for them, and re-layouts: 20.4 us -> 2.52 us  [the longest x1 0.77 us: fast_device(): bn[:, 0]]
    ppermute x25 -> x1, starting transfers between devices: 16.1 us -> 3 us  [fast_device(): other = lax.ppermute(fill[:, 0], 'ctx', [(0, 1), (1, 0)])[:, None]]
    another operation x34 -> x6, local copies, waits for them, and re-layouts: 13.2 us -> 0.77 us  [the longest x2 0.57 us: fast_device(): jnp.stack([got['at', l]['r_in'].reshape(RB, 3, dim) for l in L])]
  transfers between devices with their start and end apart: 26 -> 1, of which waited for: 10 -> 0; matrix products, arithmetic and copies ran while one was open for 17% -> 2% of each run, Pallas kernels for 21% -> 5%
where the time goes in v2:
time: 871 us; the launch traced here: 864 us
  Pallas kernels  814 us (93%)
  local copies, waits for them, and re-layouts  29.9 us (3%)
  other arithmetic  15.1 us (2%)
    pallas_call x10, Pallas kernels, run_kernel(): pl.pallas_call(kernel, out_shape=[jax.ShapeDtypeStruct(outs[n][0], outs[n...  814 us
  transfers between devices with their start and end apart: 1, of which 0 were waited for; matrix products, arithmetic and copies ran while one was open for 2% of the time, Pallas kernels for 5%

profile of v2, /device:TPU:0, one launch (start us, length us, event | category | flops | bytes accessed | tf_op | source)
XLA Modules:
  0.0 864.1 jit_solution(1546457793217765801)
XLA Ops:
  1.4 3.0 collective-permute-start
  7.3 1.9 fusion.2
  14.3 1.6 convert_multiply_fusion.refs_0_.refs_2_
  15.9 1.6 pad_convert_fusion.refs_0_
  17.5 2.5 concatenate.18
  20.8 2.5 concatenate.19
  27.4 41.6 %gather.1 = (bf16[1024,1536]{1,0:T(8,128)(2,1)}, bf16[1024,512]{1,0:T(8,128)(2,1)}) custom-call(bf16[64,1536]{1,0:T(8,128)(2,1)} %bitcast.90, bf16[64,512]{1,0:T(8,128)(2,1)} %get-tuple-element.167.refs_1_), custom_call_target="tpu_custom_call" | custom-call | tf_op jit(solution)/shard_map/gather/pallas_call | solution.py:1045
  69.9 1.0 broadcast_in_dim.35.refs_2_.refs_3_
  70.9 111.3 %attend.2 = (f32[528,1024]{1,0:T(8,128)}, bf16[528,512]{1,0:T(8,128)(2,1)}, bf16[1056,512]{1,0:T(8,128)(2,1)}, bf16[1056,512]{1,0:T(8,128)(2,1)}, f32[8,528]{1,0...) custom-call(f32[528,1024]{1,0:T(8,128)} %convert_multiply_fusion.ref, ...), custom_call_target="tpu_custom_call" | custom-call | tf_op jit(solution)/shard_map/attend/pallas_call | solution.py:1045
  182.2 51.2 %hidden.2 = (f32[528,1024]{1,0:T(8,128)}, f32[528,1408]{1,0:T(8,128)}, f32[528,1408]{1,0:T(8,128)}, f32[528,128]{1,0:T(8,128)}, bf16[1024,1536]{1,0:T(8,128)(2,1)}, /*index=5*/bf16[1024,512]{1,0:T(8,128)(2,1)}) custom-call(f32[528,1024]{1,0:T(8,128)} %get-tuple-element.72.refs_0_.refs_2_, f32[528,128]{1,0:T(8,128)} %broadcast_in_dim.31.refs_1_, ...), custom_call_target="tpu_custom_call" | custom-call | tf_op jit(solution)/shard_map/hidden/pallas_call | solution.py:1045
  233.4 112.3 %attend.3 = (f32[528,1024]{1,0:T(8,128)}, bf16[528,512]{1,0:T(8,128)(2,1)}, bf16[1056,512]{1,0:T(8,128)(2,1)}, bf16[1056,512]{1,0:T(8,128)(2,1)}, f32[8,528]{1,0...) custom-call(f32[528,1024]{1,0:T(8,128)} %get-tuple-element.75.refs_0, ...), custom_call_target="tpu_custom_call" | custom-call | tf_op jit(solution)/shard_map/attend/pallas_call | solution.py:1045
  345.8 22.4 %hidden.3 = (f32[528,1024]{1,0:T(8,128)}, f32[528,1408]{1,0:T(8,128)}, f32[528,1408]{1,0:T(8,128)}, f32[528,128]{1,0:T(8,128)}) custom-call(f32[528,1024]{1,0:T(8,128)} %get-tuple-element.78.refs_0_.refs_2_, f32[528,128]{1,0:T(8,128)} %broadcast_in_dim.31.refs_1_, bf16[1024,2816]{1,0:T(8,128)(2,1)} %get-tuple-element.79.refs_2_.refs_6_, ...), custom_call_target="tpu_custom_call" | custom-call | tf_op jit(solution)/shard_map/hidden/pallas_call | solution.py:1045
  368.2 37.6 %hidden_back.2 = (f32[528,1024]{1,0:T(8,128)}, bf16[1024,2816]{1,0:T(8,128)(2,1)}, bf16[1024,1408]{1,0:T(8,128)(2,1)}, f32[8,1408]{1,0:T(8,128)}) custom-call(f32[528,1024]{1,0:T(8,128)} %pad_convert_fusion.refs_0_, f32[528,128]{1,0:T(8,128)} %broadcast_in_dim.31.refs_1_, f32[528,1024]{1,0:T(8,128)} %get-tuple-element.78.refs_0_.refs_2_, ...), custom_call_target="tpu_custom_call" | custom-call | tf_op jit(solution)/shard_map/hidden_back/pallas_call | solution.py:1045
  405.9 126.1 %attend_back.2 = (f32[528,1024]{1,0:T(8,128)}, bf16[1024,1536]{1,0:T(8,128)(2,1)}, bf16[1024,512]{1,0:T(8,128)(2,1)}, f32[8,1408]{1,0:T(8,128)}, f32[64,2816]{1,...) custom-call(f32[528,1024]{1,0:T(8,128)} %get-tuple-element.85.refs_0_, f32[528,128]{1,0:T(8,128)} %broadcast_in_dim.31.refs_1_, ...), custom_call_target="tpu_custom_call" | custom-call | tf_op jit(solution)/shard_map/attend_back/pallas_call | solution.py:1045
  531.9 97.7 %hidden_back.3 = (f32[528,1024]{1,0:T(8,128)}, bf16[1024,2816]{1,0:T(8,128)(2,1)}, bf16[1024,1408]{1,0:T(8,128)(2,1)}, f32[8,1408]{1,0:T(8,128)}, f32[64,1536]{1...) custom-call(f32[528,1024]{1,0:T(8,128)} %get-tuple-element.95.refs_0_, f32[528,128]{1,0:T(8,128)} %broadcast_in_dim.31.refs_1_, ...), custom_call_target="tpu_custom_call" | custom-call | tf_op jit(solution)/shard_map/hidden_back/pallas_call | solution.py:1045
  629.7 134.9 %attend_back.3 = (f32[528,1024]{1,0:T(8,128)}, bf16[1024,1536]{1,0:T(8,128)(2,1)}, bf16[1024,512]{1,0:T(8,128)(2,1)}, f32[8,1408]{1,0:T(8,128)}, f32[64,2816]{1,...) custom-call(f32[528,1024]{1,0:T(8,128)} %get-tuple-element.102.refs_0_, f32[528,128]{1,0:T(8,128)} %broadcast_in_dim.31.refs_1_, ...), custom_call_target="tpu_custom_call" | custom-call | tf_op jit(solution)/shard_map/attend_back/pallas_call | solution.py:1045
  764.6 78.9 %scatter.1 = (f32[64,1536]{1,0:T(8,128)}, f32[64,512]{1,0:T(8,128)}, f32[8,1408]{1,0:T(8,128)}) custom-call(bf16[1024,1536]{1,0:T(8,128)(2,1)} %get-tuple-element.113.refs_0_, bf16[1024,512]{1,0:T(8,128)(2,1)} %get-tuple-element.114.refs_1_, f32[8,1408]{1,0:T(8,128)} %get-tuple-element.115.refs_2_), custom_call_target="tpu_custom_call" | custom-call | tf_op jit(solution)/shard_map/scatter/pallas_call | solution.py:1045
  843.6 1.5 fusion.22
  845.1 1.5 fusion.13
  848.0 2.7 fusion.1
  851.0 3.5 copy.42
  855.4 1.1 copy.43
  861.2 1.8 pad_maximum_fusion
  863.0 0.9 pad_maximum_fusion.2
  (102 shorter events, 20.8 us)
Async XLA Ops:
  1.4 67.6 %collective-permute-start = (f32[528]{0:T(1024)S(1)}, f32[528]{0:T(1024)S(1)}, u32[]{:S(2)}, u32[]{:S(2)}) collective-permute-start(f32[528]{0:T(1024)S(1)} %get-tuple-element.152), channel_id=1, source_target_pairs={{0,2},{2,0},{1,3},{3,1},{4,6},{6,4},{5,7},{7,5},{8,10},{10,8},{9,1... | collective-permute-start | bytes 6344 | tf_op jit(solution)/shard_map/ppermute | solution.py:1639
  5.1 4.3 copy-start.11
  9.2 0.9 copy-start.15
  9.2 1.6 copy-start.18
  9.2 2.2 copy-start.20
  9.2 2.2 copy-start.22
  9.3 2.9 copy-start.3
  9.3 3.5 copy-start.12
  9.4 4.2 copy-start.19
  9.4 4.2 copy-start.21
  9.5 4.9 copy-start.1
  12.8 3.1 copy-start.2
  764.5 79.0 %copy-start.6 = (f32[8,1408]{1,0:T(8,128)S(1)}, f32[8,1408]{1,0:T(8,128)}, u32[]{:S(2)}) copy-start(f32[8,1408]{1,0:T(8,128)} %get-tuple-element.127) | copy-start | bytes 135172
  764.5 79.0 %copy-start.7 = (f32[8,1408]{1,0:T(8,128)S(1)}, f32[8,1408]{1,0:T(8,128)}, u32[]{:S(2)}) copy-start(f32[8,1408]{1,0:T(8,128)} %get-tuple-element.125) | copy-start | bytes 135172
  764.6 79.0 %copy-start.8 = (f32[8,1408]{1,0:T(8,128)S(1)}, f32[8,1408]{1,0:T(8,128)}, u32[]{:S(2)}) copy-start(f32[8,1408]{1,0:T(8,128)} %get-tuple-element.126) | copy-start | bytes 135172
  843.5 7.3 copy-start
  851.0 3.5 copy-start.9
  851.0 3.8 copy-start.10
  855.1 1.4 copy-start.4
  855.3 1.7 copy-start.5
  856.9 1.0 copy-start.13
  857.0 1.0 copy-start.14
  857.0 3.5 copy-start.16
  857.0 3.5 copy-start.17

commit v3 on v2

--- a/solution.py
+++ b/solution.py
@@ -524,13 +524,14 @@
         w=self.w
         self.emit(None,w.z,0,own=True)
         yield
-        for k in (1,2,3,4):
-            if k<4:
-                for kk,zz,cond in ((k,w.z-k,w.z>=k),(k+3,w.z+k,w.z+k<=3)):
-                    @pl.when(cond)
-                    def _(zz=zz): self.arrived(*self.pq(zz,True),zz)
-                    self.emit(cond,zz,kk)
-            for kk,zz,cond in (((0,w.z,None),) if k==1 else ((k-1,w.z-k+1,w.z>=k-1),(k+2,w.z+k-1,w.z+k-1<=3))):
+        for k in (1,2,3):
+            for kk,zz,cond in ((k,w.z-k,w.z>=k),(k+3,w.z+k,w.z+k<=3)):
+                @pl.when(cond)
+                def _(zz=zz): self.arrived(*self.pq(zz,True),zz)
+                self.emit(cond,zz,kk)
+            yield
+        for k in (0,1,2,3):
+            for kk,zz,cond in (((0,w.z,None),) if k==0 else ((k,w.z-k,w.z>=k),(k+3,w.z+k,w.z+k<=3))):
                 b=self.pq(zz,False)
                 def go(zz=zz,b=b): self.arrived(*b,4+zz)
                 if cond is None: go()
@@ -565,12 +566,12 @@
         yield
         b=self.blk(w.z,1); self.arrived(*b,0)
         self.send(None,*b,w.ny(),2,2)
-        self.vert(None,w.z,1,0)
+        yield
+        yield
+        yield
         self.arrived(*self.blk(w.z,2),1)
-        self.vert(None,w.z,2,0)
-        yield
         self.arrived(*self.blk(w.z,3),2)
-        self.vert(None,w.z,3,0)
+        for j in range(1,4): self.vert(None,w.z,j,0)
         yield
         for k in (1,2,3):
             for j in range(4):
@@ -628,53 +629,48 @@
         w=self.w; rq,rp,ru=self.bufs
         pdev=w.ny() if self.order=="zyx" else w.nx()
         qdev=w.nx() if self.order=="zyx" else w.ny()
-        self.loc=[]
+        loc={}
+        for k in (1,0):
+            for zz in ZORD:
+                c=pltpu.make_async_copy(self.src.at[self.rows(*self.mine(zz,k==0))],self.own.at[zz*2+k],self.lsem.at[zz*2+k]); c.start(); loc[zz*2+k]=c
         for zz in ZORD:
-            for k in (1,0):
-                self.send(None,self.src.at[self.rows(*self.theirs(zz,k==0))],rq.at[zz*2+k],qdev,zz*2+k,zz*2+k)
-            for k in (1,0):
-                c=pltpu.make_async_copy(self.src.at[self.rows(*self.mine(zz,k==0))],self.own.at[zz*2+k],self.lsem.at[zz*2+k]); c.start(); self.loc.append((zz*2+k,c))
-        loc=dict(self.loc)
+            self.send(None,self.src.at[self.rows(*self.theirs(zz,False))],rq.at[zz*2+1],qdev,zz*2+1,zz*2+1)
         yield
         for zz in ZORD:
             i=zz*2+1
             loc[i].wait(); self.wait(None,rq.at[i],i)
             self.total(rq.at[i],[self.own.at[i],rq.at[i]])
             self.send(None,rq.at[i],rp.at[zz],pdev,8+zz,8+zz)
+            self.send(None,self.src.at[self.rows(*self.theirs(zz,True))],rq.at[zz*2],qdev,zz*2,zz*2)
             yield
-        for zz in ZORD:
-            i=zz*2
-            loc[i].wait(); self.wait(None,rq.at[i],i)
-            self.wait(None,rp.at[zz],8+zz)
-            base=[self.own.at[i],rq.at[i],rp.at[zz]]
-            if zz>0:
-                @pl.when(w.z==0)
-                def _(): self.total(rp.at[zz],base)
-                @pl.when(jnp.logical_and(w.z>0,w.z<zz))
-                def _():
-                    self.wait(None,ru.at[zz],12+zz)
-                    self.total(rp.at[zz],base+[ru.at[zz]])
-                self.send(w.z<zz,rp.at[zz],ru.at[zz],w.up(),12+zz,12+zz)
-            if zz<3:
-                @pl.when(w.z==3)
-                def _(): self.total(rp.at[zz],base)
-                @pl.when(jnp.logical_and(w.z<3,w.z>zz))
-                def _():
-                    self.wait(None,ru.at[zz],12+zz)
-                    self.total(rp.at[zz],base+[ru.at[zz]])
-                to=jnp.where(w.z-1==zz,4,zz)
-                self.send(w.z>zz,rp.at[zz],ru.at[to],w.dn(),12+zz,12+to)
+        def ready(zz):
+            loc[zz*2].wait(); self.wait(None,rq.at[zz*2],zz*2); self.wait(None,rp.at[zz],8+zz)
+            return [self.own.at[zz*2],rq.at[zz*2],rp.at[zz]]
+        for t in (1,2,3):
+            for i in range(4):
+                for up in (True,False):
+                    m=i if up else 3-i
+                    if m>=t: continue
+                    zz=4-t+m if up else t-1-m
+                    @pl.when(w.z==i)
+                    def _():
+                        terms=ready(zz)
+                        if m>0:
+                            self.wait(None,ru.at[zz],12+zz); terms.append(ru.at[zz])
+                        self.total(rp.at[zz],terms)
+                    if up: self.send(w.z==i,rp.at[zz],ru.at[zz],w.up(),12+zz,12+zz)
+                    else:
+                        to=4 if zz==i-1 else zz
+                        self.send(w.z==i,rp.at[zz],ru.at[to],w.dn(),12+zz,12+to)
             yield
         o=self.out.at[pl.ds(self.r0,self.nr)]
         for zz in range(4):
-            base=[self.own.at[zz*2],rq.at[zz*2],rp.at[zz]]
-            if zz>0: base=base+[ru.at[zz]]
-            if zz<3: base=base+[ru.at[4]]
             @pl.when(w.z==zz)
             def _():
-                if zz>0: self.wait(None,ru.at[zz],12+zz)
-                if zz<3: self.wait(None,ru.at[4],16)
-                self.total(o,base)
+                terms=ready(zz)
+                if zz>0: self.wait(None,ru.at[zz],12+zz); terms.append(ru.at[zz])
+                if zz<3: self.wait(None,ru.at[4],16); terms.append(ru.at[4])
+                self.total(o,terms)
         yield
 
 class ScatterX(Scatter):
@@ -690,31 +686,32 @@
             for j in (3,2,1,0):
                 i=zz*4+j
                 c=pltpu.make_async_copy(self.src.at[self.rows(*self.blk(zz,j))],self.own.at[i],self.lsem.at[i]); c.start(); loc[i]=c
-        for j in (3,2,1,0):
-            for zz in ZORD:
-                i=zz*4+j
-                if zz>0: self.send(w.z==0,self.src.at[self.rows(*self.blk(zz,j))],ru.at[i],w.up(),i,i)
-                if zz<3: self.send(w.z==3,self.src.at[self.rows(*self.blk(zz,j))],ru.at[down(zz,j)],w.dn(),i,down(zz,j))
+        J=(3,2,1,0)
+        for zz in (3,2,1):
+            for j in J: self.send(w.z==0,self.src.at[self.rows(*self.blk(zz,j))],ru.at[zz*4+j],w.up(),zz*4+j,zz*4+j)
+        for zz in (0,1,2):
+            for j in J:
+                to=16+j if zz==2 else zz*4+j
+                self.send(w.z==3,self.src.at[self.rows(*self.blk(zz,j))],ru.at[to],w.dn(),zz*4+j,to)
+        yield
         for i in loc: loc[i].wait()
-        yield
-        for j in (3,2,1,0):
-            for zz in ZORD:
-                i=zz*4+j
-                if zz>1:
-                    cu=jnp.logical_and(w.z>0,w.z<zz)
-                    @pl.when(cu)
-                    def _():
-                        self.wait(None,ru.at[i],i)
-                        self.total(ru.at[i],[self.own.at[i],ru.at[i]])
-                    self.send(cu,ru.at[i],ru.at[i],w.up(),i,i)
-                if zz<2:
-                    cd=jnp.logical_and(w.z<3,w.z>zz)
-                    @pl.when(cd)
-                    def _():
-                        self.wait(None,ru.at[i],i)
-                        self.total(ru.at[i],[self.own.at[i],ru.at[i]])
-                    self.send(cd,ru.at[i],ru.at[down(zz,j)],w.dn(),i,down(zz,j))
-            yield
+        def hop(c,zz,j,up):
+            i=zz*4+j
+            @pl.when(w.z==c)
+            def _():
+                self.wait(None,ru.at[i],i)
+                self.total(ru.at[i],[self.own.at[i],ru.at[i]])
+            if up: self.send(w.z==c,ru.at[i],ru.at[i],w.up(),i,i)
+            else:
+                to=16+j if zz==c-1 else i
+                self.send(w.z==c,ru.at[i],ru.at[to],w.dn(),i,to)
+        for j in J:
+            hop(1,3,j,True); hop(2,0,j,False)
+            if j%2==0: yield
+        for j in J:
+            hop(1,2,j,True); hop(2,1,j,False)
+            hop(2,3,j,True); hop(1,0,j,False)
+            if j%2==0: yield
         def zsum(j,dst,extra):
             for zz in range(4):
                 i=zz*4+j
@@ -748,10 +745,6 @@
 EPS = 1e-06
 
 
-class Bag:
-    pass
-
-
 def step_all(gens):
     gens = list(gens)
     while gens:
@@ -764,22 +757,17 @@
             yield
 
 
-def drive(compute, comm, ratio):
-    comm_live = True
-    for _ in compute:
-        for _ in range(ratio):
-            if comm_live:
-                try:
-                    next(comm)
-                except StopIteration:
-                    comm_live = False
+def drive(compute, comm, plan, rest):
+    for i, _ in enumerate(compute):
+        for _ in range(plan[i] if i < len(plan) else rest):
+            next(comm, None)
     for _ in comm:
         pass
 
 
 class GatherSet:
-    def __init__(self, parts, names):
-        self.parts, self.names = parts, names
+    def __init__(self, parts, names, cut=32):
+        self.parts, self.names, self.cut = parts, names, cut
 
     def scratch(self):
         out = []
@@ -804,8 +792,8 @@
             if cols is not None:
                 s, o = s.at[:, cols[0] : cols[1]], o.at[:, cols[0] : cols[1]]
             if kind == "z":
-                for r0, order in ((0, "zyx"), (32, "zxy")):
-                    self.live.append(GatherZ(w, order, s, o, r0, 32, sems.pop(0), sems.pop(0), None))
+                for r0, nr, order in ((0, self.cut, "zyx"), (self.cut, RB - self.cut, "zxy")):
+                    self.live.append(GatherZ(w, order, s, o, r0, nr, sems.pop(0), sems.pop(0), None))
             else:
                 self.live.append(GatherX(w, "xyz", s, o, 0, 64, sems.pop(0), sems.pop(0), None))
         return step_all([p.rounds() for p in self.live])
@@ -834,19 +822,23 @@
         mid = jnp.logical_and(w.z > 0, w.z < 3)
         self.mk(self.src, 0, w.nx(), 0).start()
         yield
+        yield
         self.mk(self.src, 0, w.nx(), 0).wait_recv()
         st[0] = self.src[...] + rv[0]
         self.mk(st.at[0], 1, w.ny(), 1).start()
+        yield
         yield
         self.mk(self.src, 1, w.ny(), 1).wait_recv()
         st[1] = st[0] + rv[1]
         pl.when(even)(lambda: self.mk(st.at[1], 2, w.up(), 2).start())
         pl.when(odd)(lambda: self.mk(st.at[1], 2, w.dn(), 2).start())
         yield
+        yield
         self.mk(self.src, 2, w.nx(), 2).wait_recv()
         st[2] = st[1] + rv[2]
         pl.when(w.z == 1)(lambda: self.mk(st.at[2], 3, w.up(), 3).start())
         pl.when(w.z == 2)(lambda: self.mk(st.at[2], 3, w.dn(), 3).start())
+        yield
         yield
 
         @pl.when(mid)
@@ -858,12 +850,14 @@
         pl.when(w.z == 1)(lambda: self.mk(st.at[3], 4, w.dn(), 4).start())
         pl.when(w.z == 2)(lambda: self.mk(st.at[3], 4, w.up(), 4).start())
         yield
+        yield
 
         @pl.when(jnp.logical_not(mid))
         def _():
             self.mk(self.src, 4, w.nx(), 4).wait_recv()
             self.out[...] = rv[4]
 
+        yield
         yield
 
     def finish(self):
@@ -879,8 +873,8 @@
 
 
 class ScatterSet:
-    def __init__(self, parts, names, widths):
-        self.parts, self.names, self.widths = parts, names, widths
+    def __init__(self, parts, names, widths, cut=32, vec=True):
+        self.parts, self.names, self.widths, self.cut, self.vec = parts, names, widths, cut, vec
 
     def scratch(self):
         V = lambda *s: pltpu.VMEM(s, BF)
@@ -888,13 +882,14 @@
         for name, cols, kind in self.parts:
             C = self.widths[name] if cols is None else cols[1] - cols[0]
             if kind == "z":
-                for _ in range(2):
+                for nr in (self.cut, RB - self.cut):
                     sc += [DMA((ScatterZ.NS,)), DMA((ScatterZ.NR,)), DMA((8,))]
-                    sc += [V(8, 32, C), V(8, 32, C), V(4, 32, C), V(5, 32, C)]
+                    sc += [V(8, nr, C), V(8, nr, C), V(4, nr, C), V(5, nr, C)]
             else:
                 sc += [DMA((ScatterX.NS,)), DMA((ScatterX.NR,)), DMA((16,))]
                 sc += [V(16, 64, C), V(20, 64, C), V(2, 64, C), V(1, 64, C), V(3, 64, C)]
-        sc += [pltpu.VMEM((4, 8, HP), F32), pltpu.VMEM((5, 8, HP), F32), DMA((5,)), DMA((5,))]
+        if self.vec:
+            sc += [pltpu.VMEM((4, 8, HP), F32), pltpu.VMEM((5, 8, HP), F32), DMA((5,)), DMA((5,))]
         return sc
 
     def start(self, w, srcs, outs, vec, vec_out, sc):
@@ -905,16 +900,17 @@
             if cols is not None:
                 s, o = s.at[:, cols[0] : cols[1]], o.at[:, cols[0] : cols[1]]
             if kind == "z":
-                for r0, order in ((0, "zyx"), (32, "zxy")):
+                for r0, nr, order in ((0, self.cut, "zyx"), (self.cut, RB - self.cut, "zxy")):
                     ss, rs, ls, own, rq, rp, ru = [sc.pop(0) for _ in range(7)]
-                    self.live.append(ScatterZ(w, order, s, o, r0, 32, ss, rs, ls, own, (rq, rp, ru)))
+                    self.live.append(ScatterZ(w, order, s, o, r0, nr, ss, rs, ls, own, (rq, rp, ru)))
             else:
                 ss, rs, ls, own, ru, ry, rx, st = [sc.pop(0) for _ in range(8)]
                 p = ScatterX(w, "xyz", s, o, 0, 64, ss, rs, ls, own, (ru, ry, rx))
                 p.bufs_stage = st
                 self.live.append(p)
-        st, rv, ss, rs = sc
-        self.live.append(VecSum(w, vec, vec_out, st, rv, ss, rs))
+        if self.vec:
+            st, rv, ss, rs = sc
+            self.live.append(VecSum(w, vec, vec_out, st, rv, ss, rs))
         return step_all([p.rounds() for p in self.live])
 
     def finish(self):
@@ -922,18 +918,21 @@
             p.finish()
 
 
+FF_CUT = 16
 AT_G = GatherSet([("in", None, "z"), ("out", None, "x")], ["in", "out"])
-FF_G = GatherSet([("gu", None, "z"), ("dn", (0, 512), "z"), ("dn", (512, 1408), "x")], ["gu", "dn"])
+FF_G = GatherSet([("gu", None, "z"), ("dn", (0, 512), "z"), ("dn", (512, 1408), "x")], ["gu", "dn"], FF_CUT)
 
 
 def at_scatter():
     return ScatterSet([("in", None, "z"), ("out", None, "x")], ["in", "out"], {"in": 1536, "out": 512})
 
 
-def ff_scatter():
-    return ScatterSet(
-        [("gu", None, "z"), ("dn", (0, 512), "z"), ("dn", (512, 1408), "x")], ["gu", "dn"], {"gu": 2816, "dn": 1408}
-    )
+def gu_scatter():
+    return ScatterSet([("gu", (0, 2176), "z"), ("gu", (2176, 2816), "x")], ["gu"], {"gu": 2816}, FF_CUT)
+
+
+def dn_scatter():
+    return ScatterSet([("dn", (0, 1024), "z"), ("dn", (1024, 1408), "x")], ["dn"], {"dn": 1408}, 32, False)
 
 
 def rows16(n, fn, step=176):
@@ -1031,23 +1030,62 @@
     pl.semaphore_wait(bar, n)
 
 
+class Bag:
+    def launch(self):
+        self.coming = {n: pltpu.make_async_copy(h, getattr(self, n), self.ld.at[i]) for i, (n, h) in enumerate(self.loads)}
+        for c in self.coming.values():
+            c.start()
+        self.going = []
+
+    def need(self, *names):
+        for n in names:
+            if n in self.coming:
+                self.coming.pop(n).wait()
+
+    def put(self, name, cols=None):
+        s, d = getattr(self, name), self.stores[name]
+        if cols is not None:
+            s, d = s.at[:, cols[0] : cols[1]], d.at[:, cols[0] : cols[1]]
+        c = pltpu.make_async_copy(s, d, self.so.at[len(self.going)])
+        c.start()
+        self.going.append(c)
+
+    def flush(self):
+        self.need(*list(self.coming))
+        for c in self.going:
+            c.wait()
+
+
 def run_kernel(body, name, cid, ins, outs, scratch, extra=()):
     iname, oname, sname = list(ins), list(outs), list(scratch)
+    ld = [n for n in iname if ins[n][1] == "LD"]
+    so = [n for n in oname if outs[n][2] == "ST"]
+    moved = [pltpu.VMEM(ins[n][0].shape, ins[n][0].dtype) for n in ld] + [pltpu.VMEM(outs[n][0], outs[n][1]) for n in so]
+    moved += [DMA((max(len(ld), 1),)), DMA((16,))]
 
     def kernel(*refs):
         b = Bag()
-        ni, no, ns = len(iname), len(oname), len(sname)
+        ni, no, ns, nm = len(iname), len(oname), len(sname), len(moved)
         for n, r in zip(iname + oname + sname, refs):
             setattr(b, n, r)
-        b.extra = refs[ni + no + ns :]
+        mv = refs[ni + no + ns : ni + no + ns + nm]
+        b.loads = [(n, getattr(b, n)) for n in ld]
+        b.stores = {n: getattr(b, n) for n in so}
+        for n, r in zip(ld + so, mv):
+            setattr(b, n, r)
+        b.ld, b.so = mv[-2:]
+        b.extra = refs[ni + no + ns + nm :]
+        b.launch()
         body(b)
-
+        b.flush()
+
+    place = lambda s: pl.BlockSpec(memory_space=pl.ANY if s in ("LD", "ST") else s)
     res = pl.pallas_call(
         kernel,
         out_shape=[jax.ShapeDtypeStruct(outs[n][0], outs[n][1]) for n in oname],
-        in_specs=[pl.BlockSpec(memory_space=ins[n][1]) for n in iname],
-        out_specs=[pl.BlockSpec(memory_space=outs[n][2]) for n in oname],
-        scratch_shapes=[scratch[n] for n in sname] + list(extra),
+        in_specs=[place(ins[n][1]) for n in iname],
+        out_specs=[place(outs[n][2]) for n in oname],
+        scratch_shapes=[scratch[n] for n in sname] + moved + list(extra),
         compiler_params=pltpu.CompilerParams(collective_id=cid, has_side_effects=True, vmem_limit_bytes=62 * 2**20),
         name=name,
     )(*[ins[n][0] for n in iname])
@@ -1056,6 +1094,7 @@
 
 VM = pltpu.VMEM
 ANY = pl.ANY
+LD, ST = "LD", "ST"
 
 
 def gather_first(srcs, gset, cid):
@@ -1078,8 +1117,9 @@
 
 def attend_body(b, w, R, core, side):
     hp = b.h.shape[1]
+    b.need("h", "vn")
     rows16(R, lambda s: norm_store(b.n, s, b.h[s], b.vn[0:1, :], b.vn[1:2, :]))
-    yield
+    b.need("w_in", "cos", "sin", "keep", "vh")
     D = 512
     for j in range(2):
         kt = dot_nn(b.n[...], b.w_in[:, D + 256 * j : D + 256 * j + 256])
@@ -1097,6 +1137,8 @@
         for hf in range(2):
             l = slice(256 * j + 128 * hf, 256 * j + 128 * hf + 128)
             b.q[:, l] = (turn(qt[:, 128 * hf : 128 * hf + 128], b.cos[...], b.sin[...]) * 0.125).astype(BF)
+    b.put("q")
+    b.need("fill")
     yield
     S = 176
     for p in range(4):
@@ -1132,6 +1174,9 @@
             b.lse[2 * p + t : 2 * p + t + 1, :] = m + jnp.log(tot)
             yield
         b.o[:, l] = jnp.concatenate(halves, axis=0).T
+    for n in ("k", "v", "lse", "o"):
+        b.put(n)
+    b.need("w_out")
 
     def stats(s):
         x = b.o[s]
@@ -1149,6 +1194,7 @@
         b.u[s] = ((b.o[s] - mean) * inv * b.vh[0:1, :] + b.vh[3:4, :]).astype(BF)
 
     rows16(R, unit)
+    b.put("st")
     yield
     for d in range(4):
         l = slice(256 * d, 256 * d + 256)
@@ -1165,6 +1211,7 @@
         b.hm[s] = b.h[s] + wide(b.keep[s], x.shape[1]) * x
 
     rows16(R, close)
+    b.put("hm")
     yield
 
 
@@ -1182,17 +1229,19 @@
         comm = gset.start(w, {n: getattr(b, "s_" + n) for n in names}, {n: getattr(b, "g_" + n) for n in names}, b.extra)
         core = Peer((w.dp, w.x, 1 - w.c), b.cs, b.cr)
         side = Peer(w.nx(), b.xs, b.xr)
-        next(comm)
-        drive(attend_body(b, w, R, core, side), comm, 2)
+        for _ in gset.live:
+            next(comm)
+        n = len(gset.live)
+        drive(attend_body(b, w, R, core, side), comm, [0, 0, n, n, n], 3)
         gset.finish()
         core.finish()
         side.finish()
 
-    ins = {"h": (h, VM), "keep": (tabs["keep"], VM), "fill": (tabs["fill"], VM), "cos": (tabs["cos"], VM),
-           "sin": (tabs["sin"], VM), "w_in": (wts["in"], VM), "w_out": (wts["out"], VM), "vn": (vn, VM), "vh": (vh, VM)}
+    ins = {"h": (h, LD), "keep": (tabs["keep"], LD), "fill": (tabs["fill"], LD), "cos": (tabs["cos"], LD),
+           "sin": (tabs["sin"], LD), "w_in": (wts["in"], LD), "w_out": (wts["out"], LD), "vn": (vn, LD), "vh": (vh, LD)}
     ins.update({"s_" + n: (srcs[n], ANY) for n in gset.names})
-    outs = {"hm": ((R, D), F32, VM), "q": ((R, 512), BF, VM), "k": ((2 * R, 512), BF, VM), "v": ((2 * R, 512), BF, VM),
-            "lse": ((8, R), F32, VM), "o": ((R, 512), F32, VM), "st": ((R, 128), F32, VM)}
+    outs = {"hm": ((R, D), F32, ST), "q": ((R, 512), BF, ST), "k": ((2 * R, 512), BF, ST), "v": ((2 * R, 512), BF, ST),
+            "lse": ((8, R), F32, ST), "o": ((R, 512), F32, ST), "st": ((R, 128), F32, ST)}
     outs.update({"g_" + n: ((16 * RB, srcs[n].shape[1]), BF, ANY) for n in gset.names})
     scratch = {"n": pltpu.VMEM((R, D), BF), "s": pltpu.VMEM((2 * R, R), F32), "p": pltpu.VMEM((2 * R, R), BF),
                "u": pltpu.VMEM((R, 512), BF), "part": pltpu.VMEM((R, D), BF), "rpart": pltpu.VMEM((R, D), BF),
@@ -1202,7 +1251,9 @@
 
 
 def hidden_body(b, w, R, core):
+    b.need("hm", "vn")
     rows16(R, lambda s: norm_store(b.n, s, b.hm[s], b.vn[2:3, :], b.vn[3:4, :]))
+    b.need("w_gu", "vf")
     yield
     for i, (a, n) in enumerate(tiles(HP)):
         b.gate[:, a : a + n] = dot_nn(b.n[...], b.w_gu[:, a : a + n]) + b.vf[1:2, a : a + n]
@@ -1210,6 +1261,9 @@
         if i % 2 == 1:
             yield
 
+    b.put("gate")
+    b.put("up")
+
     def stats(s):
         g = b.gate[s]
         z = g * jax.nn.sigmoid(g) * b.up[s]
@@ -1229,6 +1283,8 @@
         b.zn[s] = ((b.z[s] - mean) * inv * b.vf[0:1, :] + b.vf[3:4, :]).astype(BF)
 
     rows16(R, unit)
+    b.put("st")
+    b.need("w_dn", "keep")
     yield
     for d in range(4):
         l = slice(256 * d, 256 * d + 256)
@@ -1245,6 +1301,7 @@
         b.ho[s] = b.hm[s] + wide(b.keep[s], x.shape[1]) * x
 
     rows16(R, close)
+    b.put("ho")
     yield
 
 
@@ -1259,16 +1316,17 @@
         if gset:
             names = gset.names
             comm = gset.start(w, {n: getattr(b, "s_" + n) for n in names}, {n: getattr(b, "g_" + n) for n in names}, b.extra)
-            next(comm)
-            drive(comp, comm, 2)
+            for _ in gset.live:
+                next(comm)
+            drive(comp, comm, [], 3)
             gset.finish()
         else:
             for _ in comp:
                 pass
         core.finish()
 
-    ins = {"hm": (hm, VM), "keep": (tabs["keep"], VM), "w_gu": (wts["gu"], VM), "w_dn": (wts["dn"], VM), "vn": (vn, VM), "vf": (vf, VM)}
-    outs = {"ho": ((R, D), F32, VM), "gate": ((R, HP), F32, VM), "up": ((R, HP), F32, VM), "st": ((R, 128), F32, VM)}
+    ins = {"hm": (hm, LD), "keep": (tabs["keep"], LD), "w_gu": (wts["gu"], LD), "w_dn": (wts["dn"], LD), "vn": (vn, LD), "vf": (vf, LD)}
+    outs = {"ho": ((R, D), F32, ST), "gate": ((R, HP), F32, ST), "up": ((R, HP), F32, ST), "st": ((R, 128), F32, ST)}
     if gset:
         ins.update({"s_" + n: (srcs[n], ANY) for n in gset.names})
         outs.update({"g_" + n: ((16 * RB, srcs[n].shape[1]), BF, ANY) for n in gset.names})
@@ -1302,6 +1360,7 @@
     D = b.g.shape[1]
     for a in (b.a0, b.a1, b.a2, b.a3, b.a4, b.a5, b.a6, b.vec):
         a[...] = jnp.zeros_like(a)
+    b.need("g", "keep", "gate", "up", "st", "vn", "vf")
 
     def unit4(s):
         g = b.gate[s]
@@ -1316,6 +1375,7 @@
         b.zn[s] = (unit4(s)[0] * b.vf[0:1, :] + b.vf[3:4, :]).astype(BF)
 
     rows16(R, first)
+    b.need("w_dn")
     yield
     for i, (a, n) in enumerate(tiles(HP)):
         b.ez[:, a : a + n] = dot_nn(b.el[...], b.w_dn[:, a : a + n])
@@ -1352,6 +1412,7 @@
         b.egu[s, HP : 2 * HP] = eu.astype(BF)
 
     rows16(R, third, 48)
+    b.need("w_gu")
     yield
     for d in range(4):
         l = slice(256 * d, 256 * d + 256)
@@ -1361,12 +1422,14 @@
     b.xT[...] = b.n[...].T
     for i, (a, n) in enumerate(tiles(2 * HP)):
         b.d_gu[:, a : a + n] = dot_nn(b.xT[...], b.egu[:, a : a + n]).astype(BF)
-        if i % 3 == 2:
+        if i % 3 == 2 or i == len(tiles(2 * HP)) - 1:
+            b.put("d_gu", (a - a % 768, a + n))
             yield
     for d in range(4):
         l = slice(256 * d, 256 * d + 256)
         core.recv(b.rpart.at[:, l], 1 + d)
     rows16(R, lambda s: close_back(b, s, b.go[s], b.vn[2:3, :], b.a0, b.a1))
+    b.put("go")
     for row, acc, n in ((0, b.a0, D), (1, b.a1, D), (2, b.a2, D), (3, b.a3, HP), (4, b.a4, HP), (5, b.a5, HP), (6, b.a6, HP)):
         put_vec(b, row, acc, n)
     yield
@@ -1377,6 +1440,7 @@
     hp = D
     for a in (b.a0, b.a1, b.a2, b.a3, b.a4, b.a5, b.a6, b.vec):
         a[...] = jnp.zeros_like(a)
+    b.need("g", "keep", "o", "st", "vn", "vh")
 
     def first(s):
         e = wide(b.keep[s], D) * b.g[s]
@@ -1387,6 +1451,7 @@
         b.u[s] = (u * b.vh[0:1, :] + b.vh[3:4, :]).astype(BF)
 
     rows16(R, first)
+    b.need("w_out")
     yield
     for a, n in tiles(512):
         b.dq[:, a : a + n] = dot_nn(b.el[...], b.w_out[:, a : a + n])
@@ -1405,6 +1470,7 @@
     yield
     for a, n in tiles(512):
         b.d_out[:, a : a + n] = dot_nn(b.xT[...], b.u[:, a : a + n]).astype(BF)
+    b.put("d_out")
     yield
     core.recv(b.rstat, 0)
 
@@ -1414,6 +1480,7 @@
         b.eo[s] = (b.st[s, 1:2] * (b.dq[s] * b.vh[0:1, :] - t[:, 0:1] - u * t[:, 1:2])).astype(BF)
 
     rows16(R, third, 48)
+    b.need("q", "k", "v", "lse", "fill")
     yield
     S = 176
     for p in range(4):
@@ -1461,6 +1528,7 @@
         b.ep[:, l2] = dv[R:].astype(BF)
         side.send(b.ep.at[:, l], b.rk.at[:, l], 2 * p)
         side.send(b.ep.at[:, l2], b.rv.at[:, l], 2 * p + 1)
+    b.need("cos", "sin", "w_in")
     yield
     side.finish()
     for p in range(4):
@@ -1491,11 +1559,13 @@
     for i, (a, n) in enumerate(tiles(1536)):
         b.d_in[:, a : a + n] = dot_nn(b.xT[...], b.ep[:, a : a + n]).astype(BF)
         if i % 3 == 2:
+            b.put("d_in", (a - a % 768, a + n))
             yield
     for d in range(4):
         l = slice(256 * d, 256 * d + 256)
         core.recv(b.rpart.at[:, l], 1 + d)
     rows16(R, lambda s: close_back(b, s, b.go[s], b.vn[0:1, :], b.a0, b.a1))
+    b.put("go")
     for row, acc, n in ((0, b.a0, D), (1, b.a1, D), (2, b.a2, D), (3, b.a3, 512), (4, b.a4, 512), (5, b.a5, 512), (6, b.a6, 512)):
         put_vec(b, row, acc, n)
     yield
@@ -1509,9 +1579,12 @@
     return ins, outs
 
 
-def scatter_start(sset, w, b):
+def scatter_start(sset, w, b, sc=None):
     n = sset.names
-    return sset.start(w, {i: getattr(b, "s_" + i) for i in n}, {i: getattr(b, "r_" + i) for i in n}, b.s_vec, b.r_vec, b.extra)
+    return sset.start(w, {i: getattr(b, "s_" + i) for i in n}, {i: getattr(b, "r_" + i) for i in n}, b.s_vec, b.r_vec, b.extra if sc is None else sc)
+
+
+HB_RATE = 2
 
 
 def backward_hidden(g, fw, hm, tabs, wts, vn, vf, sset, grads, vec, cid):
@@ -1519,35 +1592,49 @@
 
     def body(b):
         w = Where()
-        greet_all(w, "all" if sset else "core")
+        greet_all(w, "all")
         core = Peer((w.dp, w.x, 1 - w.c), b.cs, b.cr)
         load = pltpu.make_async_copy(b.hm, b.go, b.ls.at[0])
         load.start()
         comp = hidden_back_body(b, w, R, core)
         if sset:
-            comm = scatter_start(sset, w, b)
+            comm = scatter_start(sset, w, b, b.extra[:split])
             for _ in sset.live:
                 next(comm)
-            load.wait()
-            drive(comp, comm, 2)
+        load.wait()
+
+        def both():
+            for _ in range(5):
+                if sset:
+                    for _ in range(3):
+                        next(comm, None)
+                yield
+            mine = dset.start(w, {"dn": b.d_dn}, {"dn": b.r_dn}, None, None, b.extra[split:])
+            for _ in dset.live:
+                next(mine)
+            yield
+            yield from step_all([mine, comm] if sset else [mine])
+
+        drive(comp, both(), [1] * 6, HB_RATE * (2 if sset else 1))
+        if sset:
             sset.finish()
-        else:
-            load.wait()
-            for _ in comp:
-                pass
+        dset.finish()
         core.finish()
 
-    ins = {"g": (g, VM), "keep": (tabs["keep"], VM), "hm": (hm, ANY), "gate": (fw["gate"], VM), "up": (fw["up"], VM), "st": (fw["st"], VM),
-           "w_gu": (wts["gu"], VM), "w_dn": (wts["dn"], VM), "vn": (vn, VM), "vf": (vf, VM)}
-    outs = {"go": ((R, D), F32, VM), "d_gu": ((D, 2 * HP), BF, VM), "d_dn": ((D, HP), BF, VM), "vec": ((8, HP), F32, VM)}
+    ins = {"g": (g, LD), "keep": (tabs["keep"], LD), "hm": (hm, ANY), "gate": (fw["gate"], LD), "up": (fw["up"], LD), "st": (fw["st"], LD),
+           "w_gu": (wts["gu"], LD), "w_dn": (wts["dn"], LD), "vn": (vn, LD), "vf": (vf, LD)}
+    outs = {"go": ((R, D), F32, ST), "d_gu": ((D, 2 * HP), BF, ST), "r_dn": ((RB, HP), F32, VM), "vec": ((8, HP), F32, VM)}
     extra = ()
+    dset = dn_scatter()
     if sset:
         i2, o2 = scatter_args(sset, grads, vec)
         ins.update(i2)
         outs.update(o2)
         extra = sset.scratch()
+    split = len(extra)
+    extra = list(extra) + dset.scratch()
     acc = lambda n: pltpu.VMEM((8, n), F32)
-    scratch = {"el": pltpu.VMEM((R, D), BF), "xT": pltpu.VMEM((D, R), BF), "n": pltpu.VMEM((R, D), BF), "ez": pltpu.VMEM((R, HP), F32),
+    scratch = {"d_dn": pltpu.VMEM((D, HP), BF), "el": pltpu.VMEM((R, D), BF), "xT": pltpu.VMEM((D, R), BF), "n": pltpu.VMEM((R, D), BF), "ez": pltpu.VMEM((R, HP), F32),
                "zn": pltpu.VMEM((R, HP), BF), "egu": pltpu.VMEM((R, 2 * HP), BF), "part": pltpu.VMEM((R, D), BF), "rpart": pltpu.VMEM((R, D), BF),
                "stat": pltpu.VMEM((R, 128), F32), "rstat": pltpu.VMEM((R, 128), F32), "cs": DMA((5,)), "cr": DMA((5,)), "ls": DMA((1,)),
                "a0": acc(D), "a1": acc(D), "a2": acc(D), "a3": acc(HP), "a4": acc(HP), "a5": acc(HP), "a6": acc(HP)}
@@ -1568,14 +1655,14 @@
         for _ in sset.live:
             next(comm)
         load.wait()
-        drive(attend_back_body(b, w, R, core, side), comm, 2)
+        drive(attend_back_body(b, w, R, core, side), comm, [], 2)
         sset.finish()
         core.finish()
 
-    ins = {"g": (g, VM), "keep": (tabs["keep"], VM), "h": (h, ANY), "fill": (tabs["fill"], VM), "cos": (tabs["cos"], VM), "sin": (tabs["sin"], VM),
-           "o": (fw["o"], VM), "st": (fw["st"], VM), "q": (fw["q"], VM), "k": (fw["k"], VM), "v": (fw["v"], VM), "lse": (fw["lse"], VM),
-           "w_in": (wts["in"], VM), "w_out": (wts["out"], VM), "vn": (vn, VM), "vh": (vh, VM)}
-    outs = {"go": ((R, D), F32, VM), "d_in": ((D, 1536), BF, VM), "d_out": ((D, 512), BF, VM), "vec": ((8, HP), F32, VM)}
+    ins = {"g": (g, LD), "keep": (tabs["keep"], LD), "h": (h, ANY), "fill": (tabs["fill"], LD), "cos": (tabs["cos"], LD), "sin": (tabs["sin"], LD),
+           "o": (fw["o"], LD), "st": (fw["st"], LD), "q": (fw["q"], LD), "k": (fw["k"], LD), "v": (fw["v"], LD), "lse": (fw["lse"], LD),
+           "w_in": (wts["in"], LD), "w_out": (wts["out"], LD), "vn": (vn, LD), "vh": (vh, LD)}
+    outs = {"go": ((R, D), F32, ST), "d_in": ((D, 1536), BF, ST), "d_out": ((D, 512), BF, ST), "vec": ((8, HP), F32, VM)}
     i2, o2 = scatter_args(sset, grads, vec)
     ins.update(i2)
     outs.update(o2)
@@ -1680,8 +1767,8 @@
         r = backward_hidden(g, ff_f[l], hms[l], tabs, ff_w[l], vn[l], vf[l], sset, grads, vec, cid)
         if grads:
             got["at", l + 1] = r
-        g, vec, grads = r["go"], r["vec"], {"gu": r["d_gu"], "dn": r["d_dn"]}
-        r = backward_attend(g, at_f[l], hs[l], tabs, at_w[l], vn[l], vh[l], ff_scatter(), grads, vec, cid + 1)
+        g, vec, grads, got["dn", l] = r["go"], r["vec"], {"gu": r["d_gu"]}, r["r_dn"]
+        r = backward_attend(g, at_f[l], hs[l], tabs, at_w[l], vn[l], vh[l], gu_scatter(), grads, vec, cid + 1)
         got["ff", l] = r
         g, vec, grads = r["go"], r["vec"], {"in": r["d_in"], "out": r["d_out"]}
         cid += 2
@@ -1696,7 +1783,7 @@
         jnp.stack([got["at", l]["r_in"].reshape(RB, 3, dim) for l in L]),
         jnp.stack([got["at", l]["r_out"] for l in L]),
         jnp.stack([got["ff", l]["r_gu"].reshape(RB, 2, HP)[:, :, :hidden] for l in L]),
-        jnp.stack([got["ff", l]["r_dn"][:, :hidden] for l in L]),
+        jnp.stack([got["dn", l][:, :hidden] for l in L]),
         jnp.stack([va[:, 0, :width], vff[:, 0, :width]], axis=1),
         jnp.stack([va[:, 1, :width], vff[:, 1, :width], va[:, 2, :width], vff[:, 2, :width]], axis=1),
         va[:, 3, :dim],

time: 871 us -> 659 us (0.76)
  Pallas kernels: 814 us -> 604 us
    pallas_call x10, Pallas kernels: 814 us -> 604 us  [run_kernel(): pl.pallas_call(kernel, out_shape=[jax.ShapeDtypeStruct(outs[n][0], outs[n...]
  transfers between devices with their start and end apart: 1 -> 1, of which waited for: 0 -> 0; matrix products, arithmetic and copies ran while one was open for 2% -> 3% of each run, Pallas kernels for 5% -> 6%
where the time goes in v3:
time: 659 us; the launch traced here: 654 us
  Pallas kernels  604 us (92%)
  local copies, waits for them, and re-layouts  29.9 us (5%)
  other arithmetic  15 us (2%)
    pallas_call x10, Pallas kernels, run_kernel(): pl.pallas_call(kernel, out_shape=[jax.ShapeDtypeStruct(outs[n][0], outs[n...  604 us
  transfers between devices with their start and end apart: 1, of which 0 were waited for; matrix products, arithmetic and copies ran while one was open for 3% of the time, Pallas kernels for 6%

profile of v3, /device:TPU:0, one launch (start us, length us, event | category | flops | bytes accessed | tf_op | source)
XLA Modules:
  0.0 653.6 jit_solution(1917764931164195388)
XLA Ops:
  1.4 3.0 collective-permute-start
  7.3 1.9 fusion.2
  14.3 1.6 convert_multiply_fusion.refs_0_.refs_2_
  15.9 1.6 pad_convert_fusion.refs_0_
  17.5 2.5 concatenate.18
  20.7 2.5 concatenate.19
  27.4 38.2 %gather.1 = (bf16[1024,1536]{1,0:T(8,128)(2,1)}, bf16[1024,512]{1,0:T(8,128)(2,1)}) custom-call(bf16[64,1536]{1,0:T(8,128)(2,1)} %bitcast.90, bf16[64,512]{1,0:T(8,128)(2,1)} %get-tuple-element.163.refs_1_), custom_call_target="tpu_custom_call" | custom-call | tf_op jit(solution)/shard_map/gather/pallas_call | solution.py:1083
  66.5 1.0 broadcast_in_dim.35.refs_2_.refs_3_
  67.5 88.3 %attend.2 = (f32[528,1024]{1,0:T(8,128)}, bf16[528,512]{1,0:T(8,128)(2,1)}, bf16[1056,512]{1,0:T(8,128)(2,1)}, bf16[1056,512]{1,0:T(8,128)(2,1)}, f32[8,528]{1,0...) custom-call(f32[528,1024]{1,0:T(8,128)} %convert_multiply_fusion.ref, ...), custom_call_target="tpu_custom_call" | custom-call | tf_op jit(solution)/shard_map/attend/pallas_call | solution.py:1083
  155.8 38.6 %hidden.2 = (f32[528,1024]{1,0:T(8,128)}, f32[528,1408]{1,0:T(8,128)}, f32[528,1408]{1,0:T(8,128)}, f32[528,128]{1,0:T(8,128)}, bf16[1024,1536]{1,0:T(8,128)(2,1)}, /*index=5*/bf16[1024,512]{1,0:T(8,128)(2,1)}) custom-call(f32[528,1024]{1,0:T(8,128)} %get-tuple-element.70.refs_0_.refs_2_, f32[528,128]{1,0:T(8,128)} %broadcast_in_dim.31.refs_1_, ...), custom_call_target="tpu_custom_call" | custom-call | tf_op jit(solution)/shard_map/hidden/pallas_call | solution.py:1083
  194.4 89.4 %attend.3 = (f32[528,1024]{1,0:T(8,128)}, bf16[528,512]{1,0:T(8,128)(2,1)}, bf16[1056,512]{1,0:T(8,128)(2,1)}, bf16[1056,512]{1,0:T(8,128)(2,1)}, f32[8,528]{1,0...) custom-call(f32[528,1024]{1,0:T(8,128)} %get-tuple-element.73.refs_0, ...), custom_call_target="tpu_custom_call" | custom-call | tf_op jit(solution)/shard_map/attend/pallas_call | solution.py:1083
  283.8 19.0 %hidden.3 = (f32[528,1024]{1,0:T(8,128)}, f32[528,1408]{1,0:T(8,128)}, f32[528,1408]{1,0:T(8,128)}, f32[528,128]{1,0:T(8,128)}) custom-call(f32[528,1024]{1,0:T(8,128)} %get-tuple-element.76.refs_0_.refs_2_, f32[528,128]{1,0:T(8,128)} %broadcast_in_dim.31.refs_1_, bf16[1024,2816]{1,0:T(8,128)(2,1)} %get-tuple-element.77.refs_2_.refs_6_, ...), custom_call_target="tpu_custom_call" | custom-call | tf_op jit(solution)/shard_map/hidden/pallas_call | solution.py:1083
  302.8 45.2 %hidden_back.2 = (f32[528,1024]{1,0:T(8,128)}, bf16[1024,2816]{1,0:T(8,128)(2,1)}, f32[64,1408]{1,0:T(8,128)}, f32[8,1408]{1,0:T(8,128)}) custom-call(f32[528,1024]{1,0:T(8,128)} %pad_convert_fusion.refs_0_, f32[528,128]{1,0:T(8,128)} %broadcast_in_dim.31.refs_1_, f32[528,1024]{1,0:T(8,128)} %get-tuple-element.76.refs_0_.refs_2_, ...), custom_call_target="tpu_custom_call" | custom-call | tf_op jit(solution)/shard_map/hidden_back/pallas_call | solution.py:1083
  348.0 88.4 %attend_back.2 = (f32[528,1024]{1,0:T(8,128)}, bf16[1024,1536]{1,0:T(8,128)(2,1)}, bf16[1024,512]{1,0:T(8,128)(2,1)}, f32[8,1408]{1,0:T(8,128)}, f32[64,2816]{1,0:T(8,128)}, /*index=5*/f32[8,1408]{1,0:T(8,128)}) custom-call(f32[528,1024]{1,0:T(8,128)} %get-tuple-element.83.refs_0_, f32[528,128]{1,0:T(8,128)} %broadcast_in_dim.31.refs_1_, ...), custom_call_target="tpu_custom_call" | custom-call | tf_op jit(solution)/shard_map/attend_back/pallas_call | solution.py:1083
  436.4 65.2 %hidden_back.3 = (f32[528,1024]{1,0:T(8,128)}, bf16[1024,2816]{1,0:T(8,128)(2,1)}, f32[64,1408]{1,0:T(8,128)}, f32[8,1408]{1,0:T(8,128)}, f32[64,1536]{1,0:T(8,1...) custom-call(f32[528,1024]{1,0:T(8,128)} %get-tuple-element.92.refs_0_, f32[528,128]{1,0:T(8,128)} %broadcast_in_dim.31.refs_1_, ...), custom_call_target="tpu_custom_call" | custom-call | tf_op jit(solution)/shard_map/hidden_back/pallas_call | solution.py:1083
  501.6 88.3 %attend_back.3 = (f32[528,1024]{1,0:T(8,128)}, bf16[1024,1536]{1,0:T(8,128)(2,1)}, bf16[1024,512]{1,0:T(8,128)(2,1)}, f32[8,1408]{1,0:T(8,128)}, f32[64,2816]{1,0:T(8,128)}, /*index=5*/f32[8,1408]{1,0:T(8,128)}) custom-call(f32[528,1024]{1,0:T(8,128)} %get-tuple-element.99.refs_0_, f32[528,128]{1,0:T(8,128)} %broadcast_in_dim.31.refs_1_, ...), custom_call_target="tpu_custom_call" | custom-call | tf_op jit(solution)/shard_map/attend_back/pallas_call | solution.py:1083
  590.0 43.1 %scatter.1 = (f32[64,1536]{1,0:T(8,128)}, f32[64,512]{1,0:T(8,128)}, f32[8,1408]{1,0:T(8,128)}) custom-call(bf16[1024,1536]{1,0:T(8,128)(2,1)} %get-tuple-element.109.refs_0_, bf16[1024,512]{1,0:T(8,128)(2,1)} %get-tuple-element.110.refs_1_, f32[8,1408]{1,0:T(8,128)} %get-tuple-element.111.refs_2_), custom_call_target="tpu_custom_call" | custom-call | tf_op jit(solution)/shard_map/scatter/pallas_call | solution.py:1083
  633.1 1.5 fusion.22
  634.6 1.5 fusion.13
  637.6 2.7 fusion.1
  640.5 3.5 copy.42
  644.9 1.1 copy.43
  650.7 1.8 pad_maximum_fusion
  652.5 0.9 pad_maximum_fusion.2
  (102 shorter events, 20.8 us)
Async XLA Ops:
  1.4 64.2 %collective-permute-start = (f32[528]{0:T(1024)S(1)}, f32[528]{0:T(1024)S(1)}, u32[]{:S(2)}, u32[]{:S(2)}) collective-permute-start(f32[528]{0:T(1024)S(1)} %get-tuple-element.148), channel_id=1, source_target_pairs={{0,2},{2,0},{1,3},{3,1},{4,6},{6,4},{5,7},{7,5},{8,10},{10,8},{9,1... | collective-permute-start | bytes 6344 | tf_op jit(solution)/shard_map/ppermute | solution.py:1726
  5.1 4.3 copy-start.11
  9.2 0.9 copy-start.15
  9.2 1.6 copy-start.18
  9.2 2.2 copy-start.20
  9.2 2.2 copy-start.22
  9.3 2.9 copy-start.3
  9.3 3.5 copy-start.12
  9.4 4.1 copy-start.19
  9.4 4.1 copy-start.21
  9.5 4.9 copy-start.1
  12.8 3.1 copy-start.2
  589.9 43.1 %copy-start.6 = (f32[8,1408]{1,0:T(8,128)S(1)}, f32[8,1408]{1,0:T(8,128)}, u32[]{:S(2)}) copy-start(f32[8,1408]{1,0:T(8,128)} %get-tuple-element.123) | copy-start | bytes 135172
  590.0 43.1 %copy-start.7 = (f32[8,1408]{1,0:T(8,128)S(1)}, f32[8,1408]{1,0:T(8,128)}, u32[]{:S(2)}) copy-start(f32[8,1408]{1,0:T(8,128)} %get-tuple-element.121) | copy-start | bytes 135172
  590.0 43.1 %copy-start.8 = (f32[8,1408]{1,0:T(8,128)S(1)}, f32[8,1408]{1,0:T(8,128)}, u32[]{:S(2)}) copy-start(f32[8,1408]{1,0:T(8,128)} %get-tuple-element.122) | copy-start | bytes 135172
  633.0 7.3 %copy-start = (f32[528,1024]{1,0:T(8,128)S(1)}, f32[528,1024]{1,0:T(8,128)}, u32[]{:S(2)}) copy-start(f32[528,1024]{1,0:T(8,128)} %get-tuple-element.108) | copy-start | bytes 6488068
  640.5 3.5 copy-start.9
  640.5 3.8 copy-start.10
  644.6 1.4 copy-start.4
  644.9 1.7 copy-start.5
  646.4 1.0 copy-start.13
  646.5 1.0 copy-start.14
  646.5 3.5 copy-start.16
  646.5 3.5 copy-start.17

commit v4 on v3

--- a/solution.py
+++ b/solution.py
@@ -538,11 +538,10 @@
                 else: pl.when(cond)(go)
                 self.send(cond,*b,self.qdev(),25+kk,8+zz*2+1)
             yield
-    def finish(self):
+    def arrive(self):
         for zz in range(4):
             for pself in (True,False):
                 self.arrived(*self.qcoord(zz,pself),8+zz*2+(0 if pself else 1))
-        self.finish_sends()
     NS,NR=32,16
 
 class GatherX(Gather):
@@ -580,8 +579,8 @@
                     def _(zz=zz,j=j): self.arrived(*self.blk(zz,j),3+zz*4+j)
                     if k<3: self.vert(cond,zz,j,kk)
                 if j%2==1: yield
-    def finish(self):
-        self.finish_sends()
+    def arrive(self):
+        pass
 
 
 ZORD=(3,0,2,1)
@@ -798,11 +797,19 @@
                 self.live.append(GatherX(w, "xyz", s, o, 0, 64, sems.pop(0), sems.pop(0), None))
         return step_all([p.rounds() for p in self.live])
 
-    def finish(self):
+    def arrive(self):
         for p in self.live:
-            p.finish()
+            p.arrive()
         for c in self.locs:
             c.wait()
+
+    def finish_sends(self):
+        for p in self.live:
+            p.finish_sends()
+
+    def finish(self):
+        self.arrive()
+        self.finish_sends()
 
 
 class VecSum:
@@ -1009,6 +1016,7 @@
     def finish(self):
         for c in self.open:
             c.wait_send()
+        self.open = []
 
 
 def greet_all(w, links):
@@ -1033,9 +1041,14 @@
 class Bag:
     def launch(self):
         self.coming = {n: pltpu.make_async_copy(h, getattr(self, n), self.ld.at[i]) for i, (n, h) in enumerate(self.loads)}
-        for c in self.coming.values():
-            c.start()
+        for n, c in self.coming.items():
+            if n not in self.late:
+                c.start()
         self.going = []
+
+    def begin(self, *names):
+        for n in names:
+            self.coming[n].start()
 
     def need(self, *names):
         for n in names:
@@ -1058,7 +1071,7 @@
 
 def run_kernel(body, name, cid, ins, outs, scratch, extra=()):
     iname, oname, sname = list(ins), list(outs), list(scratch)
-    ld = [n for n in iname if ins[n][1] == "LD"]
+    ld = [n for n in iname if ins[n][1] in (LD, LATE)]
     so = [n for n in oname if outs[n][2] == "ST"]
     moved = [pltpu.VMEM(ins[n][0].shape, ins[n][0].dtype) for n in ld] + [pltpu.VMEM(outs[n][0], outs[n][1]) for n in so]
     moved += [DMA((max(len(ld), 1),)), DMA((16,))]
@@ -1070,6 +1083,7 @@
             setattr(b, n, r)
         mv = refs[ni + no + ns : ni + no + ns + nm]
         b.loads = [(n, getattr(b, n)) for n in ld]
+        b.late = [n for n in ld if ins[n][1] == LATE]
         b.stores = {n: getattr(b, n) for n in so}
         for n, r in zip(ld + so, mv):
             setattr(b, n, r)
@@ -1079,7 +1093,7 @@
         body(b)
         b.flush()
 
-    place = lambda s: pl.BlockSpec(memory_space=pl.ANY if s in ("LD", "ST") else s)
+    place = lambda s: pl.BlockSpec(memory_space=pl.ANY if s in (LD, ST, LATE) else s)
     res = pl.pallas_call(
         kernel,
         out_shape=[jax.ShapeDtypeStruct(outs[n][0], outs[n][1]) for n in oname],
@@ -1094,25 +1108,34 @@
 
 VM = pltpu.VMEM
 ANY = pl.ANY
-LD, ST = "LD", "ST"
-
-
-def gather_first(srcs, gset, cid):
+LD, ST, LATE = "LD", "ST", "LATE"
+
+
+def gather_first(srcs, gset, fill, cid):
     names = gset.names
+    R = fill.shape[1]
 
     def body(b):
         w = Where()
         greet(w)
+        side = Peer(w.nx(), b.xs, b.xr)
+        b.need("fill")
+        side.send(b.fill, b.other, 0)
         g = gset.start(w, {n: getattr(b, "s_" + n) for n in names}, {n: getattr(b, "w_" + n) for n in names}, b.extra)
         for _ in g:
             pass
+        side.recv(b.other, 0)
+        b.both[0:R, :] = jnp.broadcast_to(b.fill[...].T[:, 0:1], (R, 128))
+        b.both[R : 2 * R, :] = jnp.broadcast_to(b.other[...].T[:, 0:1], (R, 128))
+        b.put("both")
         gset.finish()
-
-    return run_kernel(
-        body, "gather", cid,
-        {"s_" + n: (srcs[n], ANY) for n in names},
-        {"w_" + n: ((16 * RB, srcs[n].shape[1]), BF, ANY) for n in names},
-        {}, gset.scratch())
+        side.finish()
+
+    ins = {"s_" + n: (srcs[n], ANY) for n in names}
+    ins["fill"] = (fill, LD)
+    outs = {"w_" + n: ((16 * RB, srcs[n].shape[1]), BF, ANY) for n in names}
+    outs["both"] = ((2 * R, 128), F32, ST)
+    return run_kernel(body, "gather", cid, ins, outs, dict(other=VM((8, R), F32), xs=DMA((1,)), xr=DMA((1,))), gset.scratch())
 
 
 def attend_body(b, w, R, core, side):
@@ -1219,41 +1242,11 @@
     dst[s] = (unit_of(x, x.shape[1])[0] * gain + bias).astype(BF)
 
 
-def forward_attend(h, tabs, wts, vn, vh, srcs, gset, cid):
-    R, D = h.shape
-
-    def body(b):
-        w = Where()
-        greet_all(w, "all")
-        names = gset.names
-        comm = gset.start(w, {n: getattr(b, "s_" + n) for n in names}, {n: getattr(b, "g_" + n) for n in names}, b.extra)
-        core = Peer((w.dp, w.x, 1 - w.c), b.cs, b.cr)
-        side = Peer(w.nx(), b.xs, b.xr)
-        for _ in gset.live:
-            next(comm)
-        n = len(gset.live)
-        drive(attend_body(b, w, R, core, side), comm, [0, 0, n, n, n], 3)
-        gset.finish()
-        core.finish()
-        side.finish()
-
-    ins = {"h": (h, LD), "keep": (tabs["keep"], LD), "fill": (tabs["fill"], LD), "cos": (tabs["cos"], LD),
-           "sin": (tabs["sin"], LD), "w_in": (wts["in"], LD), "w_out": (wts["out"], LD), "vn": (vn, LD), "vh": (vh, LD)}
-    ins.update({"s_" + n: (srcs[n], ANY) for n in gset.names})
-    outs = {"hm": ((R, D), F32, ST), "q": ((R, 512), BF, ST), "k": ((2 * R, 512), BF, ST), "v": ((2 * R, 512), BF, ST),
-            "lse": ((8, R), F32, ST), "o": ((R, 512), F32, ST), "st": ((R, 128), F32, ST)}
-    outs.update({"g_" + n: ((16 * RB, srcs[n].shape[1]), BF, ANY) for n in gset.names})
-    scratch = {"n": pltpu.VMEM((R, D), BF), "s": pltpu.VMEM((2 * R, R), F32), "p": pltpu.VMEM((2 * R, R), BF),
-               "u": pltpu.VMEM((R, 512), BF), "part": pltpu.VMEM((R, D), BF), "rpart": pltpu.VMEM((R, D), BF),
-               "stat": pltpu.VMEM((R, 128), F32), "rstat": pltpu.VMEM((R, 128), F32),
-               "cs": DMA((5,)), "cr": DMA((5,)), "xs": DMA((4,)), "xr": DMA((4,))}
-    return run_kernel(body, "attend", cid, ins, outs, scratch, gset.scratch())
-
-
-def hidden_body(b, w, R, core):
-    b.need("hm", "vn")
+def hidden_body(b, w, R, core, fetch):
     rows16(R, lambda s: norm_store(b.n, s, b.hm[s], b.vn[2:3, :], b.vn[3:4, :]))
-    b.need("w_gu", "vf")
+    loads = fetch()
+    b.need("vf")
+    loads[0].wait()
     yield
     for i, (a, n) in enumerate(tiles(HP)):
         b.gate[:, a : a + n] = dot_nn(b.n[...], b.w_gu[:, a : a + n]) + b.vf[1:2, a : a + n]
@@ -1279,12 +1272,12 @@
         t = b.stat[s] + b.rstat[s]
         mean = t[:, 0:1] / FF
         inv = lax.rsqrt(t[:, 1:2] / FF - mean * mean + EPS)
-        b.st[s] = two_cols(mean, inv)
+        b.zst[s] = two_cols(mean, inv)
         b.zn[s] = ((b.z[s] - mean) * inv * b.vf[0:1, :] + b.vf[3:4, :]).astype(BF)
 
     rows16(R, unit)
-    b.put("st")
-    b.need("w_dn", "keep")
+    b.put("zst")
+    loads[1].wait()
     yield
     for d in range(4):
         l = slice(256 * d, 256 * d + 256)
@@ -1305,35 +1298,72 @@
     yield
 
 
-def forward_hidden(hm, tabs, wts, vn, vf, srcs, gset, cid):
-    R, D = hm.shape
+def forward_layer(h, tabs, wts, vn, vh, vf, srcs, nxt, cid):
+    R, D = h.shape
+    fset = FF_G
+    aset = AT_G if nxt else None
 
     def body(b):
         w = Where()
-        greet_all(w, "all" if gset else "core")
+        greet_all(w, "all")
+        ends = lambda g: ({n: getattr(b, "s_" + n) for n in g.names}, {n: getattr(b, "g_" + n) for n in g.names})
+        ffc = fset.start(w, *ends(fset), b.extra[:split])
         core = Peer((w.dp, w.x, 1 - w.c), b.cs, b.cr)
-        comp = hidden_body(b, w, R, core)
-        if gset:
-            names = gset.names
-            comm = gset.start(w, {n: getattr(b, "s_" + n) for n in names}, {n: getattr(b, "g_" + n) for n in names}, b.extra)
-            for _ in gset.live:
-                next(comm)
-            drive(comp, comm, [], 3)
-            gset.finish()
-        else:
-            for _ in comp:
+        side = Peer(w.nx(), b.xs, b.xr)
+        n = len(fset.live)
+        for _ in range(n):
+            next(ffc)
+
+        def comm_all():
+            yield from ffc
+            if aset:
+                yield from aset.start(w, *ends(aset), b.extra[split:])
+
+        comm = comm_all()
+
+        def fetch():
+            for _ in ffc:
                 pass
+            if aset:
+                for _ in range(3):
+                    next(comm)
+            fset.arrive()
+            loads = [pltpu.make_async_copy(b.g_gu, b.w_gu, b.ls.at[0]), pltpu.make_async_copy(b.g_dn, b.w_dn, b.ls.at[1])]
+            for c in loads:
+                c.start()
+            return loads
+
+        def comp():
+            yield from attend_body(b, w, R, core, side)
+            core.finish()
+            yield from hidden_body(b, w, R, core, fetch)
+
+        drive(comp(), comm, [0, 0, n, n, n], 3)
+        fset.finish_sends()
+        if aset:
+            aset.finish()
         core.finish()
-
-    ins = {"hm": (hm, LD), "keep": (tabs["keep"], LD), "w_gu": (wts["gu"], LD), "w_dn": (wts["dn"], LD), "vn": (vn, LD), "vf": (vf, LD)}
-    outs = {"ho": ((R, D), F32, ST), "gate": ((R, HP), F32, ST), "up": ((R, HP), F32, ST), "st": ((R, 128), F32, ST)}
-    if gset:
-        ins.update({"s_" + n: (srcs[n], ANY) for n in gset.names})
-        outs.update({"g_" + n: ((16 * RB, srcs[n].shape[1]), BF, ANY) for n in gset.names})
-    scratch = {"n": pltpu.VMEM((R, D), BF), "z": pltpu.VMEM((R, HP), F32), "zn": pltpu.VMEM((R, HP), BF),
-               "part": pltpu.VMEM((R, D), BF), "rpart": pltpu.VMEM((R, D), BF),
-               "stat": pltpu.VMEM((R, 128), F32), "rstat": pltpu.VMEM((R, 128), F32), "cs": DMA((5,)), "cr": DMA((5,))}
-    return run_kernel(body, "hidden", cid, ins, outs, scratch, gset.scratch() if gset else ())
+        side.finish()
+
+    ins = dict(h=(h, LD), keep=(tabs["keep"], LD), fill=(tabs["fill"], LD), cos=(tabs["cos"], LD), sin=(tabs["sin"], LD),
+        w_in=(wts["in"], LD), w_out=(wts["out"], LD), vn=(vn, LD), vh=(vh, LD), vf=(vf, LD))
+    outs = dict(hm=((R, D), F32, ST), q=((R, 512), BF, ST), k=((2 * R, 512), BF, ST), v=((2 * R, 512), BF, ST),
+        lse=((8, R), F32, ST), o=((R, 512), F32, ST), st=((R, 128), F32, ST), ho=((R, D), F32, ST),
+        gate=((R, HP), F32, ST), up=((R, HP), F32, ST), zst=((R, 128), F32, ST))
+    extra = fset.scratch()
+    split = len(extra)
+    for g, src in ((fset, srcs), (aset, nxt)):
+        if g:
+            ins.update({"s_" + n: (src[n], ANY) for n in g.names})
+            outs.update({"g_" + n: ((16 * RB, src[n].shape[1]), BF, ANY) for n in g.names})
+    if aset:
+        extra = extra + aset.scratch()
+    B = lambda *s: pltpu.VMEM(s, BF)
+    F = lambda *s: pltpu.VMEM(s, F32)
+    scratch = dict(n=B(R, D), s=F(2 * R, R), p=B(2 * R, R), u=B(R, 512), part=B(R, D), rpart=B(R, D), stat=F(R, 128),
+        rstat=F(R, 128), z=F(R, HP), zn=B(R, HP), w_gu=B(D, 2 * HP), w_dn=B(D, HP), cs=DMA((5,)), cr=DMA((5,)),
+        xs=DMA((4,)), xr=DMA((4,)), ls=DMA((2,)))
+    return run_kernel(body, "layer", cid, ins, outs, scratch, extra)
 
 
 def add8(acc, x):
@@ -1360,7 +1390,7 @@
     D = b.g.shape[1]
     for a in (b.a0, b.a1, b.a2, b.a3, b.a4, b.a5, b.a6, b.vec):
         a[...] = jnp.zeros_like(a)
-    b.need("g", "keep", "gate", "up", "st", "vn", "vf")
+    b.need("g", "keep")
 
     def unit4(s):
         g = b.gate[s]
@@ -1371,11 +1401,16 @@
         e = wide(b.keep[s], D) * b.g[s]
         b.el[s] = e.astype(BF)
         add8(b.a2, e)
+
+    def norms(s):
         norm_store(b.n, s, b.go[s], b.vn[2:3, :], b.vn[3:4, :])
         b.zn[s] = (unit4(s)[0] * b.vf[0:1, :] + b.vf[3:4, :]).astype(BF)
 
     rows16(R, first)
+    b.need("gate", "up", "st", "vn", "vf")
+    rows16(R, norms)
     b.need("w_dn")
+    b.begin("w_gu")
     yield
     for i, (a, n) in enumerate(tiles(HP)):
         b.ez[:, a : a + n] = dot_nn(b.el[...], b.w_dn[:, a : a + n])
@@ -1452,6 +1487,7 @@
 
     rows16(R, first)
     b.need("w_out")
+    b.begin("q", "k", "v", "lse", "fill", "cos", "sin", "w_in")
     yield
     for a, n in tiles(512):
         b.dq[:, a : a + n] = dot_nn(b.el[...], b.w_out[:, a : a + n])
@@ -1621,9 +1657,9 @@
         dset.finish()
         core.finish()
 
-    ins = {"g": (g, LD), "keep": (tabs["keep"], LD), "hm": (hm, ANY), "gate": (fw["gate"], LD), "up": (fw["up"], LD), "st": (fw["st"], LD),
-           "w_gu": (wts["gu"], LD), "w_dn": (wts["dn"], LD), "vn": (vn, LD), "vf": (vf, LD)}
-    outs = {"go": ((R, D), F32, ST), "d_gu": ((D, 2 * HP), BF, ST), "r_dn": ((RB, HP), F32, VM), "vec": ((8, HP), F32, VM)}
+    ins = dict(g=(g, LD), keep=(tabs["keep"], LD), hm=(hm, ANY), gate=(fw["gate"], LD), up=(fw["up"], LD),
+        st=(fw["zst"], LD), w_gu=(wts["gu"], LATE), w_dn=(wts["dn"], LD), vn=(vn, LD), vf=(vf, LD))
+    outs = dict(go=((R, D), F32, ST), d_gu=((D, 2 * HP), BF, ST), r_dn=((RB, HP), F32, VM), vec=((8, HP), F32, VM))
     extra = ()
     dset = dn_scatter()
     if sset:
@@ -1634,10 +1670,11 @@
     split = len(extra)
     extra = list(extra) + dset.scratch()
     acc = lambda n: pltpu.VMEM((8, n), F32)
-    scratch = {"d_dn": pltpu.VMEM((D, HP), BF), "el": pltpu.VMEM((R, D), BF), "xT": pltpu.VMEM((D, R), BF), "n": pltpu.VMEM((R, D), BF), "ez": pltpu.VMEM((R, HP), F32),
-               "zn": pltpu.VMEM((R, HP), BF), "egu": pltpu.VMEM((R, 2 * HP), BF), "part": pltpu.VMEM((R, D), BF), "rpart": pltpu.VMEM((R, D), BF),
-               "stat": pltpu.VMEM((R, 128), F32), "rstat": pltpu.VMEM((R, 128), F32), "cs": DMA((5,)), "cr": DMA((5,)), "ls": DMA((1,)),
-               "a0": acc(D), "a1": acc(D), "a2": acc(D), "a3": acc(HP), "a4": acc(HP), "a5": acc(HP), "a6": acc(HP)}
+    scratch = dict(d_dn=pltpu.VMEM((D, HP), BF), el=pltpu.VMEM((R, D), BF), xT=pltpu.VMEM((D, R), BF), n=pltpu.VMEM((R, D), BF),
+        ez=pltpu.VMEM((R, HP), F32), zn=pltpu.VMEM((R, HP), BF), egu=pltpu.VMEM((R, 2 * HP), BF),
+        part=pltpu.VMEM((R, D), BF), rpart=pltpu.VMEM((R, D), BF), stat=pltpu.VMEM((R, 128), F32),
+        rstat=pltpu.VMEM((R, 128), F32), cs=DMA((5,)), cr=DMA((5,)), ls=DMA((1,)), a0=acc(D), a1=acc(D), a2=acc(D),
+        a3=acc(HP), a4=acc(HP), a5=acc(HP), a6=acc(HP))
     return run_kernel(body, "hidden_back", cid, ins, outs, scratch, extra)
 
 
@@ -1655,25 +1692,26 @@
         for _ in sset.live:
             next(comm)
         load.wait()
-        drive(attend_back_body(b, w, R, core, side), comm, [], 2)
+        drive(attend_back_body(b, w, R, core, side), comm, [1] * 4 + [1, 2] * 8, 2)
         sset.finish()
         core.finish()
 
-    ins = {"g": (g, LD), "keep": (tabs["keep"], LD), "h": (h, ANY), "fill": (tabs["fill"], LD), "cos": (tabs["cos"], LD), "sin": (tabs["sin"], LD),
-           "o": (fw["o"], LD), "st": (fw["st"], LD), "q": (fw["q"], LD), "k": (fw["k"], LD), "v": (fw["v"], LD), "lse": (fw["lse"], LD),
-           "w_in": (wts["in"], LD), "w_out": (wts["out"], LD), "vn": (vn, LD), "vh": (vh, LD)}
-    outs = {"go": ((R, D), F32, ST), "d_in": ((D, 1536), BF, ST), "d_out": ((D, 512), BF, ST), "vec": ((8, HP), F32, VM)}
+    ins = dict(g=(g, LD), keep=(tabs["keep"], LD), h=(h, ANY), fill=(tabs["fill"], LATE), cos=(tabs["cos"], LATE),
+        sin=(tabs["sin"], LATE), o=(fw["o"], LD), st=(fw["st"], LD), q=(fw["q"], LATE), k=(fw["k"], LATE),
+        v=(fw["v"], LATE), lse=(fw["lse"], LATE), w_in=(wts["in"], LATE), w_out=(wts["out"], LD), vn=(vn, LD),
+        vh=(vh, LD))
+    outs = dict(go=((R, D), F32, ST), d_in=((D, 1536), BF, ST), d_out=((D, 512), BF, ST), vec=((8, HP), F32, VM))
     i2, o2 = scatter_args(sset, grads, vec)
     ins.update(i2)
     outs.update(o2)
     acc = lambda n: pltpu.VMEM((8, n), F32)
     B = lambda *s: pltpu.VMEM(s, BF)
     F = lambda *s: pltpu.VMEM(s, F32)
-    scratch = {"el": B(R, D), "xT": B(D, R), "n": B(R, D), "u": B(R, 512), "eo": B(R, 512), "s": F(2 * R, R), "dp": F(2 * R, R),
-               "p": B(2 * R, R), "ds": B(2 * R, R), "dq": F(R, 512), "dk": F(R, 512), "dv": F(R, 512),
-               "rk": B(R, 512), "rv": B(R, 512), "ep": B(R, 1536), "part": B(R, D), "rpart": B(R, D), "stat": F(R, 128), "rstat": F(R, 128),
-               "cs": DMA((5,)), "cr": DMA((5,)), "ls": DMA((1,)), "xs": DMA((8,)), "xr": DMA((8,)),
-               "a0": acc(D), "a1": acc(D), "a2": acc(D), "a3": acc(512), "a4": acc(512), "a5": acc(512), "a6": acc(512)}
+    scratch = dict(el=B(R, D), xT=B(D, R), n=B(R, D), u=B(R, 512), eo=B(R, 512), s=F(2 * R, R), dp=F(2 * R, R), p=B(2 * R, R),
+        ds=B(2 * R, R), dq=F(R, 512), dk=F(R, 512), dv=F(R, 512), rk=B(R, 512), rv=B(R, 512), ep=B(R, 1536),
+        part=B(R, D), rpart=B(R, D), stat=F(R, 128), rstat=F(R, 128), cs=DMA((5,)), cr=DMA((5,)), ls=DMA((1,)),
+        xs=DMA((8,)), xr=DMA((8,)), a0=acc(D), a1=acc(D), a2=acc(D), a3=acc(512), a4=acc(512), a5=acc(512),
+        a6=acc(512))
     return run_kernel(body, "attend_back", cid, ins, outs, scratch, sset.scratch())
 
 
@@ -1722,14 +1760,11 @@
     c0, c1, s0, s1 = cosine[:, 0], cosine[:, 1], sine[:, 0], sine[:, 1]
     low = lambda a: jnp.pad(a, ((0, more), (0, 0)))
     keep = low(key_mask.astype(F32).reshape(rows, 1))
-    fill = jnp.where(jnp.arange(R)[:, None] < rows, (keep - 1.0) * 10000.0, -1.0e30)
-    other = lax.ppermute(fill[:, 0], "ctx", [(0, 1), (1, 0)])[:, None]
-    tabs = {
-        "keep": jnp.broadcast_to(keep, (R, 128)),
-        "fill": jnp.broadcast_to(jnp.concatenate([fill, other]), (2 * R, 128)),
-        "cos": low(jnp.concatenate([c0, c0, c1, c1] * 2, axis=1)),
-        "sin": low(jnp.concatenate([-s0, s0, -s1, s1] * 2, axis=1)),
-    }
+    real = jnp.pad(key_mask.astype(F32).reshape(1, rows), ((0, 0), (0, more)))
+    fill = jnp.where(jnp.arange(R)[None] < rows, (real - 1.0) * 10000.0, -1.0e30)
+    fill = jnp.broadcast_to(fill, (8, R))
+    tabs = dict(keep=jnp.broadcast_to(keep, (R, 128)), cos=low(jnp.concatenate([c0, c0, c1, c1] * 2, axis=1)),
+        sin=low(jnp.concatenate([-s0, s0, -s1, s1] * 2, axis=1)))
     gn = norm_gains.astype(F32)
     bn = norm_biases.astype(F32)
     gh = head_gains.astype(F32)[:, None]
@@ -1745,30 +1780,29 @@
     ff_src = [{"gu": gu[l].reshape(RB, 2 * HP), "dn": dn[l]} for l in range(layers)]
     grab = lambda d, names: {n: d["g_" + n] for n in names}
     h = low(tokens_in.astype(F32).reshape(rows, width)) * keep
-    first = gather_first(at_src[0], AT_G, 0)
+    first = gather_first(at_src[0], AT_G, fill, 0)
+    tabs["fill"] = first["both"]
     at_w = {0: {n: first["w_" + n] for n in AT_G.names}}
-    ff_w, hs, hms, at_f, ff_f = {}, {}, {}, {}, {}
+    ff_w, hs, fw = {}, {}, {}
     for l in range(layers):
         hs[l] = h
-        at_f[l] = forward_attend(h, tabs, at_w[l], vn[l], vh[l], ff_src[l], FF_G, 1 + 2 * l)
-        ff_w[l] = grab(at_f[l], FF_G.names)
-        hms[l] = at_f[l]["hm"]
         nxt = l + 1 < layers
-        ff_f[l] = forward_hidden(hms[l], tabs, ff_w[l], vn[l], vf[l], at_src[l + 1] if nxt else None, AT_G if nxt else None, 2 + 2 * l)
+        r = forward_layer(h, tabs, at_w[l], vn[l], vh[l], vf[l], ff_src[l], at_src[l + 1] if nxt else None, 1 + l)
+        fw[l], h = r, r["ho"]
+        ff_w[l] = grab(r, FF_G.names)
         if nxt:
-            at_w[l + 1] = grab(ff_f[l], AT_G.names)
-        h = ff_f[l]["ho"]
+            at_w[l + 1] = grab(r, AT_G.names)
     activations = h[:rows].astype(BF).reshape(1, rows, width)
     g = low(cotangent.astype(F32).reshape(rows, width))
     got = {}
-    grads, vec, cid = None, None, 2 * layers + 1
+    grads, vec, cid = None, None, layers + 1
     for l in reversed(range(layers)):
         sset = at_scatter() if grads else None
-        r = backward_hidden(g, ff_f[l], hms[l], tabs, ff_w[l], vn[l], vf[l], sset, grads, vec, cid)
+        r = backward_hidden(g, fw[l], fw[l]["hm"], tabs, ff_w[l], vn[l], vf[l], sset, grads, vec, cid)
         if grads:
             got["at", l + 1] = r
         g, vec, grads, got["dn", l] = r["go"], r["vec"], {"gu": r["d_gu"]}, r["r_dn"]
-        r = backward_attend(g, at_f[l], hs[l], tabs, at_w[l], vn[l], vh[l], gu_scatter(), grads, vec, cid + 1)
+        r = backward_attend(g, fw[l], hs[l], tabs, at_w[l], vn[l], vh[l], gu_scatter(), grads, vec, cid + 1)
         got["ff", l] = r
         g, vec, grads = r["go"], r["vec"], {"in": r["d_in"], "out": r["d_out"]}
         cid += 2
@@ -1795,7 +1829,7 @@
 
 def solution(mesh):
     sizes = dict(mesh.shape)
-    fits = sizes == {"dp": 8, "ctx": 2, "tp": 2}
+    fits = sizes == dict(dp=8, ctx=2, tp=2)
     return jax.shard_map(
         fast_device if fits else on_device,
         mesh=mesh,

time: 659 us -> 640 us (0.971)
  Pallas kernels: 604 us -> 579 us
    pallas_call x10 -> x8, Pallas kernels: 604 us -> 579 us  [run_kernel(): pl.pallas_call(kernel, out_shape=[jax.ShapeDtypeStruct(outs[n][0], outs[n...]
  transfers between devices with their start and end apart: 1 -> 0, of which waited for: 0 -> 0; matrix products, arithmetic and copies ran while one was open for 3% -> 0% of each run, Pallas kernels for 6% -> 0%
where the time goes in v4:
time: 640 us; the launch traced here: 633 us
  Pallas kernels  579 us (90%)
  local copies, waits for them, and re-layouts  34.8 us (5%)
  other arithmetic  17.4 us (3%)
    pallas_call x8, Pallas kernels, run_kernel(): pl.pallas_call(kernel, out_shape=[jax.ShapeDtypeStruct(outs[n][0], outs[n...  579 us

profile of v4, /device:TPU:0, one launch (start us, length us, event | category | flops | bytes accessed | tf_op | source)
XLA Modules:
  0.0 633.5 jit_solution(4484670817255997047)
XLA Ops:
  10.5 1.5 slice_bitcast_fusion.8
  12.9 1.8 fusion.5
  18.7 1.9 fusion.2
  20.8 2.6 concatenate.15
  24.1 2.5 concatenate.14
  27.4 1.6 convert_multiply_fusion.refs_0_.refs_2_
  28.9 1.6 pad_convert_fusion.refs_0_
  30.5 40.7 %gather.1 = (bf16[1024,1536]{1,0:T(8,128)(2,1)}, bf16[1024,512]{1,0:T(8,128)(2,1)}, f32[1056,128]{1,0:T(8,128)}) custom-call(bf16[64,1536]{1,0:T(8,128)(2,1)} %bitcast.90, bf16[64,512]{1,0:T(8,128)(2,1)} %get-tuple-element.163.refs_1_, f32[8,528]{1,0:T(8,128)} %broadcast_in_dim.31.refs_2_), custom_call_target="tpu_custom_call" | custom-call | tf_op jit(solution)/shard_map/gather/pallas_call | solution.py:1097
  71.2 128.1 %layer.2 = (f32[528,1024]{1,0:T(8,128)}, bf16[528,512]{1,0:T(8,128)(2,1)}, bf16[1056,512]{1,0:T(8,128)(2,1)}, bf16[1056,512]{1,0:T(8,128)(2,1)}, f32[8,528]{1,0:...) custom-call(f32[528,1024]{1,0:T(8,128)} %convert_multiply_fusion.ref, ...), custom_call_target="tpu_custom_call" | custom-call | tf_op jit(solution)/shard_map/layer/pallas_call | solution.py:1097
  199.3 104.9 %layer.3 = (f32[528,1024]{1,0:T(8,128)}, bf16[528,512]{1,0:T(8,128)(2,1)}, bf16[1056,512]{1,0:T(8,128)(2,1)}, bf16[1056,512]{1,0:T(8,128)(2,1)}, f32[8,528]{1,0:...) custom-call(f32[528,1024]{1,0:T(8,128)} %get-tuple-element.72.refs_0, ...), custom_call_target="tpu_custom_call" | custom-call | tf_op jit(solution)/shard_map/layer/pallas_call | solution.py:1097
  304.2 2.7 fusion.1
  306.9 43.2 %hidden_back.2 = (f32[528,1024]{1,0:T(8,128)}, bf16[1024,2816]{1,0:T(8,128)(2,1)}, f32[64,1408]{1,0:T(8,128)}, f32[8,1408]{1,0:T(8,128)}) custom-call(f32[528,1024]{1,0:T(8,128)} %pad_convert_fusion.refs_0_, f32[528,128]{1,0:T(8,128)} %broadcast_in_dim.28.refs_1_, f32[528,1024]{1,0:T(8,128)} %get-tuple-element.76.refs_2_, ...), custom_call_target="tpu_custom_call" | custom-call | tf_op jit(solution)/shard_map/hidden_back/pallas_call | solution.py:1097
  350.1 75.5 %attend_back.2 = (f32[528,1024]{1,0:T(8,128)}, bf16[1024,1536]{1,0:T(8,128)(2,1)}, bf16[1024,512]{1,0:T(8,128)(2,1)}, f32[8,1408]{1,0:T(8,128)}, f32[64,2816]{1,0:T(8,128)}, /*index=5*/f32[8,1408]{1,0:T(8,128)}) custom-call(f32[528,1024]{1,0:T(8,128)} %get-tuple-element.82.refs_0_, f32[528,128]{1,0:T(8,128)} %broadcast_in_dim.28.refs_1_, ...), custom_call_target="tpu_custom_call" | custom-call | tf_op jit(solution)/shard_map/attend_back/pallas_call | solution.py:1097
  425.6 66.7 %hidden_back.3 = (f32[528,1024]{1,0:T(8,128)}, bf16[1024,2816]{1,0:T(8,128)(2,1)}, f32[64,1408]{1,0:T(8,128)}, f32[8,1408]{1,0:T(8,128)}, f32[64,1536]{1,0:T(8,1...) custom-call(f32[528,1024]{1,0:T(8,128)} %get-tuple-element.91.refs_0_, f32[528,128]{1,0:T(8,128)} %broadcast_in_dim.28.refs_1_, ...), custom_call_target="tpu_custom_call" | custom-call | tf_op jit(solution)/shard_map/hidden_back/pallas_call | solution.py:1097
  492.3 75.1 %attend_back.3 = (f32[528,1024]{1,0:T(8,128)}, bf16[1024,1536]{1,0:T(8,128)(2,1)}, bf16[1024,512]{1,0:T(8,128)(2,1)}, f32[8,1408]{1,0:T(8,128)}, f32[64,2816]{1,0:T(8,128)}, /*index=5*/f32[8,1408]{1,0:T(8,128)}) custom-call(f32[528,1024]{1,0:T(8,128)} %get-tuple-element.101.refs_0_, f32[528,128]{1,0:T(8,128)} %broadcast_in_dim.28.refs_1_, ...), custom_call_target="tpu_custom_call" | custom-call | tf_op jit(solution)/shard_map/attend_back/pallas_call | solution.py:1097
  567.3 1.8 fusion
  569.2 3.5 copy.42
  575.3 45.3 %scatter.1 = (f32[64,1536]{1,0:T(8,128)}, f32[64,512]{1,0:T(8,128)}, f32[8,1408]{1,0:T(8,128)}) custom-call(bf16[1024,1536]{1,0:T(8,128)(2,1)} %get-tuple-element.111.refs_0_, bf16[1024,512]{1,0:T(8,128)(2,1)} %get-tuple-element.112.refs_1_, f32[8,1408]{1,0:T(8,128)} %get-tuple-element.113.refs_2_), custom_call_target="tpu_custom_call" | custom-call | tf_op jit(solution)/shard_map/scatter/pallas_call | solution.py:1097
  620.6 1.6 pad_maximum_fusion.3
  623.6 1.4 fusion.22
  624.9 1.5 fusion.13
  627.7 1.3 stack_reshape.6
  629.4 1.1 copy.43
  631.5 1.8 pad_maximum_fusion
  (77 shorter events, 22.0 us)
Async XLA Ops:
  0.6 14.0 %copy-start.9 = (bf16[2,64,3,512]{3,1,2,0:T(8,128)(2,1)S(1)}, bf16[2,64,3,512]{3,1,2,0:T(8,128)(2,1)}, u32[]{:S(2)}) copy-start(bf16[2,64,3,512]{3,1,2,0:T(8,128)(2,1)} %param.20) | copy-start | bytes 1179652
  9.2 7.3 %copy-start.2 = (bf16[2,64,2,1365]{3,2,1,0:T(2,128)(2,1)S(1)}, bf16[2,64,2,1365]{3,2,1,0:T(2,128)(2,1)}, u32[]{:S(2)}) copy-start(bf16[2,64,2,1365]{3,2,1,0:T(2,128)(2,1)} %param.22) | copy-start | bytes 2096644
  23.3 4.0 copy-start
  26.6 2.3 copy-start.1
  569.1 3.5 copy-start.5
  569.2 3.5 copy-start.7
  569.2 4.8 copy-start.11
  569.2 4.8 copy-start.10
  572.7 2.3 copy-start.8
  575.2 45.4 %copy-start.12 = (f32[64,512]{1,0:T(8,128)S(1)}, f32[64,512]{1,0:T(8,128)}, u32[]{:S(2)}) copy-start(f32[64,512]{1,0:T(8,128)} %get-tuple-element.117) | copy-start | bytes 393220
  575.2 47.0 %copy-start.6 = (f32[8,1408]{1,0:T(8,128)S(1)}, f32[8,1408]{1,0:T(8,128)}, u32[]{:S(2)}) copy-start(f32[8,1408]{1,0:T(8,128)} %get-tuple-element.123) | copy-start | bytes 135172
  629.0 1.5 copy-start.4
  629.3 1.6 copy-start.3

commit v5 on v4

--- a/solution.py
+++ b/solution.py
@@ -1338,7 +1338,7 @@
             core.finish()
             yield from hidden_body(b, w, R, core, fetch)
 
-        drive(comp(), comm, [0, 0, n, n, n], 3)
+        drive(comp(), comm, [0, 0, n, 0, n, 0, n], 2)
         fset.finish_sends()
         if aset:
             aset.finish()

time: 640 us -> 634 us (level)
  no operation moved by 1% of the time
where the time goes in v5:
time: 634 us; the launch traced here: 628 us
  Pallas kernels  574 us (91%)
  local copies, waits for them, and re-layouts  34.8 us (5%)
  other arithmetic  17.4 us (3%)
    pallas_call x8, Pallas kernels, run_kernel(): pl.pallas_call(kernel, out_shape=[jax.ShapeDtypeStruct(outs[n][0], outs[n...  574 us

profile of v5, /device:TPU:0, one launch (start us, length us, event | category | flops | bytes accessed | tf_op | source)
XLA Modules:
  0.0 628.4 jit_solution(3640683188370711647)
XLA Ops:
  10.5 1.5 slice_bitcast_fusion.8
  12.9 1.8 fusion.5
  18.7 1.9 fusion.2
  20.8 2.6 concatenate.15
  24.1 2.5 concatenate.14
  27.4 1.6 convert_multiply_fusion.refs_0_.refs_2_
  28.9 1.6 pad_convert_fusion.refs_0_
  30.5 40.7 %gather.1 = (bf16[1024,1536]{1,0:T(8,128)(2,1)}, bf16[1024,512]{1,0:T(8,128)(2,1)}, f32[1056,128]{1,0:T(8,128)}) custom-call(bf16[64,1536]{1,0:T(8,128)(2,1)} %bitcast.90, bf16[64,512]{1,0:T(8,128)(2,1)} %get-tuple-element.163.refs_1_, f32[8,528]{1,0:T(8,128)} %broadcast_in_dim.31.refs_2_), custom_call_target="tpu_custom_call" | custom-call | tf_op jit(solution)/shard_map/gather/pallas_call | solution.py:1097
  71.2 123.6 %layer.2 = (f32[528,1024]{1,0:T(8,128)}, bf16[528,512]{1,0:T(8,128)(2,1)}, bf16[1056,512]{1,0:T(8,128)(2,1)}, bf16[1056,512]{1,0:T(8,128)(2,1)}, f32[8,528]{1,0:...) custom-call(f32[528,1024]{1,0:T(8,128)} %convert_multiply_fusion.ref, ...), custom_call_target="tpu_custom_call" | custom-call | tf_op jit(solution)/shard_map/layer/pallas_call | solution.py:1097
  194.8 103.2 %layer.3 = (f32[528,1024]{1,0:T(8,128)}, bf16[528,512]{1,0:T(8,128)(2,1)}, bf16[1056,512]{1,0:T(8,128)(2,1)}, bf16[1056,512]{1,0:T(8,128)(2,1)}, f32[8,528]{1,0:...) custom-call(f32[528,1024]{1,0:T(8,128)} %get-tuple-element.72.refs_0, ...), custom_call_target="tpu_custom_call" | custom-call | tf_op jit(solution)/shard_map/layer/pallas_call | solution.py:1097
  298.0 2.7 fusion.1
  300.8 43.6 %hidden_back.2 = (f32[528,1024]{1,0:T(8,128)}, bf16[1024,2816]{1,0:T(8,128)(2,1)}, f32[64,1408]{1,0:T(8,128)}, f32[8,1408]{1,0:T(8,128)}) custom-call(f32[528,1024]{1,0:T(8,128)} %pad_convert_fusion.refs_0_, f32[528,128]{1,0:T(8,128)} %broadcast_in_dim.28.refs_1_, f32[528,1024]{1,0:T(8,128)} %get-tuple-element.76.refs_2_, ...), custom_call_target="tpu_custom_call" | custom-call | tf_op jit(solution)/shard_map/hidden_back/pallas_call | solution.py:1097
  344.3 76.0 %attend_back.2 = (f32[528,1024]{1,0:T(8,128)}, bf16[1024,1536]{1,0:T(8,128)(2,1)}, bf16[1024,512]{1,0:T(8,128)(2,1)}, f32[8,1408]{1,0:T(8,128)}, f32[64,2816]{1,0:T(8,128)}, /*index=5*/f32[8,1408]{1,0:T(8,128)}) custom-call(f32[528,1024]{1,0:T(8,128)} %get-tuple-element.82.refs_0_, f32[528,128]{1,0:T(8,128)} %broadcast_in_dim.28.refs_1_, ...), custom_call_target="tpu_custom_call" | custom-call | tf_op jit(solution)/shard_map/attend_back/pallas_call | solution.py:1097
  420.3 67.4 %hidden_back.3 = (f32[528,1024]{1,0:T(8,128)}, bf16[1024,2816]{1,0:T(8,128)(2,1)}, f32[64,1408]{1,0:T(8,128)}, f32[8,1408]{1,0:T(8,128)}, f32[64,1536]{1,0:T(8,1...) custom-call(f32[528,1024]{1,0:T(8,128)} %get-tuple-element.91.refs_0_, f32[528,128]{1,0:T(8,128)} %broadcast_in_dim.28.refs_1_, ...), custom_call_target="tpu_custom_call" | custom-call | tf_op jit(solution)/shard_map/hidden_back/pallas_call | solution.py:1097
  487.7 74.8 %attend_back.3 = (f32[528,1024]{1,0:T(8,128)}, bf16[1024,1536]{1,0:T(8,128)(2,1)}, bf16[1024,512]{1,0:T(8,128)(2,1)}, f32[8,1408]{1,0:T(8,128)}, f32[64,2816]{1,0:T(8,128)}, /*index=5*/f32[8,1408]{1,0:T(8,128)}) custom-call(f32[528,1024]{1,0:T(8,128)} %get-tuple-element.101.refs_0_, f32[528,128]{1,0:T(8,128)} %broadcast_in_dim.28.refs_1_, ...), custom_call_target="tpu_custom_call" | custom-call | tf_op jit(solution)/shard_map/attend_back/pallas_call | solution.py:1097
  562.6 1.8 fusion
  564.4 3.5 copy.42
  570.5 45.0 %scatter.1 = (f32[64,1536]{1,0:T(8,128)}, f32[64,512]{1,0:T(8,128)}, f32[8,1408]{1,0:T(8,128)}) custom-call(bf16[1024,1536]{1,0:T(8,128)(2,1)} %get-tuple-element.111.refs_0_, bf16[1024,512]{1,0:T(8,128)(2,1)} %get-tuple-element.112.refs_1_, f32[8,1408]{1,0:T(8,128)} %get-tuple-element.113.refs_2_), custom_call_target="tpu_custom_call" | custom-call | tf_op jit(solution)/shard_map/scatter/pallas_call | solution.py:1097
  615.5 1.6 pad_maximum_fusion.3
  618.4 1.4 fusion.22
  619.8 1.5 fusion.13
  622.6 1.3 stack_reshape.6
  624.3 1.1 copy.43
  626.4 1.8 pad_maximum_fusion
  (77 shorter events, 22.0 us)
Async XLA Ops:
  0.6 14.0 %copy-start.9 = (bf16[2,64,3,512]{3,1,2,0:T(8,128)(2,1)S(1)}, bf16[2,64,3,512]{3,1,2,0:T(8,128)(2,1)}, u32[]{:S(2)}) copy-start(bf16[2,64,3,512]{3,1,2,0:T(8,128)(2,1)} %param.20) | copy-start | bytes 1179652
  9.2 7.3 %copy-start.2 = (bf16[2,64,2,1365]{3,2,1,0:T(2,128)(2,1)S(1)}, bf16[2,64,2,1365]{3,2,1,0:T(2,128)(2,1)}, u32[]{:S(2)}) copy-start(bf16[2,64,2,1365]{3,2,1,0:T(2,128)(2,1)} %param.22) | copy-start | bytes 2096644
  23.3 4.0 copy-start
  26.6 2.3 copy-start.1
  564.4 3.5 copy-start.5
  564.4 3.5 copy-start.7
  564.4 4.8 copy-start.11
  564.4 4.8 copy-start.10
  567.9 2.3 copy-start.8
  570.5 45.0 %copy-start.12 = (f32[64,512]{1,0:T(8,128)S(1)}, f32[64,512]{1,0:T(8,128)}, u32[]{:S(2)}) copy-start(f32[64,512]{1,0:T(8,128)} %get-tuple-element.117) | copy-start | bytes 393220
  570.5 46.7 %copy-start.6 = (f32[8,1408]{1,0:T(8,128)S(1)}, f32[8,1408]{1,0:T(8,128)}, u32[]{:S(2)}) copy-start(f32[8,1408]{1,0:T(8,128)} %get-tuple-element.123) | copy-start | bytes 135172
  623.9 1.5 copy-start.4
  624.2 1.6 copy-start.3

commit v6 on v5

--- a/solution.py
+++ b/solution.py
@@ -1338,7 +1338,7 @@
             core.finish()
             yield from hidden_body(b, w, R, core, fetch)
 
-        drive(comp(), comm, [0, 0, n, 0, n, 0, n], 2)
+        drive(comp(), comm, [0, 0, n, 0, n, 0, n] + [1] * 4, 3)
         fset.finish_sends()
         if aset:
             aset.finish()

time: 634 us -> 622 us (0.981)
  Pallas kernels: 574 us -> 561 us
    pallas_call x8, Pallas kernels: 574 us -> 561 us  [run_kernel(): pl.pallas_call(kernel, out_shape=[jax.ShapeDtypeStruct(outs[n][0], outs[n...]
where the time goes in v6:
time: 622 us; the launch traced here: 615 us
  Pallas kernels  561 us (90%)
  local copies, waits for them, and re-layouts  34.8 us (6%)
  other arithmetic  17.4 us (3%)
    pallas_call x8, Pallas kernels, run_kernel(): pl.pallas_call(kernel, out_shape=[jax.ShapeDtypeStruct(outs[n][0], outs[n...  561 us

profile of v6, /device:TPU:0, one launch (start us, length us, event | category | flops | bytes accessed | tf_op | source)
XLA Modules:
  0.0 615.4 jit_solution(17488433055166776966)
XLA Ops:
  10.5 1.5 slice_bitcast_fusion.8
  12.9 1.8 fusion.5
  18.7 1.9 fusion.2
  20.8 2.6 concatenate.15
  24.1 2.5 concatenate.14
  27.4 1.6 convert_multiply_fusion.refs_0_.refs_2_
  28.9 1.6 pad_convert_fusion.refs_0_
  30.5 40.7 %gather.1 = (bf16[1024,1536]{1,0:T(8,128)(2,1)}, bf16[1024,512]{1,0:T(8,128)(2,1)}, f32[1056,128]{1,0:T(8,128)}) custom-call(bf16[64,1536]{1,0:T(8,128)(2,1)} %bitcast.90, bf16[64,512]{1,0:T(8,128)(2,1)} %get-tuple-element.163.refs_1_, f32[8,528]{1,0:T(8,128)} %broadcast_in_dim.31.refs_2_), custom_call_target="tpu_custom_call" | custom-call | tf_op jit(solution)/shard_map/gather/pallas_call | solution.py:1097
  71.2 118.4 %layer.2 = (f32[528,1024]{1,0:T(8,128)}, bf16[528,512]{1,0:T(8,128)(2,1)}, bf16[1056,512]{1,0:T(8,128)(2,1)}, bf16[1056,512]{1,0:T(8,128)(2,1)}, f32[8,528]{1,0:...) custom-call(f32[528,1024]{1,0:T(8,128)} %convert_multiply_fusion.ref, ...), custom_call_target="tpu_custom_call" | custom-call | tf_op jit(solution)/shard_map/layer/pallas_call | solution.py:1097
  189.7 96.2 %layer.3 = (f32[528,1024]{1,0:T(8,128)}, bf16[528,512]{1,0:T(8,128)(2,1)}, bf16[1056,512]{1,0:T(8,128)(2,1)}, bf16[1056,512]{1,0:T(8,128)(2,1)}, f32[8,528]{1,0:...) custom-call(f32[528,1024]{1,0:T(8,128)} %get-tuple-element.72.refs_0, ...), custom_call_target="tpu_custom_call" | custom-call | tf_op jit(solution)/shard_map/layer/pallas_call | solution.py:1097
  285.9 2.7 fusion.1
  288.6 43.6 %hidden_back.2 = (f32[528,1024]{1,0:T(8,128)}, bf16[1024,2816]{1,0:T(8,128)(2,1)}, f32[64,1408]{1,0:T(8,128)}, f32[8,1408]{1,0:T(8,128)}) custom-call(f32[528,1024]{1,0:T(8,128)} %pad_convert_fusion.refs_0_, f32[528,128]{1,0:T(8,128)} %broadcast_in_dim.28.refs_1_, f32[528,1024]{1,0:T(8,128)} %get-tuple-element.76.refs_2_, ...), custom_call_target="tpu_custom_call" | custom-call | tf_op jit(solution)/shard_map/hidden_back/pallas_call | solution.py:1097
  332.2 74.9 %attend_back.2 = (f32[528,1024]{1,0:T(8,128)}, bf16[1024,1536]{1,0:T(8,128)(2,1)}, bf16[1024,512]{1,0:T(8,128)(2,1)}, f32[8,1408]{1,0:T(8,128)}, f32[64,2816]{1,0:T(8,128)}, /*index=5*/f32[8,1408]{1,0:T(8,128)}) custom-call(f32[528,1024]{1,0:T(8,128)} %get-tuple-element.82.refs_0_, f32[528,128]{1,0:T(8,128)} %broadcast_in_dim.28.refs_1_, ...), custom_call_target="tpu_custom_call" | custom-call | tf_op jit(solution)/shard_map/attend_back/pallas_call | solution.py:1097
  407.1 67.5 %hidden_back.3 = (f32[528,1024]{1,0:T(8,128)}, bf16[1024,2816]{1,0:T(8,128)(2,1)}, f32[64,1408]{1,0:T(8,128)}, f32[8,1408]{1,0:T(8,128)}, f32[64,1536]{1,0:T(8,1...) custom-call(f32[528,1024]{1,0:T(8,128)} %get-tuple-element.91.refs_0_, f32[528,128]{1,0:T(8,128)} %broadcast_in_dim.28.refs_1_, ...), custom_call_target="tpu_custom_call" | custom-call | tf_op jit(solution)/shard_map/hidden_back/pallas_call | solution.py:1097
  474.6 74.4 %attend_back.3 = (f32[528,1024]{1,0:T(8,128)}, bf16[1024,1536]{1,0:T(8,128)(2,1)}, bf16[1024,512]{1,0:T(8,128)(2,1)}, f32[8,1408]{1,0:T(8,128)}, f32[64,2816]{1,0:T(8,128)}, /*index=5*/f32[8,1408]{1,0:T(8,128)}) custom-call(f32[528,1024]{1,0:T(8,128)} %get-tuple-element.101.refs_0_, f32[528,128]{1,0:T(8,128)} %broadcast_in_dim.28.refs_1_, ...), custom_call_target="tpu_custom_call" | custom-call | tf_op jit(solution)/shard_map/attend_back/pallas_call | solution.py:1097
  549.1 1.8 fusion
  550.9 3.5 copy.42
  557.0 45.5 %scatter.1 = (f32[64,1536]{1,0:T(8,128)}, f32[64,512]{1,0:T(8,128)}, f32[8,1408]{1,0:T(8,128)}) custom-call(bf16[1024,1536]{1,0:T(8,128)(2,1)} %get-tuple-element.111.refs_0_, bf16[1024,512]{1,0:T(8,128)(2,1)} %get-tuple-element.112.refs_1_, f32[8,1408]{1,0:T(8,128)} %get-tuple-element.113.refs_2_), custom_call_target="tpu_custom_call" | custom-call | tf_op jit(solution)/shard_map/scatter/pallas_call | solution.py:1097
  602.5 1.6 pad_maximum_fusion.3
  605.4 1.4 fusion.22
  606.8 1.5 fusion.13
  609.6 1.3 stack_reshape.6
  611.2 1.1 copy.43
  613.4 1.8 pad_maximum_fusion
  (77 shorter events, 22.0 us)
Async XLA Ops:
  0.6 14.0 %copy-start.9 = (bf16[2,64,3,512]{3,1,2,0:T(8,128)(2,1)S(1)}, bf16[2,64,3,512]{3,1,2,0:T(8,128)(2,1)}, u32[]{:S(2)}) copy-start(bf16[2,64,3,512]{3,1,2,0:T(8,128)(2,1)} %param.20) | copy-start | bytes 1179652
  9.2 7.3 %copy-start.2 = (bf16[2,64,2,1365]{3,2,1,0:T(2,128)(2,1)S(1)}, bf16[2,64,2,1365]{3,2,1,0:T(2,128)(2,1)}, u32[]{:S(2)}) copy-start(bf16[2,64,2,1365]{3,2,1,0:T(2,128)(2,1)} %param.22) | copy-start | bytes 2096644
  23.3 4.0 copy-start
  26.6 2.3 copy-start.1
  550.9 3.5 copy-start.5
  550.9 3.5 copy-start.7
  550.9 4.8 copy-start.11
  550.9 4.8 copy-start.10
  554.4 2.3 copy-start.8
  557.0 45.5 %copy-start.12 = (f32[64,512]{1,0:T(8,128)S(1)}, f32[64,512]{1,0:T(8,128)}, u32[]{:S(2)}) copy-start(f32[64,512]{1,0:T(8,128)} %get-tuple-element.117) | copy-start | bytes 393220
  557.0 47.1 %copy-start.6 = (f32[8,1408]{1,0:T(8,128)S(1)}, f32[8,1408]{1,0:T(8,128)}, u32[]{:S(2)}) copy-start(f32[8,1408]{1,0:T(8,128)} %get-tuple-element.123) | copy-start | bytes 135172
  610.9 1.5 copy-start.4
  611.2 1.6 copy-start.3
